TPU v7x, 512 devices: a whole 4x8x8 slice. The times are simulated.
512 devices in a mesh: space: 64 (over z, y), tensor: 8 (over x, core).
Axes of the slice: x: 4, y: 8, z: 8, core: 2. Of those that a mesh axis runs over, the one named last changes fastest.
Arguments:
- tokens: bfloat16 [57344, 1024], P('space', 'tensor'), may hold values from -16 to 16
- first_weight: bfloat16 [1024, 1024], P(None, 'tensor'), may hold values from -0.1875 to 0.1875
- second_weight: bfloat16 [1024, 1024], P(None, 'tensor'), may hold values from -0.1875 to 0.1875
- head_weight: bfloat16 [352, 1024], P('tensor'), may hold values from -0.1875 to 0.1875
- targets: float32 [352, 57344], P('tensor', 'space'), may hold values from -6 to 6
- land_mask: int32 [4, 57344], P(None, 'space'), may hold values from 0 to 1, as said below
- variable_kind: int32 [88], P('tensor'), may hold values from 0 to 2
- loss_scale: float32 [], replicated, may hold values from 2523136 to 20185088
Outputs:
- loss: float32 [], replicated
- token_grad: float32 [57344, 1024], P('space', 'tensor')
- first_grad: float32 [1024, 1024], P('space', 'tensor')
- second_grad: float32 [1024, 1024], P('space', 'tensor')
- head_grad: float32 [352, 1024], P('tensor', 'space')
Inputs may be any that keep to these rules, and one draw needn't show every extreme that they name: `land_mask`: every aligned group of 8 entries along the last dimension holds at least one 1 and one 0. `variable_kind`: 0 scores a variable on all cells, 1 on land cells, 2 on ocean cells.
All inputs are finite; a program needn't handle non-finite values.
Results may differ from a plain program's by a relative error of at most 0.0056.
Values may be sent and summed in bfloat16 or wider, within the bound.
No kernel may reach another device: no remote copies, remote signals or barrier semaphores. Data moves between devices by JAX's collectives and lax.ppermute only.
A program may use at most 64 MiB of HBM per device.

v0:
```python
import math

import jax
import jax.numpy as jnp
from jax import lax
from jax.sharding import PartitionSpec as P

V = 88
PP = 4
PROW_DEV = 4
LONP = 224


def sent_to_all(shard, axis):
    copies = jnp.broadcast_to(shard, (lax.axis_size(axis), *shard.shape))
    return lax.all_to_all(copies, axis, split_axis=0, concat_axis=0, tiled=True)


def over_copies(shard, axis):
    everything = sent_to_all(shard, axis)
    return jnp.sum(everything, axis=0)


def split_up(shard, dim, size):
    before, after = (shard.shape[:dim], shard.shape[dim + 1 :])
    return jnp.moveaxis(shard.reshape(*before, size, -1, *after), dim, 0)


def sent_and_summed(shard, axis, dim):
    size = lax.axis_size(axis)
    parts = lax.all_to_all(split_up(shard, dim, size), axis, 0, 0, tiled=True)
    return jnp.sum(parts, axis=0)


def laid_out(parts, dim):
    parts = jnp.moveaxis(parts, 0, dim)
    lengths = parts.shape
    return parts.reshape(*lengths[:dim], lengths[dim] * lengths[dim + 1], *lengths[dim + 2 :])


def gather_directly(shard, axis, dim):
    parts = sent_to_all(shard, axis)
    return laid_out(parts, dim)


def sum_at_owner(shard, axis, dim):
    parts = split_up(shard, dim, lax.axis_size(axis))
    arrived = lax.all_to_all(parts, axis, split_axis=0, concat_axis=0, tiled=True)
    return arrived.astype(jnp.float32).sum(axis=0)


def slope(z):
    cdf = 0.5 * (1.0 + lax.erf(z / math.sqrt(2.0)))
    return cdf + z * jnp.exp(-0.5 * z * z) / math.sqrt(2.0 * math.pi)


def column_folder(weights, piece):
    return lax.dot_general(
        piece, weights, (((1,), (1,)), ((), ())), preferred_element_type=jnp.float32
    )


def row_folder(weights, piece):
    return lax.dot_general(
        piece, weights, (((0,), (0,)), ((), ())), preferred_element_type=jnp.float32
    )


def per_device(
    tokens, first_weight, second_weight, head_weight, targets, land_mask, variable_kind, loss_scale
):
    count = tokens.shape[0]
    width = first_weight.shape[1]
    kinds = head_weight.shape[0] // PP
    rows_first, rows_second = (
        lax.all_to_all(first_weight, "tensor", split_axis=0, concat_axis=1, tiled=True),
        lax.all_to_all(second_weight, "tensor", split_axis=0, concat_axis=1, tiled=True),
    )
    head_cols = lax.all_to_all(head_weight, "tensor", split_axis=1, concat_axis=0, tiled=True)
    position = lax.axis_index("space") * count + jnp.arange(count, dtype=jnp.int32)
    cell = jnp.arange(PP, dtype=jnp.int32)
    lat_row = 2 * (position // LONP)[None, :] + (cell // 2)[:, None]
    nlat = 2 * PROW_DEV * lax.axis_size("space")
    cell_weight = jnp.cos(math.pi / 2.0 * (lat_row.astype(jnp.float32) + 0.5) / nlat)
    land = land_mask.astype(jnp.float32)
    kind = variable_kind[:, None, None]
    valid = jnp.where(kind == 0, 1.0, jnp.where(kind == 1, land[None], 1.0 - land[None]))
    masked = cell_weight[None] * valid
    local_weight = jnp.sum(masked, axis=(1, 2))
    weight_sum = over_copies(local_weight, "space")
    full_in = lax.all_gather(tokens, "tensor", axis=1, tiled=True)
    pre_one = jnp.dot(full_in, first_weight, preferred_element_type=jnp.float32)
    hidden_one = jax.nn.gelu(pre_one, approximate=False).astype(jnp.bfloat16)
    full_one = lax.all_gather(hidden_one, "tensor", axis=1, tiled=True)
    pre_two = jnp.dot(full_one, second_weight, preferred_element_type=jnp.float32)
    hidden_two = jax.nn.gelu(pre_two, approximate=False).astype(jnp.bfloat16)
    full_two = lax.all_gather(hidden_two, "tensor", axis=1, tiled=True)
    predicted = lax.dot_general(
        head_weight, full_two, (((1,), (1,)), ((), ())), preferred_element_type=jnp.float32
    )
    error = predicted.reshape(kinds, PP, count) - targets.reshape(kinds, PP, count)
    local_error = jnp.sum(masked * error * error, axis=(1, 2))
    error_sum = over_copies(local_error, "space")
    root = jnp.sqrt(error_sum / weight_sum + 1e-06)
    loss = lax.psum(jnp.sum(root), "tensor") / V
    coef = loss_scale / (V * root * weight_sum)
    grad_pred = (
        (coef[:, None, None] * masked * error).reshape(kinds * PP, count).astype(jnp.bfloat16)
    )
    back_two = row_folder(head_cols, lax.all_gather(grad_pred, "tensor", axis=0, tiled=True))
    head_term = jnp.dot(grad_pred, full_two, preferred_element_type=jnp.float32)
    head_grad = sent_and_summed(head_term, "space", 1)
    grad_two = (back_two * slope(pre_two)).astype(jnp.bfloat16)
    back_one = column_folder(rows_second, gather_directly(grad_two, "tensor", 1))
    grad_one = (back_one * slope(pre_one)).astype(jnp.bfloat16)
    joined = sum_at_owner(
        jnp.concatenate(
            [
                lax.dot_general(
                    full_one, grad_two, (((0,), (0,)), ((), ())), preferred_element_type=jnp.float32
                ),
                lax.dot_general(
                    full_in, grad_one, (((0,), (0,)), ((), ())), preferred_element_type=jnp.float32
                ),
            ],
            axis=1,
        ).astype(jnp.bfloat16),
        "space",
        0,
    )
    second_grad = joined[:, :width]
    first_grad = joined[:, width:]
    token_grad = column_folder(rows_first, lax.all_gather(grad_one, "tensor", axis=1, tiled=True))
    return (loss, token_grad, first_grad, second_grad, head_grad)


def solution(mesh):
    return jax.shard_map(
        per_device,
        mesh=mesh,
        in_specs=(
            P("space", "tensor"),
            P(None, "tensor"),
            P(None, "tensor"),
            P("tensor", None),
            P("tensor", "space"),
            P(None, "space"),
            P("tensor"),
            P(),
        ),
        out_specs=(
            P(),
            P("space", "tensor"),
            P("space", "tensor"),
            P("space", "tensor"),
            P("tensor", "space"),
        ),
        check_vma=False,
    )
```

profile of v0, /device:TPU:2, one launch (start us, length us, event | category | flops | bytes accessed | tf_op | source)
XLA Modules:
  0.0 263.2 jit_solution(2993436347642144659)
XLA Ops:
  7.9 37.8 %all-gather.6.cloned.1.call-done = bf16[896,1024]{1,0:T(8,128)(2,1)} async-done(((bf16[896,128]{1,0:T(8,128)(2,1)}), bf16[896,1024]{1,0:T(8,128)(2,1)}) %all-gather.6.cloned.1.call-update) | async-done | bytes 1835024 | tf_op jit(solution)/shard_map/all_gather | solution.py:91
  45.7 3.6 %fusion.21 = (bf16[896,128]{1,0:T(8,128)(2,1)}, f32[896,128]{1,0:T(8,128)S(1)}) fusion(bf16[896,1024]{1,0:T(8,128)(2,1)} %all-gather.6.cloned.1.call-done, bf16[1024,128]{1,0:T(8,128)(2,1)} %param.9), kind=kOutput, calls=%fused_computation.23 | convolution fusion | flops 242335744 | bytes 2785280 | tf_op jit(solution)/shard_map/dot_general | solution.py:92
  49.5 32.6 %all-gather.8.cloned.1.call-done = bf16[896,1024]{1,0:T(8,128)(2,1)} async-done(((bf16[896,128]{1,0:T(8,128)(2,1)}), bf16[896,1024]{1,0:T(8,128)(2,1)}) %all-gather.8.cloned.1.call-update) | async-done | bytes 1835024 | tf_op jit(solution)/shard_map/all_gather | solution.py:94
  82.0 3.6 %fusion.24 = (bf16[896,128]{1,0:T(8,128)(2,1)}, f32[896,128]{1,0:T(8,128)S(1)}) fusion(bf16[896,1024]{1,0:T(8,128)(2,1)} %all-gather.8.cloned.1.call-done, bf16[1024,128]{1,0:T(8,128)(2,1)} %param.10), kind=kOutput, calls=%fused_computation.26 | convolution fusion | flops 242335744 | bytes 2785280 | tf_op jit(solution)/shard_map/dot_general | solution.py:95
  86.9 13.3 %all-to-all-start.1 = ((f32[64,1,11]{2,1,0:T(1,128)}), f32[64,1,11]{2,1,0:T(1,128)S(1)}, u32[]{:S(2)}, u32[]{:S(2)}) async-start(f32[64,1,11]{2,1,0:T(1,128)} %broadcast_in_dim.85), calls=%async_computation.1 | async-start | bytes 65536 | tf_op jit(solution)/shard_map/all_to_all | solution.py:16
  101.5 10.7 %all-to-all-done.1 = f32[64,1,11]{2,1,0:T(1,128)S(1)} async-done(((f32[64,1,11]{2,1,0:T(1,128)}), f32[64,1,11]{2,1,0:T(1,128)S(1)}, u32[]{:S(2)}, u32[]{:S(2)}) %all-to-all-start.1) | async-done | bytes 2848 | tf_op jit(solution)/shard_map/all_to_all | solution.py:16
  112.1 5.1 %all-to-all-start.2 = ((bf16[44,8,128]{2,0,1:T(8,128)(2,1)}), bf16[44,8,128]{2,0,1:T(8,128)(2,1)S(1)}, u32[]{:S(2)}, u32[]{:S(2)}) async-start(bf16[44,8,128]{2,0,1:T(8,128)(2,1)} %copy.46), calls=%async_computation.2 | async-start | bytes 196608 | tf_op jit(solution)/shard_map/all_to_all | solution.py:79
  118.2 2.3 fusion.48
  122.2 13.9 %all-to-all-start = ((f32[64,1,11]{2,1,0:T(1,128)}), f32[64,1,11]{2,1,0:T(1,128)S(1)}, u32[]{:S(2)}, u32[]{:S(2)}) async-start(f32[64,1,11]{2,1,0:T(1,128)} %broadcast_in_dim.81), calls=%async_computation | async-start | bytes 65536 | tf_op jit(solution)/shard_map/all_to_all | solution.py:16
  136.8 11.2 %all-to-all-done = f32[64,1,11]{2,1,0:T(1,128)S(1)} async-done(((f32[64,1,11]{2,1,0:T(1,128)}), f32[64,1,11]{2,1,0:T(1,128)S(1)}, u32[]{:S(2)}, u32[]{:S(2)}) %all-to-all-start) | async-done | bytes 2848 | tf_op jit(solution)/shard_map/all_to_all | solution.py:16
  148.0 4.4 %all-to-all-start.4 = ((bf16[8,128,128]{2,1,0:T(8,128)(2,1)}), bf16[8,128,128]{2,1,0:T(8,128)(2,1)S(1)}, u32[]{:S(2)}, u32[]{:S(2)}) async-start(bf16[8,128,128]{2,1,0:T(8,128)(2,1)} %bitcast.4), calls=%async_computation.4 | async-start | bytes 524288 | tf_op jit(solution)/shard_map/all_to_all | solution.py:77
  152.8 13.4 %all-gather = bf16[8,44,896]{2,1,0:T(8,128)(2,1)S(1)} all-gather(bf16[1,44,896]{2,1,0:T(8,128)(2,1)S(1)} %bitcast.69), channel_id=1, replica_groups=mesh['space'=64,'tensor'=8] {'tensor'}, dimensions={0}, use_global_device_ids=true | all-gather | bytes 709632 | tf_op jit(solution)/shard_map/all_gather | solution.py:110
  167.0 27.5 %all_to_all.81 = bf16[8,896,128]{2,1,0:T(8,128)(2,1)S(1)} all-to-all(bf16[8,896,128]{2,1,0:T(8,128)(2,1)S(1)} %broadcast_in_dim.86), channel_id=1, replica_groups=mesh['space'=64,'tensor'=8] {'tensor'}, dimensions={0} | all-to-all | bytes 3670016 | tf_op jit(solution)/shard_map/all_to_all | solution.py:16
  194.5 1.3 fusion.13
  195.9 4.8 %all-to-all-start.5 = ((bf16[8,128,128]{2,1,0:T(8,128)(2,1)}), bf16[8,128,128]{2,1,0:T(8,128)(2,1)S(1)}, u32[]{:S(2)}, u32[]{:S(2)}) async-start(bf16[8,128,128]{2,1,0:T(8,128)(2,1)} %bitcast.7), calls=%async_computation.5 | async-start | bytes 524288 | tf_op jit(solution)/shard_map/all_to_all | solution.py:76
  200.7 2.5 copy.49
  203.1 2.6 fusion.7
  207.3 2.2 convolution_convert_fusion.1
  209.5 4.8 %all-to-all-start.7 = ((f32[64,1,704]{2,1,0:T(1,128)}), f32[64,1,704]{2,1,0:T(1,128)S(1)}, u32[]{:S(2)}, u32[]{:S(2)}) async-start(f32[64,1,704]{2,1,0:T(1,128)} %reshape.129), calls=%async_computation.7 | async-start | bytes 393216 | tf_op jit(solution)/shard_map/all_to_all | solution.py:31
  215.8 12.9 %all-to-all-done.7 = f32[64,1,704]{2,1,0:T(1,128)S(1)} async-done(((f32[64,1,704]{2,1,0:T(1,128)}), f32[64,1,704]{2,1,0:T(1,128)S(1)}, u32[]{:S(2)}, u32[]{:S(2)}) %all-to-all-start.7) | async-done | bytes 180256 | tf_op jit(solution)/shard_map/all_to_all | solution.py:31
  228.7 4.6 %all-to-all-start.6 = ((bf16[64,16,256]{2,1,0:T(8,128)(2,1)}), bf16[64,16,256]{2,1,0:T(8,128)(2,1)S(1)}, u32[]{:S(2)}, u32[]{:S(2)}) async-start(bf16[64,16,256]{2,1,0:T(8,128)(2,1)} %pad_maximum_fusion), calls=%async_computation.6 | async-start | bytes 1048576 | tf_op jit(solution)/shard_map/all_to_all | solution.py:48
  234.1 11.2 %psum.7 = f32[]{:T(128)} all-reduce(f32[]{:T(128)} %reduce_sum.76), channel_id=1, replica_groups=mesh['space'=64,'tensor'=8] {'tensor'}, use_global_device_ids=true, to_apply=%region_6.7 | all-reduce | flops 1 | bytes 8 | tf_op jit(solution)/shard_map/psum | solution.py:105
  248.7 3.2 %all-to-all-done.6 = bf16[64,16,256]{2,1,0:T(8,128)(2,1)S(1)} async-done(((bf16[64,16,256]{2,1,0:T(8,128)(2,1)}), bf16[64,16,256]{2,1,0:T(8,128)(2,1)S(1)}, u32[]{:S(2)}, u32[]{:S(2)}) %all-to-all-start.6) | async-done | bytes 524320 | tf_op jit(solution)/shard_map/all_to_all | solution.py:48
  252.6 2.9 %fusion.53 = f32[896,128]{1,0:T(8,128)} fusion(bf16[896,1024]{1,0:T(8,128)(2,1)} %all-gather.12.cloned.1.call-done, bf16[128,1024]{0,1:T(8,128)(2,1)S(1)} %bitcast.62), kind=kOutput, calls=%fused_computation.90 | convolution fusion | flops 234881024 | bytes 2555904 | tf_op jit(solution)/shard_map/dot_general | solution.py:58
  (73 shorter events, 14.4 us)
Async XLA Ops:
  7.2 38.6 %all-gather.6.cloned.1.call-start = ((), (), s32[]{:S(2)}) async-start(), calls=%async_computation.8 | async-start | bytes 2064384 | tf_op jit(solution)/shard_map/all_gather | solution.py:91
  7.9 74.1 %all-gather.8.cloned.1.call-start = ((), (), s32[]{:S(2)}) async-start(), calls=%async_computation.9 | async-start | bytes 2064384 | tf_op jit(solution)/shard_map/all_gather | solution.py:94
  49.4 36.3 %copy-start.5 = (s32[4,896]{1,0:T(4,128)S(1)}, s32[4,896]{1,0:T(4,128)}, u32[]{:S(2)}) copy-start(s32[4,896]{1,0:T(4,128)} %param.13) | copy-start | bytes 43012
  49.4 36.4 %copy-start.6 = (s32[11]{0:T(128)S(1)}, s32[11]{0:T(128)}, u32[]{:S(2)}) copy-start(s32[11]{0:T(128)} %param.14) | copy-start | bytes 136
  49.4 51.1 %copy-start.3 = (bf16[44,1024]{1,0:T(8,128)(2,1)S(1)}, bf16[44,1024]{1,0:T(8,128)(2,1)}, u32[]{:S(2)}) copy-start(bf16[44,1024]{1,0:T(8,128)(2,1)} %param.11) | copy-start | bytes 270340
  49.4 68.8 %all-gather.10.cloned.1.call-start = ((), (), s32[]{:S(2)}) async-start(), calls=%async_computation.10 | async-start | bytes 2064384 | tf_op jit(solution)/shard_map/all_gather | solution.py:97
  85.7 32.6 %copy-start.4 = (f32[44,896]{1,0:T(8,128)S(1)}, f32[44,896]{1,0:T(8,128)}, u32[]{:S(2)}) copy-start(f32[44,896]{1,0:T(8,128)} %param.12) | copy-start | bytes 473092
  86.9 25.3 %all-to-all-start.1 = ((f32[64,1,11]{2,1,0:T(1,128)}), f32[64,1,11]{2,1,0:T(1,128)S(1)}, u32[]{:S(2)}, u32[]{:S(2)}) async-start(f32[64,1,11]{2,1,0:T(1,128)} %broadcast_in_dim.85), calls=%async_computation.1 | async-start | bytes 65536 | tf_op jit(solution)/shard_map/all_to_all | solution.py:16
  112.1 9.4 %all-to-all-start.2 = ((bf16[44,8,128]{2,0,1:T(8,128)(2,1)}), bf16[44,8,128]{2,0,1:T(8,128)(2,1)S(1)}, u32[]{:S(2)}, u32[]{:S(2)}) async-start(bf16[44,8,128]{2,0,1:T(8,128)(2,1)} %copy.46), calls=%async_computation.2 | async-start | bytes 196608 | tf_op jit(solution)/shard_map/all_to_all | solution.py:79
  122.2 25.8 %all-to-all-start = ((f32[64,1,11]{2,1,0:T(1,128)}), f32[64,1,11]{2,1,0:T(1,128)S(1)}, u32[]{:S(2)}, u32[]{:S(2)}) async-start(f32[64,1,11]{2,1,0:T(1,128)} %broadcast_in_dim.81), calls=%async_computation | async-start | bytes 65536 | tf_op jit(solution)/shard_map/all_to_all | solution.py:16
  148.0 18.7 %all-to-all-start.4 = ((bf16[8,128,128]{2,1,0:T(8,128)(2,1)}), bf16[8,128,128]{2,1,0:T(8,128)(2,1)S(1)}, u32[]{:S(2)}, u32[]{:S(2)}) async-start(bf16[8,128,128]{2,1,0:T(8,128)(2,1)} %bitcast.4), calls=%async_computation.4 | async-start | bytes 524288 | tf_op jit(solution)/shard_map/all_to_all | solution.py:77
  152.4 100.2 %all-gather.12.cloned.1.call-start = ((), (), s32[]{:S(2)}) async-start(), calls=%async_computation.11 | async-start | bytes 2064384 | tf_op jit(solution)/shard_map/all_gather | solution.py:133
  194.5 6.2 %copy-start = (bf16[896,1024]{1,0:T(8,128)(2,1)S(1)}, bf16[896,1024]{1,0:T(8,128)(2,1)}, u32[]{:S(2)}) copy-start(bf16[896,1024]{1,0:T(8,128)(2,1)} %all-gather.10.cloned.1.call-done) | copy-start | bytes 5505028
  195.9 13.6 %all-to-all-start.5 = ((bf16[8,128,128]{2,1,0:T(8,128)(2,1)}), bf16[8,128,128]{2,1,0:T(8,128)(2,1)S(1)}, u32[]{:S(2)}, u32[]{:S(2)}) async-start(bf16[8,128,128]{2,1,0:T(8,128)(2,1)} %bitcast.7), calls=%async_computation.5 | async-start | bytes 524288 | tf_op jit(solution)/shard_map/all_to_all | solution.py:76
  206.1 8.3 %copy-start.1 = (bf16[896,1024]{1,0:T(8,128)(2,1)S(1)}, bf16[896,1024]{1,0:T(8,128)(2,1)}, u32[]{:S(2)}) copy-start(bf16[896,1024]{1,0:T(8,128)(2,1)} %all-gather.6.cloned.1.call-done) | copy-start | bytes 5505028
  206.1 8.3 %copy-start.2 = (bf16[896,128]{1,0:T(8,128)(2,1)S(1)}, bf16[896,128]{1,0:T(8,128)(2,1)}, u32[]{:S(2)}) copy-start(bf16[896,128]{1,0:T(8,128)(2,1)} %fusion.13) | copy-start | bytes 688132
  209.5 19.2 %all-to-all-start.7 = ((f32[64,1,704]{2,1,0:T(1,128)}), f32[64,1,704]{2,1,0:T(1,128)S(1)}, u32[]{:S(2)}, u32[]{:S(2)}) async-start(f32[64,1,704]{2,1,0:T(1,128)} %reshape.129), calls=%async_computation.7 | async-start | bytes 393216 | tf_op jit(solution)/shard_map/all_to_all | solution.py:31
  228.7 23.2 %all-to-all-start.6 = ((bf16[64,16,256]{2,1,0:T(8,128)(2,1)}), bf16[64,16,256]{2,1,0:T(8,128)(2,1)S(1)}, u32[]{:S(2)}, u32[]{:S(2)}) async-start(bf16[64,16,256]{2,1,0:T(8,128)(2,1)} %pad_maximum_fusion), calls=%async_computation.6 | async-start | bytes 1048576 | tf_op jit(solution)/shard_map/all_to_all | solution.py:48
Sparse Core Ops, SparseCore 0:
  10.1 35.5 all-gather.5
  49.5 32.4 all-gather.7
  85.8 32.3 all-gather.9
  196.0 23.8 all-gather.11
where the time goes:
time: 264 us; the launch traced here: 263 us
  waiting for transfers between devices  111 us (42%)
  blocking collectives  52.2 us (20%)
  starting transfers between devices  51 us (19%)
  matrix products  19.4 us (7%)
  between operations  16.5 us (6%)
  local copies, waits for them, and re-layouts  9.01 us (3%)
  other arithmetic  4.24 us (2%)
    all_gather x1, waiting for transfers between devices, per_device(): full_in = lax.all_gather(tokens, 'tensor', axis=1, tiled=True)  37.8 us
    all_gather x1, waiting for transfers between devices, per_device(): full_one = lax.all_gather(hidden_one, 'tensor', axis=1, tiled=True)  32.6 us
    all_to_all x1, blocking collectives, sent_to_all(): return lax.all_to_all(copies, axis, split_axis=0, concat_axis=0, tiled=True)  27.5 us
    all_to_all x2, starting transfers between devices, sent_to_all(): return lax.all_to_all(copies, axis, split_axis=0, concat_axis=0, tiled=True)  27.2 us
    all_to_all x2, waiting for transfers between devices, sent_to_all(): return lax.all_to_all(copies, axis, split_axis=0, concat_axis=0, tiled=True)  21.8 us
    all_gather x1, blocking collectives, per_device(): lax.all_gather(grad_pred, 'tensor', axis=0, tiled=True)  13.4 us
    all_to_all x1, waiting for transfers between devices, sent_and_summed(): parts = lax.all_to_all(split_up(shard, dim, size), axis, 0, 0, tiled=True)  12.9 us
    psum x1, blocking collectives, per_device(): loss = lax.psum(jnp.sum(root), 'tensor') / V  11.2 us
  transfers between devices with their start and end apart: 11, of which 8 were waited for; matrix products, arithmetic and copies ran while one was open for 8% of the time, Pallas kernels for 0%

commit v1 on v0

v1 whole, which is shorter than its diff:
```python
import math

import jax
import jax.numpy as jnp
from jax import lax
from jax.experimental import pallas as pl
from jax.experimental.pallas import tpu as pltpu
from jax.sharding import Mesh
from jax.sharding import PartitionSpec as P

V = 88
PP = 4
LONP = 224
D = 1024
OWN = 112
HEAD = 48
COLS = 8 * HEAD
BF = jnp.bfloat16
F32 = jnp.float32
SPACE = ("z", "y")
TENSOR = ("x", "core")
OFFS = (0, 3, 1, 2)


def dot(a, b, da, db):
    return lax.dot_general(a, b, (((da,), (db,)), ((), ())), preferred_element_type=F32)


def lanes(j):
    return pl.ds(pl.multiple_of(j * 128, 128), 128)


def call(body, name, outs, args, smem=(), scratch=(), flops=0, vmem=56):
    specs = [
        pl.BlockSpec(memory_space=pltpu.SMEM if i in smem else pltpu.VMEM) for i in range(len(args))
    ]
    return pl.pallas_call(
        body,
        name=name,
        out_shape=tuple(jax.ShapeDtypeStruct(s, t) for s, t in outs),
        in_specs=specs,
        out_specs=tuple(pl.BlockSpec(memory_space=pltpu.VMEM) for _ in outs),
        scratch_shapes=list(scratch),
        compiler_params=pltpu.CompilerParams(vmem_limit_bytes=vmem * 2**20),
        cost_estimate=pl.CostEstimate(flops=flops, bytes_accessed=4 * 2**20, transcendentals=0),
    )(*args)


def prep_body(head, second, targets, kinds, packed, tgt):
    packed[:D, :] = second[...]
    for i in range(8):
        packed[D + HEAD * i : D + HEAD * (i + 1), :] = head[:, 128 * i : 128 * (i + 1)]
        tgt[i, :, :OWN] = targets[:, OWN * i : OWN * (i + 1)]
        tgt[i, :, OWN:] = jnp.broadcast_to(kinds[...], (HEAD, 128 - OWN))


def gelu_parts(z):
    cdf = 0.5 * (1.0 + lax.erf(z * (1.0 / math.sqrt(2.0))))
    return z * cdf, cdf + z * jnp.exp(-0.5 * z * z) * (1.0 / math.sqrt(2.0 * math.pi))


def pairs(near, far):
    for a, ref in enumerate((near, far)):
        for s in (0, 2):
            yield ref, s, 4 * a + s


def forward_body(
    idx, tok, w1n, w1f, w2n, w2f, tgt, land, weights,
    xh, slope1, slope2, hidden2, me, sums, head, pre,
):
    for j in range(8):
        xh[:, 128 * j : 128 * (j + 1)] = tok[j]
    for a, ref in enumerate((w2n, w2f)):
        for s in range(4):
            rows = pl.ds(pl.multiple_of(idx[4 * a + s] * HEAD, HEAD), HEAD)
            for i in range(8):
                head[rows, 128 * i : 128 * (i + 1)] = ref[s, D + HEAD * i : D + HEAD * (i + 1), :]

    def layer(value, near, far):
        for ref, s, at in pairs(near, far):
            both = jnp.concatenate([ref[s, :D, :], ref[s + 1, :D, :]], axis=1)
            z = dot(value, both, 1, 0)
            pre[:, lanes(idx[at])] = z[:, :128]
            pre[:, lanes(idx[at + 1])] = z[:, 128:]

    layer(xh[:, :D], w1n, w1f)
    hidden, slope = gelu_parts(pre[...])
    xh[:, D:] = hidden.astype(BF)
    slope1[...] = slope
    layer(xh[:, D:], w2n, w2f)
    hidden, slope = gelu_parts(pre[...])
    hidden2[...] = hidden.astype(BF)
    slope2[...] = slope
    predicted = dot(hidden2[...], head[...], 1, 1)
    flipped = tgt[...].reshape(COLS, 128).T
    kind = flipped[OWN : OWN + 1, :]
    column = lax.broadcasted_iota(jnp.int32, (8, COLS), 1)
    picks = (column % PP == lax.broadcasted_iota(jnp.int32, (8, COLS), 0)).astype(BF)
    on_land = dot(land[...], picks, 0, 0)[:OWN, :]
    valid = jnp.where(kind == 0.0, 1.0, jnp.where(kind == 1.0, on_land, 1.0 - on_land))
    masked = weights[...] * valid
    error = predicted - flipped[:OWN, :]
    product = masked * error
    me[...] = product
    sums[0:1, :] = jnp.sum(product * error, axis=0, keepdims=True)
    sums[1:2, :] = jnp.sum(masked, axis=0, keepdims=True)


def head_body(idx, me, hidden2, keep, send, full):
    full[...] = dot(me[...].astype(BF), hidden2[...], 0, 0)
    core = idx[8]
    for k in range(4):
        for ref, c in ((keep, core), (send, 1 - core)):
            rows = pl.ds(pl.multiple_of((2 * k + c) * HEAD, HEAD), HEAD)
            ref[k] = full[rows, :].astype(BF)


def pair_body(idx, keep, came, own, up, down, across):
    x = idx[9]
    for ref, off in ((own, 0), (up, 1), (down, 3), (across, 2)):
        k = lax.rem(x + off, 4)
        ref[...] = (keep[k].astype(F32) + came[k].astype(F32)).astype(BF)


def over_cells(v):
    column = lax.broadcasted_iota(jnp.int32, v.shape, 1)
    n = v.shape[1]
    for step in (1, 2):
        ahead = pltpu.roll(v, n - step, 1)
        behind = pltpu.roll(v, step, 1)
        v = v + jnp.where((column // step) % 2 == 0, ahead, behind)
    return v


def backward_body(
    idx, scale, sums, me, slope1, slope2, head, w2n, w2f, joined, grad1, coefs, loss, g2
):
    total = over_cells(jnp.sum(sums[...], axis=0))
    column = lax.broadcasted_iota(jnp.int32, (1, COLS), 1)
    real = column % HEAD < V * PP // 8
    weight = jnp.where(real, total[1:2, :], 1.0)
    root = jnp.sqrt(total[0:1, :] / weight + 1e-06)
    loss[...] = jnp.sum(jnp.where(real, root, 0.0), axis=1, keepdims=True) / (V * PP)
    coef = jnp.where(real, scale[0] / (V * root * weight), 0.0)
    coefs[...] = coef
    grad_pred = (coef * me[...]).astype(BF)
    g2[...] = (dot(grad_pred, head[...], 1, 0) * slope2[...]).astype(BF)
    back = jnp.zeros((OWN, D), F32)
    for ref, s, at in pairs(w2n, w2f):
        both = jnp.concatenate([ref[s, :D, :], ref[s + 1, :D, :]], axis=1)
        left = jnp.concatenate([g2[:, lanes(idx[at])], g2[:, lanes(idx[at + 1])]], axis=1)
        back += dot(left, both, 1, 1)
    grad1[...] = (back * slope1[...]).astype(BF)
    for j in range(8):
        joined[j, :, :128] = g2[:, 128 * j : 128 * (j + 1)]
        joined[j, :, 128:] = grad1[:, 128 * j : 128 * (j + 1)]


def token_body(idx, grad1, w1n, w1f, out):
    grad = jnp.zeros((OWN, D), F32)
    for ref, s, at in pairs(w1n, w1f):
        both = jnp.concatenate([ref[s], ref[s + 1]], axis=1)
        left = jnp.concatenate([grad1[:, lanes(idx[at])], grad1[:, lanes(idx[at + 1])]], axis=1)
        grad += dot(left, both, 1, 1)
    for j in range(8):
        out[j] = grad[:, 128 * j : 128 * (j + 1)]


def weight_body(idx, xhn, xhf, joined, own, a, b, c, out, order):
    for at in range(8):
        order[OWN * at : OWN * (at + 1), :] = joined[idx[at]]
    half = 4 * OWN
    near, far = xhn[...].reshape(half, 2 * D), xhf[...].reshape(half, 2 * D)
    for to, at in ((0, D), (128, 0)):
        grad = dot(order[:half, to : to + 128], near[:, at : at + D], 0, 0)
        grad += dot(order[half:, to : to + 128], far[:, at : at + D], 0, 0)
        out[:, :, to : to + 128] = grad.T.astype(BF).reshape(64, 16, 128)
    part = own[...].astype(F32) + a[...].astype(F32) + b[...].astype(F32) + c[...].astype(F32)
    part = jnp.concatenate([part, jnp.zeros((128 - HEAD, D), F32)], axis=0)
    out[:, :, 256:] = part.T.astype(BF).reshape(64, 16, 128)


def shift(v, by):
    return lax.ppermute(v, "x", [(i, (i + by) % 4) for i in range(4)])


def flip(v):
    return lax.ppermute(v, "core", [(0, 1), (1, 0)])


def per_device(
    tokens, first_weight, second_weight, head_weight, targets, land_mask, variable_kind, loss_scale
):
    x, core = lax.axis_index("x"), lax.axis_index("core")
    mine = lax.axis_index(TENSOR)
    places = [2 * ((x + off) % 4) + c for c in (core, 1 - core) for off in OFFS]
    idx = jnp.stack([*places, core, x]).astype(jnp.int32)

    padded_head = jnp.pad(head_weight, ((0, HEAD - 44), (0, 0)))
    padded_targets = jnp.pad(targets, ((0, HEAD - 44), (0, 0)))
    kinds = jnp.pad(jnp.repeat(variable_kind, PP), (0, HEAD - 44)).astype(F32)[:, None]
    packed, tgt = call(
        prep_body, "prep", [((D + COLS, 128), BF), ((8, HEAD, 128), F32)],
        [padded_head, second_weight, padded_targets, kinds],
    )

    own_tokens = lax.all_to_all(tokens.reshape(8, OWN, 128), TENSOR, 0, 0, tiled=True)
    w1_m1, w1_p1 = shift(first_weight, 1), shift(first_weight, 3)
    w2_m1, w2_p1 = shift(packed, 1), shift(packed, 3)
    w1_p2, w2_p2 = shift(w1_m1, 1), shift(w2_p1, 3)
    w1n = jnp.stack([first_weight, w1_m1, w1_p1, w1_p2])
    w2n = jnp.stack([packed, w2_m1, w2_p1, w2_p2])
    w1f, w2f = flip(w1n), flip(w2n)
    tgt = lax.all_to_all(tgt, TENSOR, 0, 0, tiled=True)

    land = lax.dynamic_slice(land_mask, (0, mine * OWN), (PP, OWN))
    land = jnp.pad(land.astype(BF), ((0, 8 - PP), (0, 128 - OWN)))
    space = lax.axis_index(SPACE)
    patch_row = (space * 8 * OWN + mine * OWN) // LONP
    nlat = 2 * (64 * 8 * OWN // LONP)
    col = jnp.arange(COLS, dtype=jnp.int32)
    lat_row = 2 * patch_row + (col % PP) // 2
    weights = jnp.cos(math.pi / 2.0 * (lat_row.astype(F32) + 0.5) / nlat)
    weights = jnp.where(col % HEAD < 44, weights, 0.0)[None, :]

    xh, slope1, slope2, hidden2, me, sums, head = call(
        forward_body, "forward",
        [((OWN, 2 * D), BF), ((OWN, D), F32), ((OWN, D), F32), ((OWN, D), BF), ((OWN, COLS), F32),
         ((2, COLS), F32), ((COLS, D), BF)],
        [idx, own_tokens, w1n, w1f, w2n, w2f, tgt, land, weights],
        smem=(0,), scratch=[pltpu.VMEM((OWN, D), F32)], flops=10**9,
    )

    sums = jnp.sum(
        lax.all_to_all(jnp.broadcast_to(sums, (8, 2, COLS)), TENSOR, 0, 0, tiled=True), axis=0
    )
    sums = lax.all_to_all(jnp.broadcast_to(sums, (64, 2, COLS)), SPACE, 0, 0, tiled=True)

    xhn = jnp.stack([xh, shift(xh, 1), shift(xh, 3), shift(xh, 2)])
    xhf = flip(xhn)
    keep, send = call(
        head_body, "head_part", [((4, HEAD, D), BF)] * 2, [idx, me, hidden2],
        smem=(0,), scratch=[pltpu.VMEM((COLS, D), F32)], flops=10**8,
    )
    own, up, down, across = call(
        pair_body, "pair", [((HEAD, D), BF)] * 4, [idx, keep, flip(send)], smem=(0,)
    )
    head_parts = [own, shift(up, 1), shift(down, 3), shift(across, 2)]

    joined, grad1, coefs, loss = call(
        backward_body, "backward",
        [((8, OWN, 256), BF), ((OWN, D), BF), ((1, COLS), F32), ((1, 1), F32)],
        [idx, loss_scale.reshape(1), sums, me, slope1, slope2, head, w2n, w2f],
        smem=(0, 1), scratch=[pltpu.VMEM((OWN, D), BF)], flops=5 * 10**8,
    )
    joined = lax.all_to_all(joined, TENSOR, 0, 0, tiled=True)
    (token_grad,) = call(
        token_body, "token", [((8, OWN, 128), F32)], [idx, grad1, w1n, w1f], smem=(0,), flops=3 * 10**8
    )
    (out,) = call(
        weight_body, "weight", [((64, 16, 384), BF)], [idx, xhn, xhf, joined, *head_parts],
        smem=(0,), scratch=[pltpu.VMEM((8 * OWN, 256), BF)], flops=5 * 10**8,
    )
    out = lax.all_to_all(out, SPACE, 0, 0, tiled=True)
    token_grad = lax.all_to_all(token_grad, TENSOR, 0, 0, tiled=True).reshape(8 * OWN, 128)
    out = jnp.sum(out.astype(F32), axis=0)
    local = lax.dynamic_slice(coefs, (0, mine * HEAD), (1, 44))
    head_grad = (out[:, 256:300] * local).T
    return loss.reshape(()), token_grad, out[:, 128:256], out[:, :128], head_grad


def solution(mesh):
    inner = Mesh(mesh.devices.reshape(8, 8, 4, 2), ("z", "y", "x", "core"))
    return jax.shard_map(
        per_device,
        mesh=inner,
        in_specs=(
            P(SPACE, TENSOR),
            P(None, TENSOR),
            P(None, TENSOR),
            P(TENSOR, None),
            P(TENSOR, SPACE),
            P(None, SPACE),
            P(TENSOR),
            P(),
        ),
        out_specs=(
            P(),
            P(SPACE, TENSOR),
            P(SPACE, TENSOR),
            P(SPACE, TENSOR),
            P(TENSOR, SPACE),
        ),
        check_vma=False,
    )
```

time: 264 us -> 220 us (0.83)
  the two profiles are of different devices: /device:TPU:2 before, /device:TPU:8 now
where the time goes in v1:
time: 220 us; the launch traced here: 219 us
  starting transfers between devices  86.2 us (39%)
  waiting for transfers between devices  82.9 us (38%)
  Pallas kernels  23.3 us (11%)
  local copies, waits for them, and re-layouts  11.9 us (5%)
  blocking collectives  7.81 us (4%)
  other arithmetic  4.74 us (2%)
    ppermute x12, starting transfers between devices, shift(): return lax.ppermute(v, 'x', [(i, (i + by) % 4) for i in range(4)])  41.3 us
    ppermute x12, waiting for transfers between devices, shift(): return lax.ppermute(v, 'x', [(i, (i + by) % 4) for i in range(4)])  34 us
    all_to_all x1, waiting for transfers between devices, per_device(): out = lax.all_to_all(out, SPACE, 0, 0, tiled=True)  23.4 us
    pallas_call x7, Pallas kernels, call(): pl.pallas_call(body, name=name, out_shape=tuple((jax.ShapeDtypeStruct(s,...  23.3 us
    all_to_all x1, starting transfers between devices, per_device(): lax.all_to_all(jnp.broadcast_to(sums, (64, 2, COLS)), SPACE, 0, 0, tiled=...  16.6 us
    all_to_all x1, waiting for transfers between devices, per_device(): lax.all_to_all(jnp.broadcast_to(sums, (64, 2, COLS)), SPACE, 0, 0, tiled=...  12.4 us
    ppermute x4, starting transfers between devices, flip(): return lax.ppermute(v, 'core', [(0, 1), (1, 0)])  8.06 us
    all_to_all x1, blocking collectives, per_device(): lax.all_to_all(jnp.broadcast_to(sums, (8, 2, COLS)), TENSOR, 0, 0, tiled=...  7.81 us
  transfers between devices with their start and end apart: 22, of which 12 were waited for; matrix products, arithmetic and copies ran while one was open for 2% of the time, Pallas kernels for 7%

profile of v1, /device:TPU:8, one launch (start us, length us, event | category | flops | bytes accessed | tf_op | source)
XLA Modules:
  0.0 218.5 jit_solution(1859558365594177571)
XLA Ops:
  7.3 4.8 %collective-permute-start.5 = (bf16[1408,128]{1,0:T(8,128)(2,1)}, bf16[1408,128]{1,0:T(8,128)(2,1)S(1)}, u32[]{:S(2)}, u32[]{:S(2)}) collective-permute-start(bf16[1408,128]{1,0:T(8,128)(2,1)} %get-tuple-element.24), channel_id=1, source_target_pairs={{0,6},{2,0},{4,2},{6,4},{1,7},{3,1},{5,3},{7,5},{8,14},{10,8},{12,... | collective-permute-start | bytes 1081352 | tf_op jit(solution)/shard_map/ppermute | solution.py:185
  14.0 6.0 %collective-permute-done.5 = bf16[1408,128]{1,0:T(8,128)(2,1)S(1)} collective-permute-done((bf16[1408,128]{1,0:T(8,128)(2,1)}, bf16[1408,128]{1,0:T(8,128)(2,1)S(1)}, u32[]{:S(2)}, u32[]{:S(2)}) %collective-permute-start.5) | collective-permute-done | bytes 360480 | tf_op jit(solution)/shard_map/ppermute | solution.py:185
  20.1 5.5 %collective-permute-start.6 = (bf16[1408,128]{1,0:T(8,128)(2,1)S(1)}, bf16[1408,128]{1,0:T(8,128)(2,1)S(1)}, u32[]{:S(2)}, u32[]{:S(2)}) collective-permute-start(bf16[1408,128]{1,0:T(8,128)(2,1)S(1)} %collective-permute-done.5), channel_id=1, source_target_pairs={{0,6},{2,0},{4,2},{6,4},{1,7},{3,1},{5,3},{7,5},{8,14},{10,8},{12,... | collective-permute-start | bytes 1081352 | tf_op jit(solution)/shard_map/ppermute | solution.py:185
  27.5 5.1 %collective-permute-start.1 = (bf16[1024,128]{1,0:T(8,128)(2,1)}, bf16[1024,128]{1,0:T(8,128)(2,1)S(1)}, u32[]{:S(2)}, u32[]{:S(2)}) collective-permute-start(bf16[1024,128]{1,0:T(8,128)(2,1)} %param.9), channel_id=1, source_target_pairs={{0,6},{2,0},{4,2},{6,4},{1,7},{3,1},{5,3},{7,5},{8,14},{10,8},{12,... | collective-permute-start | bytes 786440 | tf_op jit(solution)/shard_map/ppermute | solution.py:185
  40.8 4.4 %collective-permute-done.2 = bf16[1024,128]{1,0:T(8,128)(2,1)S(1)} collective-permute-done((bf16[1024,128]{1,0:T(8,128)(2,1)S(1)}, bf16[1024,128]{1,0:T(8,128)(2,1)S(1)}, u32[]{:S(2)}, u32[]{:S(2)}) %collective-permute-start.2) | collective-permute-done | bytes 262176 | tf_op jit(solution)/shard_map/ppermute | solution.py:185
  47.3 4.0 %all-to-all-start.1 = ((f32[8,48,128]{2,1,0:T(8,128)}), f32[8,48,128]{2,1,0:T(8,128)}, u32[]{:S(2)}, u32[]{:S(2)}) async-start(f32[8,48,128]{2,1,0:T(8,128)} %get-tuple-element.25), calls=%async_computation.1 | async-start | bytes 393216 | tf_op jit(solution)/shard_map/all_to_all | solution.py:215
  51.4 6.8 %all-to-all-done.1.tgt = f32[8,48,128]{2,1,0:T(8,128)} async-done(((f32[8,48,128]{2,1,0:T(8,128)}), f32[8,48,128]{2,1,0:T(8,128)}, u32[]{:S(2)}, u32[]{:S(2)}) %all-to-all-start.1) | async-done | bytes 196640 | tf_op jit(solution)/shard_map/all_to_all | solution.py:215
  58.2 4.0 %all-to-all-start = ((bf16[8,112,128]{2,1,0:T(8,128)(2,1)}), bf16[8,112,128]{2,1,0:T(8,128)(2,1)}, u32[]{:S(2)}, u32[]{:S(2)}) async-start(bf16[8,112,128]{2,1,0:T(8,128)(2,1)} %bitcast.46), calls=%async_computation | async-start | bytes 458752 | tf_op jit(solution)/shard_map/all_to_all | solution.py:208
  64.8 4.6 %all-to-all-done.tok = bf16[8,112,128]{2,1,0:T(8,128)(2,1)} async-done(((bf16[8,112,128]{2,1,0:T(8,128)(2,1)}), bf16[8,112,128]{2,1,0:T(8,128)(2,1)}, u32[]{:S(2)}, u32[]{:S(2)}) %all-to-all-start) | async-done | bytes 229408 | tf_op jit(solution)/shard_map/all_to_all | solution.py:208
  70.5 5.2 %forward.1 = (bf16[112,2048]{1,0:T(8,128)(2,1)}, f32[112,1024]{1,0:T(8,128)}, f32[112,1024]{1,0:T(8,128)}, bf16[112,1024]{1,0:T(8,128)(2,1)}, f32[112,384]{1,0:T...) custom-call(s32[10]{0:T(128)} %stack.88.idx, bf16[8,112,128]{2,1,0:T(8,128)(2,1)} %all-to-all-done.tok, ...), custom_call_target="tpu_custom_call" | custom-call | flops 1000000000 | bytes 4194304 | tf_op jit(solution)/shard_map/forward/pallas_call | solution.py:37
  78.0 4.7 %collective-permute-start.9 = (bf16[112,2048]{1,0:T(8,128)(2,1)}, bf16[112,2048]{1,0:T(8,128)(2,1)S(1)}, u32[]{:S(2)}, u32[]{:S(2)}) collective-permute-start(bf16[112,2048]{1,0:T(8,128)(2,1)} %get-tuple-element.33), channel_id=1, source_target_pairs={{0,6},{2,0},{4,2},{6,4},{1,7},{3,1},{5,3},{7,5},{8,14},{10,8},{12,... | collective-permute-start | bytes 1376264 | tf_op jit(solution)/shard_map/ppermute | solution.py:185
  84.6 8.1 %collective-permute-done.10 = bf16[112,2048]{1,0:T(8,128)(2,1)S(1)} collective-permute-done((bf16[112,2048]{1,0:T(8,128)(2,1)}, bf16[112,2048]{1,0:T(8,128)(2,1)S(1)}, u32[]{:S(2)}, u32[]{:S(2)}) %collective-permute-start.10) | collective-permute-done | bytes 458784 | tf_op jit(solution)/shard_map/ppermute | solution.py:185
  92.7 6.8 %collective-permute-done.9 = bf16[112,2048]{1,0:T(8,128)(2,1)S(1)} collective-permute-done((bf16[112,2048]{1,0:T(8,128)(2,1)}, bf16[112,2048]{1,0:T(8,128)(2,1)S(1)}, u32[]{:S(2)}, u32[]{:S(2)}) %collective-permute-start.9) | collective-permute-done | bytes 458784 | tf_op jit(solution)/shard_map/ppermute | solution.py:185
  104.2 7.8 %all_to_all.35 = f32[8,2,384]{2,1,0:T(2,128)S(1)} all-to-all(f32[8,2,384]{2,1,0:T(2,128)S(1)} %broadcast_in_dim.20), channel_id=1, replica_groups=mesh['z'=8,'y'=8,'x'=4,'core'=2] {'x','core'}, dimensions={0} | all-to-all | bytes 49152 | tf_op jit(solution)/shard_map/all_to_all | solution.py:236
  112.8 16.6 %all-to-all-start.3 = ((f32[64,2,384]{2,1,0:T(2,128)}), f32[64,2,384]{2,1,0:T(2,128)S(1)}, u32[]{:S(2)}, u32[]{:S(2)}) async-start(f32[64,2,384]{2,1,0:T(2,128)} %broadcast_in_dim.21), calls=%async_computation.3 | async-start | bytes 393216 | tf_op jit(solution)/shard_map/all_to_all | solution.py:238
  130.0 12.4 %all-to-all-done.3.sums = f32[64,2,384]{2,1,0:T(2,128)S(1)} async-done(((f32[64,2,384]{2,1,0:T(2,128)}), f32[64,2,384]{2,1,0:T(2,128)S(1)}, u32[]{:S(2)}, u32[]{:S(2)}) %all-to-all-start.3) | async-done | bytes 196640 | tf_op jit(solution)/shard_map/all_to_all | solution.py:238
  143.1 4.7 %backward.1 = (bf16[8,112,256]{2,1,0:T(8,128)(2,1)}, bf16[112,1024]{1,0:T(8,128)(2,1)}, f32[1,384]{1,0:T(1,128)}, f32[1,1]{1,0:T(1,128)}) custom-call(s32[10]{0:T(128)} %stack.88.idx, f32[1]{0:T(128)} %bitcast.32.scale, f32[64,2,384]{2,1,0:T(2,128)} %copy-done.5, f32[112,384]{1,0:T(8,128)} %get-tuple-element.27.me, f32[112,1024]{1,0:T(8,128)} %get-tuple-element.28.slope1, ...), custom_call_target="tpu_custom_call" | custom-call | flops 500000000 | bytes 4194304 | tf_op jit(solution)/shard_map/backward/pallas_call | solution.py:37
  147.8 3.5 %all-to-all-start.5 = ((bf16[8,112,256]{2,1,0:T(8,128)(2,1)}), bf16[8,112,256]{2,1,0:T(8,128)(2,1)S(1)}, u32[]{:S(2)}, u32[]{:S(2)}) async-start(bf16[8,112,256]{2,1,0:T(8,128)(2,1)} %get-tuple-element.34), calls=%async_computation.5 | async-start | bytes 917504 | tf_op jit(solution)/shard_map/all_to_all | solution.py:257
  167.1 3.8 %collective-permute-start.13 = (bf16[48,1024]{1,0:T(8,128)(2,1)}, bf16[48,1024]{1,0:T(8,128)(2,1)S(1)}, u32[]{:S(2)}, u32[]{:S(2)}) collective-permute-start(bf16[48,1024]{1,0:T(8,128)(2,1)} %get-tuple-element.39), channel_id=1, source_target_pairs={{0,2},{2,4},{4,6},{6,0},{1,3},{3,5},{5,7},{7,1},{8,10},{10,12},{12... | collective-permute-start | bytes 294920 | tf_op jit(solution)/shard_map/ppermute | solution.py:185
  174.2 4.1 %collective-permute-start.15 = (bf16[48,1024]{1,0:T(8,128)(2,1)}, bf16[48,1024]{1,0:T(8,128)(2,1)S(1)}, u32[]{:S(2)}, u32[]{:S(2)}) collective-permute-start(bf16[48,1024]{1,0:T(8,128)(2,1)} %get-tuple-element.41), channel_id=1, source_target_pairs={{0,4},{2,6},{4,0},{6,2},{1,5},{3,7},{5,1},{7,3},{8,12},{10,14},{12... | collective-permute-start | bytes 294920 | tf_op jit(solution)/shard_map/ppermute | solution.py:185
  178.3 4.0 %collective-permute-done.15.c = bf16[48,1024]{1,0:T(8,128)(2,1)S(1)} collective-permute-done((bf16[48,1024]{1,0:T(8,128)(2,1)}, bf16[48,1024]{1,0:T(8,128)(2,1)S(1)}, u32[]{:S(2)}, u32[]{:S(2)}) %collective-permute-start.15) | collective-permute-done | bytes 98336 | tf_op jit(solution)/shard_map/ppermute | solution.py:185
  183.0 4.0 %weight.1 = bf16[64,16,384]{2,1,0:T(8,128)(2,1)} custom-call(s32[10]{0:T(128)} %stack.88.idx, bf16[4,112,2048]{2,1,0:T(8,128)(2,1)} %copy-done.2, bf16[4,112,2048]{2,1,0:T(8,128)(2,1)} %collective-permute-done.11.xhf, bf16[8,112,256]{2,1,0:T(8,128)(2,1)} %copy-done.4, bf16[48,1024]{1,0:T(8,128)(2,1)} %get-tuple-element.38.own, bf16[48,1024]{1,0:T(8,128)(2,1)} %copy-done.8, ...), custom_call_target="tpu_custom_call" | custom-call | flops 500000000 | bytes 4194304 | tf_op jit(solution)/shard_map/weight/pallas_call | solution.py:37
  187.1 5.2 %all-to-all-start.6 = ((bf16[64,16,384]{2,1,0:T(8,128)(2,1)}), bf16[64,16,384]{2,1,0:T(8,128)(2,1)S(1)}, u32[]{:S(2)}, u32[]{:S(2)}) async-start(bf16[64,16,384]{2,1,0:T(8,128)(2,1)} %weight.1), calls=%async_computation.6 | async-start | bytes 1572864 | tf_op jit(solution)/shard_map/all_to_all | solution.py:265
  193.0 23.4 %all-to-all-done.6 = bf16[64,16,384]{2,1,0:T(8,128)(2,1)S(1)} async-done(((bf16[64,16,384]{2,1,0:T(8,128)(2,1)}), bf16[64,16,384]{2,1,0:T(8,128)(2,1)S(1)}, u32[]{:S(2)}, u32[]{:S(2)}) %all-to-all-start.6) | async-done | bytes 786464 | tf_op jit(solution)/shard_map/all_to_all | solution.py:265
  (73 shorter events, 57.2 us)
Async XLA Ops:
  7.3 37.9 %copy-start.7 = (bf16[1024,128]{1,0:T(8,128)(2,1)S(1)}, bf16[1024,128]{1,0:T(8,128)(2,1)}, u32[]{:S(2)}) copy-start(bf16[1024,128]{1,0:T(8,128)(2,1)} %param.9) | copy-start | bytes 786436
  7.3 12.8 %collective-permute-start.5 = (bf16[1408,128]{1,0:T(8,128)(2,1)}, bf16[1408,128]{1,0:T(8,128)(2,1)S(1)}, u32[]{:S(2)}, u32[]{:S(2)}) collective-permute-start(bf16[1408,128]{1,0:T(8,128)(2,1)} %get-tuple-element.24), channel_id=1, source_target_pairs={{0,6},{2,0},{4,2},{6,4},{1,7},{3,1},{5,3},{7,5},{8,14},{10,8},{12,... | collective-permute-start | bytes 1081352 | tf_op jit(solution)/shard_map/ppermute | solution.py:185
  12.1 25.6 %collective-permute-start.4 = (bf16[1408,128]{1,0:T(8,128)(2,1)}, bf16[1408,128]{1,0:T(8,128)(2,1)S(1)}, u32[]{:S(2)}, u32[]{:S(2)}) collective-permute-start(bf16[1408,128]{1,0:T(8,128)(2,1)} %get-tuple-element.24), channel_id=1, source_target_pairs={{0,2},{2,4},{4,6},{6,0},{1,3},{3,5},{5,7},{7,1},{8,10},{10,12},{12... | collective-permute-start | bytes 1081352 | tf_op jit(solution)/shard_map/ppermute | solution.py:185
  20.1 17.6 %collective-permute-start.6 = (bf16[1408,128]{1,0:T(8,128)(2,1)S(1)}, bf16[1408,128]{1,0:T(8,128)(2,1)S(1)}, u32[]{:S(2)}, u32[]{:S(2)}) collective-permute-start(bf16[1408,128]{1,0:T(8,128)(2,1)S(1)} %collective-permute-done.5), channel_id=1, source_target_pairs={{0,6},{2,0},{4,2},{6,4},{1,7},{3,1},{5,3},{7,5},{8,14},{10,8},{12,... | collective-permute-start | bytes 1081352 | tf_op jit(solution)/shard_map/ppermute | solution.py:185
  25.5 10.2 %collective-permute-start = (bf16[1024,128]{1,0:T(8,128)(2,1)}, bf16[1024,128]{1,0:T(8,128)(2,1)S(1)}, u32[]{:S(2)}, u32[]{:S(2)}) collective-permute-start(bf16[1024,128]{1,0:T(8,128)(2,1)} %param.9), channel_id=1, source_target_pairs={{0,2},{2,4},{4,6},{6,0},{1,3},{3,5},{5,7},{7,1},{8,10},{10,12},{12... | collective-permute-start | bytes 786440 | tf_op jit(solution)/shard_map/ppermute | solution.py:185
  27.5 13.3 %collective-permute-start.1 = (bf16[1024,128]{1,0:T(8,128)(2,1)}, bf16[1024,128]{1,0:T(8,128)(2,1)S(1)}, u32[]{:S(2)}, u32[]{:S(2)}) collective-permute-start(bf16[1024,128]{1,0:T(8,128)(2,1)} %param.9), channel_id=1, source_target_pairs={{0,6},{2,0},{4,2},{6,4},{1,7},{3,1},{5,3},{7,5},{8,14},{10,8},{12,... | collective-permute-start | bytes 786440 | tf_op jit(solution)/shard_map/ppermute | solution.py:185
  35.8 9.5 %collective-permute-start.2 = (bf16[1024,128]{1,0:T(8,128)(2,1)S(1)}, bf16[1024,128]{1,0:T(8,128)(2,1)S(1)}, u32[]{:S(2)}, u32[]{:S(2)}) collective-permute-start(bf16[1024,128]{1,0:T(8,128)(2,1)S(1)} %collective-permute-done), channel_id=1, source_target_pairs={{0,2},{2,4},{4,6},{6,0},{1,3},{3,5},{5,7},{7,1},{8,10},{10,12},{12... | collective-permute-start | bytes 786440 | tf_op jit(solution)/shard_map/ppermute | solution.py:185
  38.9 30.5 %collective-permute-start.7 = (bf16[4,1408,128]{2,1,0:T(8,128)(2,1)S(1)}, bf16[4,1408,128]{2,1,0:T(8,128)(2,1)}, u32[]{:S(2)}, u32[]{:S(2)}) collective-permute-start(bf16[4,1408,128]{2,1,0:T(8,128)(2,1)S(1)} %pad_maximum_fusion.1.w2n), channel_id=1, source_target_pairs={{0,1},{1,0},{2,3},{3,2},{4,5},{5,4},{6,7},{7,6},{8,9},{9,8},{10,11... | collective-permute-start | bytes 4325384 | tf_op jit(solution)/shard_map/ppermute | solution.py:189
  45.4 24.0 %collective-permute-start.3 = (bf16[4,1024,128]{2,1,0:T(8,128)(2,1)S(1)}, bf16[4,1024,128]{2,1,0:T(8,128)(2,1)S(1)}, u32[]{:S(2)}, u32[]{:S(2)}) collective-permute-start(bf16[4,1024,128]{2,1,0:T(8,128)(2,1)S(1)} %pad_maximum_fusion.2.w1n), channel_id=1, source_target_pairs={{0,1},{1,0},{2,3},{3,2},{4,5},{5,4},{6,7},{7,6},{8,9},{9,8},{10,11... | collective-permute-start | bytes 3145736 | tf_op jit(solution)/shard_map/ppermute | solution.py:189
  47.3 10.9 %all-to-all-start.1 = ((f32[8,48,128]{2,1,0:T(8,128)}), f32[8,48,128]{2,1,0:T(8,128)}, u32[]{:S(2)}, u32[]{:S(2)}) async-start(f32[8,48,128]{2,1,0:T(8,128)} %get-tuple-element.25), calls=%async_computation.1 | async-start | bytes 393216 | tf_op jit(solution)/shard_map/all_to_all | solution.py:215
  58.2 11.2 %all-to-all-start = ((bf16[8,112,128]{2,1,0:T(8,128)(2,1)}), bf16[8,112,128]{2,1,0:T(8,128)(2,1)}, u32[]{:S(2)}, u32[]{:S(2)}) async-start(bf16[8,112,128]{2,1,0:T(8,128)(2,1)} %bitcast.46), calls=%async_computation | async-start | bytes 458752 | tf_op jit(solution)/shard_map/all_to_all | solution.py:208
  75.6 17.1 %collective-permute-start.10 = (bf16[112,2048]{1,0:T(8,128)(2,1)}, bf16[112,2048]{1,0:T(8,128)(2,1)S(1)}, u32[]{:S(2)}, u32[]{:S(2)}) collective-permute-start(bf16[112,2048]{1,0:T(8,128)(2,1)} %get-tuple-element.33), channel_id=1, source_target_pairs={{0,4},{2,6},{4,0},{6,2},{1,5},{3,7},{5,1},{7,3},{8,12},{10,14},{12... | collective-permute-start | bytes 1376264 | tf_op jit(solution)/shard_map/ppermute | solution.py:185
  78.0 21.6 %collective-permute-start.9 = (bf16[112,2048]{1,0:T(8,128)(2,1)}, bf16[112,2048]{1,0:T(8,128)(2,1)S(1)}, u32[]{:S(2)}, u32[]{:S(2)}) collective-permute-start(bf16[112,2048]{1,0:T(8,128)(2,1)} %get-tuple-element.33), channel_id=1, source_target_pairs={{0,6},{2,0},{4,2},{6,4},{1,7},{3,1},{5,3},{7,5},{8,14},{10,8},{12,... | collective-permute-start | bytes 1376264 | tf_op jit(solution)/shard_map/ppermute | solution.py:185
  82.7 18.3 %collective-permute-start.8 = (bf16[112,2048]{1,0:T(8,128)(2,1)}, bf16[112,2048]{1,0:T(8,128)(2,1)S(1)}, u32[]{:S(2)}, u32[]{:S(2)}) collective-permute-start(bf16[112,2048]{1,0:T(8,128)(2,1)} %get-tuple-element.33), channel_id=1, source_target_pairs={{0,2},{2,4},{4,6},{6,0},{1,3},{3,5},{5,7},{7,1},{8,10},{10,12},{12... | collective-permute-start | bytes 1376264 | tf_op jit(solution)/shard_map/ppermute | solution.py:185
  102.3 45.6 %copy-start.2 = (bf16[4,112,2048]{2,1,0:T(8,128)(2,1)}, bf16[4,112,2048]{2,1,0:T(8,128)(2,1)S(1)}, u32[]{:S(2)}) copy-start(bf16[4,112,2048]{2,1,0:T(8,128)(2,1)S(1)} %pad_maximum_fusion.xhn) | copy-start | bytes 5505028
  102.3 80.1 %collective-permute-start.11 = (bf16[4,112,2048]{2,1,0:T(8,128)(2,1)S(1)}, bf16[4,112,2048]{2,1,0:T(8,128)(2,1)}, u32[]{:S(2)}, u32[]{:S(2)}) collective-permute-start(bf16[4,112,2048]{2,1,0:T(8,128)(2,1)S(1)} %pad_maximum_fusion.xhn), channel_id=1, source_target_pairs={{0,1},{1,0},{2,3},{3,2},{4,5},{5,4},{6,7},{7,6},{8,9},{9,8},{10,11... | collective-permute-start | bytes 5505032 | tf_op jit(solution)/shard_map/ppermute | solution.py:189
  112.8 29.7 %all-to-all-start.3 = ((f32[64,2,384]{2,1,0:T(2,128)}), f32[64,2,384]{2,1,0:T(2,128)S(1)}, u32[]{:S(2)}, u32[]{:S(2)}) async-start(f32[64,2,384]{2,1,0:T(2,128)} %broadcast_in_dim.21), calls=%async_computation.3 | async-start | bytes 393216 | tf_op jit(solution)/shard_map/all_to_all | solution.py:238
  147.8 13.1 %all-to-all-start.5 = ((bf16[8,112,256]{2,1,0:T(8,128)(2,1)}), bf16[8,112,256]{2,1,0:T(8,128)(2,1)S(1)}, u32[]{:S(2)}, u32[]{:S(2)}) async-start(bf16[8,112,256]{2,1,0:T(8,128)(2,1)} %get-tuple-element.34), calls=%async_computation.5 | async-start | bytes 917504 | tf_op jit(solution)/shard_map/all_to_all | solution.py:257
  153.7 10.7 %collective-permute-start.12 = (bf16[4,48,1024]{2,1,0:T(8,128)(2,1)}, bf16[4,48,1024]{2,1,0:T(8,128)(2,1)S(1)}, u32[]{:S(2)}, u32[]{:S(2)}) collective-permute-start(bf16[4,48,1024]{2,1,0:T(8,128)(2,1)} %get-tuple-element.37), channel_id=1, source_target_pairs={{0,1},{1,0},{2,3},{3,2},{4,5},{5,4},{6,7},{7,6},{8,9},{9,8},{10,11... | collective-permute-start | bytes 1179656 | tf_op jit(solution)/shard_map/ppermute | solution.py:189
  160.9 26.1 %all-to-all-start.4 = ((f32[8,112,128]{2,1,0:T(8,128)}), f32[8,112,128]{2,1,0:T(8,128)S(1)}, u32[]{:S(2)}, u32[]{:S(2)}) async-start(f32[8,112,128]{2,1,0:T(8,128)} %token_.1), calls=%async_computation.4 | async-start | bytes 917504 | tf_op jit(solution)/shard_map/all_to_all | solution.py:266
  167.1 11.2 %collective-permute-start.13 = (bf16[48,1024]{1,0:T(8,128)(2,1)}, bf16[48,1024]{1,0:T(8,128)(2,1)S(1)}, u32[]{:S(2)}, u32[]{:S(2)}) collective-permute-start(bf16[48,1024]{1,0:T(8,128)(2,1)} %get-tuple-element.39), channel_id=1, source_target_pairs={{0,2},{2,4},{4,6},{6,0},{1,3},{3,5},{5,7},{7,1},{8,10},{10,12},{12... | collective-permute-start | bytes 294920 | tf_op jit(solution)/shard_map/ppermute | solution.py:185
  170.9 7.4 %collective-permute-start.14 = (bf16[48,1024]{1,0:T(8,128)(2,1)}, bf16[48,1024]{1,0:T(8,128)(2,1)S(1)}, u32[]{:S(2)}, u32[]{:S(2)}) collective-permute-start(bf16[48,1024]{1,0:T(8,128)(2,1)} %get-tuple-element.40), channel_id=1, source_target_pairs={{0,6},{2,0},{4,2},{6,4},{1,7},{3,1},{5,3},{7,5},{8,14},{10,8},{12,... | collective-permute-start | bytes 294920 | tf_op jit(solution)/shard_map/ppermute | solution.py:185
  174.2 8.2 %collective-permute-start.15 = (bf16[48,1024]{1,0:T(8,128)(2,1)}, bf16[48,1024]{1,0:T(8,128)(2,1)S(1)}, u32[]{:S(2)}, u32[]{:S(2)}) collective-permute-start(bf16[48,1024]{1,0:T(8,128)(2,1)} %get-tuple-element.41), channel_id=1, source_target_pairs={{0,4},{2,6},{4,0},{6,2},{1,5},{3,7},{5,1},{7,3},{8,12},{10,14},{12... | collective-permute-start | bytes 294920 | tf_op jit(solution)/shard_map/ppermute | solution.py:185
  187.1 29.4 %all-to-all-start.6 = ((bf16[64,16,384]{2,1,0:T(8,128)(2,1)}), bf16[64,16,384]{2,1,0:T(8,128)(2,1)S(1)}, u32[]{:S(2)}, u32[]{:S(2)}) async-start(bf16[64,16,384]{2,1,0:T(8,128)(2,1)} %weight.1), calls=%async_computation.6 | async-start | bytes 1572864 | tf_op jit(solution)/shard_map/all_to_all | solution.py:265
  (10 other events, 84.8 us)

commit v2 on v1

--- a/solution.py
+++ b/solution.py
@@ -14,6 +14,7 @@
 D = 1024
 OWN = 112
 HEAD = 48
+WIDE = 64
 COLS = 8 * HEAD
 BF = jnp.bfloat16
 F32 = jnp.float32
@@ -46,12 +47,21 @@
     )(*args)
 
 
-def prep_body(head, second, targets, kinds, packed, tgt):
-    packed[:D, :] = second[...]
+def prep_body(kinds, tokens, targets, out):
+    real = V * PP // 8
+    row = lax.broadcasted_iota(jnp.int32, (HEAD, 128 - OWN), 0)
+    kind = jnp.zeros(row.shape, F32)
+    for v in range(V // 8):
+        kind = jnp.where(row // PP == v, kinds[v].astype(F32), kind)
     for i in range(8):
-        packed[D + HEAD * i : D + HEAD * (i + 1), :] = head[:, 128 * i : 128 * (i + 1)]
-        tgt[i, :, :OWN] = targets[:, OWN * i : OWN * (i + 1)]
-        tgt[i, :, OWN:] = jnp.broadcast_to(kinds[...], (HEAD, 128 - OWN))
+        out[i, :OWN, :] = tokens[OWN * i : OWN * (i + 1), :]
+        rest = jnp.concatenate([targets[:, OWN * i : OWN * (i + 1)], kind[:real]], axis=1)
+        rest = jnp.concatenate([rest, jnp.zeros((HEAD - real, 128), F32)], axis=0)
+        for piece in range(3):
+            at = OWN + HEAD * piece
+            part = rest.astype(BF)
+            out[i, at : at + HEAD, :] = part
+            rest = rest - part.astype(F32)
 
 
 def gelu_parts(z):
@@ -66,34 +76,31 @@
 
 
 def forward_body(
-    idx, tok, w1n, w1f, w2n, w2f, tgt, land, weights,
-    xh, slope1, slope2, hidden2, me, sums, head, pre,
+    idx, given, w1n, w1f, w2n, w2f, heads, land, weights,
+    hidden1, slope1, slope2, hidden2, me, sums, head, own, pre,
 ):
     for j in range(8):
-        xh[:, 128 * j : 128 * (j + 1)] = tok[j]
-    for a, ref in enumerate((w2n, w2f)):
-        for s in range(4):
-            rows = pl.ds(pl.multiple_of(idx[4 * a + s] * HEAD, HEAD), HEAD)
-            for i in range(8):
-                head[rows, 128 * i : 128 * (i + 1)] = ref[s, D + HEAD * i : D + HEAD * (i + 1), :]
+        own[:, 128 * j : 128 * (j + 1)] = given[j, :OWN, :]
+        head[HEAD * j : HEAD * (j + 1), :] = heads[WIDE * j : WIDE * j + HEAD, :]
 
     def layer(value, near, far):
         for ref, s, at in pairs(near, far):
-            both = jnp.concatenate([ref[s, :D, :], ref[s + 1, :D, :]], axis=1)
+            both = jnp.concatenate([ref[s], ref[s + 1]], axis=1)
             z = dot(value, both, 1, 0)
             pre[:, lanes(idx[at])] = z[:, :128]
             pre[:, lanes(idx[at + 1])] = z[:, 128:]
 
-    layer(xh[:, :D], w1n, w1f)
+    layer(own[...], w1n, w1f)
     hidden, slope = gelu_parts(pre[...])
-    xh[:, D:] = hidden.astype(BF)
+    hidden1[...] = hidden.astype(BF)
     slope1[...] = slope
-    layer(xh[:, D:], w2n, w2f)
+    layer(hidden1[...], w2n, w2f)
     hidden, slope = gelu_parts(pre[...])
     hidden2[...] = hidden.astype(BF)
     slope2[...] = slope
     predicted = dot(hidden2[...], head[...], 1, 1)
-    flipped = tgt[...].reshape(COLS, 128).T
+    pieces = [given[:, OWN + HEAD * p : OWN + HEAD * (p + 1), :].astype(F32) for p in range(3)]
+    flipped = (pieces[0] + (pieces[1] + pieces[2])).reshape(COLS, 128).T
     kind = flipped[OWN : OWN + 1, :]
     column = lax.broadcasted_iota(jnp.int32, (8, COLS), 1)
     picks = (column % PP == lax.broadcasted_iota(jnp.int32, (8, COLS), 0)).astype(BF)
@@ -148,7 +155,7 @@
     g2[...] = (dot(grad_pred, head[...], 1, 0) * slope2[...]).astype(BF)
     back = jnp.zeros((OWN, D), F32)
     for ref, s, at in pairs(w2n, w2f):
-        both = jnp.concatenate([ref[s, :D, :], ref[s + 1, :D, :]], axis=1)
+        both = jnp.concatenate([ref[s], ref[s + 1]], axis=1)
         left = jnp.concatenate([g2[:, lanes(idx[at])], g2[:, lanes(idx[at + 1])]], axis=1)
         back += dot(left, both, 1, 1)
     grad1[...] = (back * slope1[...]).astype(BF)
@@ -158,23 +165,19 @@
 
 
 def token_body(idx, grad1, w1n, w1f, out):
-    grad = jnp.zeros((OWN, D), F32)
+    rows = lanes(idx[10])
+    grad = jnp.zeros((8 * OWN, 128), F32)
     for ref, s, at in pairs(w1n, w1f):
-        both = jnp.concatenate([ref[s], ref[s + 1]], axis=1)
+        both = jnp.concatenate([ref[s, rows, :], ref[s + 1, rows, :]], axis=1)
         left = jnp.concatenate([grad1[:, lanes(idx[at])], grad1[:, lanes(idx[at + 1])]], axis=1)
         grad += dot(left, both, 1, 1)
-    for j in range(8):
-        out[j] = grad[:, 128 * j : 128 * (j + 1)]
-
-
-def weight_body(idx, xhn, xhf, joined, own, a, b, c, out, order):
-    for at in range(8):
-        order[OWN * at : OWN * (at + 1), :] = joined[idx[at]]
-    half = 4 * OWN
-    near, far = xhn[...].reshape(half, 2 * D), xhf[...].reshape(half, 2 * D)
-    for to, at in ((0, D), (128, 0)):
-        grad = dot(order[:half, to : to + 128], near[:, at : at + D], 0, 0)
-        grad += dot(order[half:, to : to + 128], far[:, at : at + D], 0, 0)
+    out[...] = grad
+
+
+def weight_body(hidden1, tokens, joined, own, a, b, c, out):
+    grads = joined[...].reshape(8 * OWN, 256)
+    for to, value in ((0, hidden1), (128, tokens)):
+        grad = dot(grads[:, to : to + 128], value[...], 0, 0)
         out[:, :, to : to + 128] = grad.T.astype(BF).reshape(64, 16, 128)
     part = own[...].astype(F32) + a[...].astype(F32) + b[...].astype(F32) + c[...].astype(F32)
     part = jnp.concatenate([part, jnp.zeros((128 - HEAD, D), F32)], axis=0)
@@ -195,24 +198,25 @@
     x, core = lax.axis_index("x"), lax.axis_index("core")
     mine = lax.axis_index(TENSOR)
     places = [2 * ((x + off) % 4) + c for c in (core, 1 - core) for off in OFFS]
-    idx = jnp.stack([*places, core, x]).astype(jnp.int32)
-
-    padded_head = jnp.pad(head_weight, ((0, HEAD - 44), (0, 0)))
-    padded_targets = jnp.pad(targets, ((0, HEAD - 44), (0, 0)))
-    kinds = jnp.pad(jnp.repeat(variable_kind, PP), (0, HEAD - 44)).astype(F32)[:, None]
-    packed, tgt = call(
-        prep_body, "prep", [((D + COLS, 128), BF), ((8, HEAD, 128), F32)],
-        [padded_head, second_weight, padded_targets, kinds],
-    )
-
-    own_tokens = lax.all_to_all(tokens.reshape(8, OWN, 128), TENSOR, 0, 0, tiled=True)
+    idx = jnp.stack([*places, core, x, mine]).astype(jnp.int32)
+
+    full_tokens = lax.all_gather(tokens, TENSOR, axis=1, tiled=True)
+    wide = jnp.pad(head_weight, ((0, WIDE - V * PP // 8), (0, 0)))
+    heads = lax.all_gather(wide, TENSOR, axis=0, tiled=True)
+    (given,) = call(
+        prep_body, "prep", [((8, OWN + 3 * HEAD, 128), BF)], [variable_kind, tokens, targets],
+        smem=(0,),
+    )
+    given = lax.all_to_all(given, TENSOR, 0, 0, tiled=True)
+
     w1_m1, w1_p1 = shift(first_weight, 1), shift(first_weight, 3)
-    w2_m1, w2_p1 = shift(packed, 1), shift(packed, 3)
+    w2_m1, w2_p1 = shift(second_weight, 1), shift(second_weight, 3)
+    w1_m1, w2_p1, given = lax.optimization_barrier((w1_m1, w2_p1, given))
     w1_p2, w2_p2 = shift(w1_m1, 1), shift(w2_p1, 3)
     w1n = jnp.stack([first_weight, w1_m1, w1_p1, w1_p2])
-    w2n = jnp.stack([packed, w2_m1, w2_p1, w2_p2])
-    w1f, w2f = flip(w1n), flip(w2n)
-    tgt = lax.all_to_all(tgt, TENSOR, 0, 0, tiled=True)
+    w2n = jnp.stack([second_weight, w2_m1, w2_p1, w2_p2])
+    w1f = flip(w1n)
+    w2f = flip(w2n)
 
     land = lax.dynamic_slice(land_mask, (0, mine * OWN), (PP, OWN))
     land = jnp.pad(land.astype(BF), ((0, 8 - PP), (0, 128 - OWN)))
@@ -224,21 +228,21 @@
     weights = jnp.cos(math.pi / 2.0 * (lat_row.astype(F32) + 0.5) / nlat)
     weights = jnp.where(col % HEAD < 44, weights, 0.0)[None, :]
 
-    xh, slope1, slope2, hidden2, me, sums, head = call(
+    hidden1, slope1, slope2, hidden2, me, sums, head = call(
         forward_body, "forward",
-        [((OWN, 2 * D), BF), ((OWN, D), F32), ((OWN, D), F32), ((OWN, D), BF), ((OWN, COLS), F32),
+        [((OWN, D), BF), ((OWN, D), F32), ((OWN, D), F32), ((OWN, D), BF), ((OWN, COLS), F32),
          ((2, COLS), F32), ((COLS, D), BF)],
-        [idx, own_tokens, w1n, w1f, w2n, w2f, tgt, land, weights],
-        smem=(0,), scratch=[pltpu.VMEM((OWN, D), F32)], flops=10**9,
-    )
+        [idx, given, w1n, w1f, w2n, w2f, heads, land, weights],
+        smem=(0,), scratch=[pltpu.VMEM((OWN, D), BF), pltpu.VMEM((OWN, D), F32)], flops=10**9,
+    )
+    full_hidden1 = lax.all_gather(hidden1, TENSOR, axis=0, tiled=True)
 
     sums = jnp.sum(
         lax.all_to_all(jnp.broadcast_to(sums, (8, 2, COLS)), TENSOR, 0, 0, tiled=True), axis=0
     )
+    sums, me, hidden2 = lax.optimization_barrier((sums, me, hidden2))
     sums = lax.all_to_all(jnp.broadcast_to(sums, (64, 2, COLS)), SPACE, 0, 0, tiled=True)
 
-    xhn = jnp.stack([xh, shift(xh, 1), shift(xh, 3), shift(xh, 2)])
-    xhf = flip(xhn)
     keep, send = call(
         head_body, "head_part", [((4, HEAD, D), BF)] * 2, [idx, me, hidden2],
         smem=(0,), scratch=[pltpu.VMEM((COLS, D), F32)], flops=10**8,
@@ -247,6 +251,7 @@
         pair_body, "pair", [((HEAD, D), BF)] * 4, [idx, keep, flip(send)], smem=(0,)
     )
     head_parts = [own, shift(up, 1), shift(down, 3), shift(across, 2)]
+    sums, head_parts = lax.optimization_barrier((sums, head_parts))
 
     joined, grad1, coefs, loss = call(
         backward_body, "backward",
@@ -255,15 +260,16 @@
         smem=(0, 1), scratch=[pltpu.VMEM((OWN, D), BF)], flops=5 * 10**8,
     )
     joined = lax.all_to_all(joined, TENSOR, 0, 0, tiled=True)
+    full_grad1 = lax.all_gather(grad1, TENSOR, axis=0, tiled=True)
+    (out,) = call(
+        weight_body, "weight", [((64, 16, 384), BF)],
+        [full_hidden1, full_tokens, joined, *head_parts], flops=5 * 10**8,
+    )
+    out = lax.all_to_all(out, SPACE, 0, 0, tiled=True)
     (token_grad,) = call(
-        token_body, "token", [((8, OWN, 128), F32)], [idx, grad1, w1n, w1f], smem=(0,), flops=3 * 10**8
-    )
-    (out,) = call(
-        weight_body, "weight", [((64, 16, 384), BF)], [idx, xhn, xhf, joined, *head_parts],
-        smem=(0,), scratch=[pltpu.VMEM((8 * OWN, 256), BF)], flops=5 * 10**8,
-    )
-    out = lax.all_to_all(out, SPACE, 0, 0, tiled=True)
-    token_grad = lax.all_to_all(token_grad, TENSOR, 0, 0, tiled=True).reshape(8 * OWN, 128)
+        token_body, "token", [((8 * OWN, 128), F32)], [idx, full_grad1, w1n, w1f],
+        smem=(0,), flops=3 * 10**8,
+    )
     out = jnp.sum(out.astype(F32), axis=0)
     local = lax.dynamic_slice(coefs, (0, mine * HEAD), (1, 44))
     head_grad = (out[:, 256:300] * local).T

time: 220 us -> 180 us (0.82)
  waiting for transfers between devices: 82.9 us -> 41.6 us
  starting transfers between devices: 86.2 us -> 66 us
  blocking collectives: 7.81 us -> 23.2 us
  between operations: 1.72 us -> 14.8 us
  local copies, waits for them, and re-layouts: 11.9 us -> 7.29 us
  other arithmetic: 4.74 us -> 2.43 us
    ppermute x12 -> x9, waiting for transfers between devices: 34 us -> 19.3 us  [shift(): return lax.ppermute(v, 'x', [(i, (i + by) % 4) for i in range(4)])]
    ppermute x12 -> x9, starting transfers between devices: 41.3 us -> 26.9 us  [shift(): return lax.ppermute(v, 'x', [(i, (i + by) % 4) for i in range(4)])]
    all_to_all x0 -> x1, blocking collectives: none -> 13.8 us  [per_device(): joined = lax.all_to_all(joined, TENSOR, 0, 0, tiled=True)]
    all_to_all x4 -> x1, waiting for transfers between devices: 13.1 us -> 0.01 us  [per_device(): given = lax.all_to_all(given, TENSOR, 0, 0, tiled=True)]
    all_to_all x4 -> x1, starting transfers between devices: 15 us -> 4.3 us  [per_device(): given = lax.all_to_all(given, TENSOR, 0, 0, tiled=True)]
    all_to_all x1, waiting for transfers between devices: 12.4 us -> 2.05 us  [per_device(): lax.all_to_all(jnp.broadcast_to(sums, (64, 2, COLS)), SPACE, 0, 0, tiled=...]
    all_to_all x1, starting transfers between devices: 5.18 us -> 12.7 us  [per_device(): out = lax.all_to_all(out, SPACE, 0, 0, tiled=True)]
    all_to_all x1, waiting for transfers between devices: 23.4 us -> 19.3 us  [per_device(): out = lax.all_to_all(out, SPACE, 0, 0, tiled=True)]
  transfers between devices with their start and end apart: 22 -> 19, of which waited for: 12 -> 8; matrix products, arithmetic and copies ran while one was open for 2% -> 3% of each run, Pallas kernels for 7% -> 13%
where the time goes in v2:
time: 180 us; the launch traced here: 179 us
  starting transfers between devices  66 us (37%)
  waiting for transfers between devices  41.6 us (23%)
  Pallas kernels  23.6 us (13%)
  blocking collectives  23.2 us (13%)
  between operations  14.8 us (8%)
  local copies, waits for them, and re-layouts  7.29 us (4%)
  other arithmetic  2.43 us (1%)
    ppermute x9, starting transfers between devices, shift(): return lax.ppermute(v, 'x', [(i, (i + by) % 4) for i in range(4)])  26.9 us
    pallas_call x7, Pallas kernels, call(): pl.pallas_call(body, name=name, out_shape=tuple((jax.ShapeDtypeStruct(s,...  23.6 us
    all_to_all x1, waiting for transfers between devices, per_device(): out = lax.all_to_all(out, SPACE, 0, 0, tiled=True)  19.3 us
    ppermute x9, waiting for transfers between devices, shift(): return lax.ppermute(v, 'x', [(i, (i + by) % 4) for i in range(4)])  19.3 us
    all_to_all x1, starting transfers between devices, per_device(): lax.all_to_all(jnp.broadcast_to(sums, (64, 2, COLS)), SPACE, 0, 0, tiled=...  16.1 us
    all_to_all x1, blocking collectives, per_device(): joined = lax.all_to_all(joined, TENSOR, 0, 0, tiled=True)  13.8 us
    all_to_all x1, starting transfers between devices, per_device(): out = lax.all_to_all(out, SPACE, 0, 0, tiled=True)  12.7 us
    all_to_all x1, blocking collectives, per_device(): lax.all_to_all(jnp.broadcast_to(sums, (8, 2, COLS)), TENSOR, 0, 0, tiled=...  9.35 us
  transfers between devices with their start and end apart: 19, of which 8 were waited for; matrix products, arithmetic and copies ran while one was open for 3% of the time, Pallas kernels for 13%

profile of v2, /device:TPU:8, one launch (start us, length us, event | category | flops | bytes accessed | tf_op | source)
XLA Modules:
  0.0 178.9 jit_solution(8700286670424240785)
XLA Ops:
  11.6 4.3 %all-to-all-start = ((bf16[8,256,128]{2,1,0:T(8,128)(2,1)}), bf16[8,256,128]{2,1,0:T(8,128)(2,1)S(1)}, u32[]{:S(2)}, u32[]{:S(2)}) async-start(bf16[8,256,128]{2,1,0:T(8,128)(2,1)} %prep.1), calls=%async_computation | async-start | bytes 1048576 | tf_op jit(solution)/shard_map/all_to_all | solution.py:210
  16.0 3.9 %collective-permute-start = (bf16[1024,128]{1,0:T(8,128)(2,1)S(1)}, bf16[1024,128]{1,0:T(8,128)(2,1)S(1)}, u32[]{:S(2)}, u32[]{:S(2)}) collective-permute-start(bf16[1024,128]{1,0:T(8,128)(2,1)S(1)} %copy-done.7), channel_id=1, source_target_pairs={{0,2},{2,4},{4,6},{6,0},{1,3},{3,5},{5,7},{7,1},{8,10},{10,12},{12... | collective-permute-start | bytes 786440 | tf_op jit(solution)/shard_map/ppermute | solution.py:188
  19.9 3.2 %collective-permute-start.1 = (bf16[1024,128]{1,0:T(8,128)(2,1)S(1)}, bf16[1024,128]{1,0:T(8,128)(2,1)S(1)}, u32[]{:S(2)}, u32[]{:S(2)}) collective-permute-start(bf16[1024,128]{1,0:T(8,128)(2,1)S(1)} %copy-done.6), channel_id=1, source_target_pairs={{0,6},{2,0},{4,2},{6,4},{1,7},{3,1},{5,3},{7,5},{8,14},{10,8},{12,... | collective-permute-start | bytes 786440 | tf_op jit(solution)/shard_map/ppermute | solution.py:188
  23.0 2.7 %collective-permute-start.5 = (bf16[1024,128]{1,0:T(8,128)(2,1)S(1)}, bf16[1024,128]{1,0:T(8,128)(2,1)S(1)}, u32[]{:S(2)}, u32[]{:S(2)}) collective-permute-start(bf16[1024,128]{1,0:T(8,128)(2,1)S(1)} %copy-done.6), channel_id=1, source_target_pairs={{0,2},{2,4},{4,6},{6,0},{1,3},{3,5},{5,7},{7,1},{8,10},{10,12},{12... | collective-permute-start | bytes 786440 | tf_op jit(solution)/shard_map/ppermute | solution.py:188
  25.7 6.2 %collective-permute-done = bf16[1024,128]{1,0:T(8,128)(2,1)S(1)} collective-permute-done((bf16[1024,128]{1,0:T(8,128)(2,1)S(1)}, bf16[1024,128]{1,0:T(8,128)(2,1)S(1)}, u32[]{:S(2)}, u32[]{:S(2)}) %collective-permute-start) | collective-permute-done | bytes 262176 | tf_op jit(solution)/shard_map/ppermute | solution.py:188
  31.9 3.1 %collective-permute-start.6 = (bf16[1024,128]{1,0:T(8,128)(2,1)S(1)}, bf16[1024,128]{1,0:T(8,128)(2,1)S(1)}, u32[]{:S(2)}, u32[]{:S(2)}) collective-permute-start(bf16[1024,128]{1,0:T(8,128)(2,1)S(1)} %collective-permute-done.1), channel_id=1, source_target_pairs={{0,6},{2,0},{4,2},{6,4},{1,7},{3,1},{5,3},{7,5},{8,14},{10,8},{12,... | collective-permute-start | bytes 786440 | tf_op jit(solution)/shard_map/ppermute | solution.py:188
  35.0 2.4 %collective-permute-start.2 = (bf16[1024,128]{1,0:T(8,128)(2,1)S(1)}, bf16[1024,128]{1,0:T(8,128)(2,1)S(1)}, u32[]{:S(2)}, u32[]{:S(2)}) collective-permute-start(bf16[1024,128]{1,0:T(8,128)(2,1)S(1)} %copy-done.7), channel_id=1, source_target_pairs={{0,6},{2,0},{4,2},{6,4},{1,7},{3,1},{5,3},{7,5},{8,14},{10,8},{12,... | collective-permute-start | bytes 786440 | tf_op jit(solution)/shard_map/ppermute | solution.py:188
  37.4 3.4 %collective-permute-start.3 = (bf16[1024,128]{1,0:T(8,128)(2,1)S(1)}, bf16[1024,128]{1,0:T(8,128)(2,1)S(1)}, u32[]{:S(2)}, u32[]{:S(2)}) collective-permute-start(bf16[1024,128]{1,0:T(8,128)(2,1)S(1)} %collective-permute-done), channel_id=1, source_target_pairs={{0,2},{2,4},{4,6},{6,0},{1,3},{3,5},{5,7},{7,1},{8,10},{10,12},{12... | collective-permute-start | bytes 786440 | tf_op jit(solution)/shard_map/ppermute | solution.py:188
  40.9 4.0 %collective-permute-done.6 = bf16[1024,128]{1,0:T(8,128)(2,1)S(1)} collective-permute-done((bf16[1024,128]{1,0:T(8,128)(2,1)S(1)}, bf16[1024,128]{1,0:T(8,128)(2,1)S(1)}, u32[]{:S(2)}, u32[]{:S(2)}) %collective-permute-start.6) | collective-permute-done | bytes 262176 | tf_op jit(solution)/shard_map/ppermute | solution.py:188
  46.9 2.8 %collective-permute-done.2 = bf16[1024,128]{1,0:T(8,128)(2,1)S(1)} collective-permute-done((bf16[1024,128]{1,0:T(8,128)(2,1)S(1)}, bf16[1024,128]{1,0:T(8,128)(2,1)S(1)}, u32[]{:S(2)}, u32[]{:S(2)}) %collective-permute-start.2) | collective-permute-done | bytes 262176 | tf_op jit(solution)/shard_map/ppermute | solution.py:188
  55.5 5.2 %forward.1 = (bf16[112,1024]{1,0:T(8,128)(2,1)}, f32[112,1024]{1,0:T(8,128)}, f32[112,1024]{1,0:T(8,128)}, bf16[112,1024]{1,0:T(8,128)(2,1)}, f32[112,384]{1,0:T...) custom-call(s32[11]{0:T(128)} %stack.77.idx, bf16[8,256,128]{2,1,0:T(8,128)(2,1)} %copy-done.3, ...), custom_call_target="tpu_custom_call" | custom-call | flops 1000000000 | bytes 4194304 | tf_op jit(solution)/shard_map/forward/pallas_call | solution.py:38
  61.5 9.3 %all_to_all.25 = f32[8,2,384]{2,1,0:T(2,128)S(1)} all-to-all(f32[8,2,384]{2,1,0:T(2,128)S(1)} %broadcast_in_dim.12), channel_id=1, replica_groups=mesh['z'=8,'y'=8,'x'=4,'core'=2] {'x','core'}, dimensions={0} | all-to-all | bytes 49152 | tf_op jit(solution)/shard_map/all_to_all | solution.py:241
  70.8 2.3 %head_part.1 = (bf16[4,48,1024]{2,1,0:T(8,128)(2,1)}, bf16[4,48,1024]{2,1,0:T(8,128)(2,1)}) custom-call(s32[11]{0:T(128)} %stack.77.idx, f32[112,384]{1,0:T(8,128)} %get-tuple-element.40.me, bf16[112,1024]{1,0:T(8,128)(2,1)} %get-tuple-element.41.hidden2), custom_call_target="tpu_custom_call" | custom-call | flops 100000000 | bytes 4194304 | tf_op jit(solution)/shard_map/head_part/pallas_call | solution.py:38
  75.8 16.1 %all-to-all-start.2 = ((f32[64,2,384]{2,1,0:T(2,128)}), f32[64,2,384]{2,1,0:T(2,128)S(1)}, u32[]{:S(2)}, u32[]{:S(2)}) async-start(f32[64,2,384]{2,1,0:T(2,128)} %broadcast_in_dim.13), calls=%async_computation.2 | async-start | bytes 393216 | tf_op jit(solution)/shard_map/all_to_all | solution.py:244
  94.7 3.0 %collective-permute-start.10 = (bf16[48,1024]{1,0:T(8,128)(2,1)}, bf16[48,1024]{1,0:T(8,128)(2,1)S(1)}, u32[]{:S(2)}, u32[]{:S(2)}) collective-permute-start(bf16[48,1024]{1,0:T(8,128)(2,1)} %get-tuple-element.46), channel_id=1, source_target_pairs={{0,6},{2,0},{4,2},{6,4},{1,7},{3,1},{5,3},{7,5},{8,14},{10,8},{12,... | collective-permute-start | bytes 294920 | tf_op jit(solution)/shard_map/ppermute | solution.py:188
  97.7 3.4 %collective-permute-start.11 = (bf16[48,1024]{1,0:T(8,128)(2,1)}, bf16[48,1024]{1,0:T(8,128)(2,1)S(1)}, u32[]{:S(2)}, u32[]{:S(2)}) collective-permute-start(bf16[48,1024]{1,0:T(8,128)(2,1)} %get-tuple-element.47), channel_id=1, source_target_pairs={{0,4},{2,6},{4,0},{6,2},{1,5},{3,7},{5,1},{7,3},{8,12},{10,14},{12... | collective-permute-start | bytes 294920 | tf_op jit(solution)/shard_map/ppermute | solution.py:188
  105.7 3.3 %collective-permute-done.11.c = bf16[48,1024]{1,0:T(8,128)(2,1)S(1)} collective-permute-done((bf16[48,1024]{1,0:T(8,128)(2,1)}, bf16[48,1024]{1,0:T(8,128)(2,1)S(1)}, u32[]{:S(2)}, u32[]{:S(2)}) %collective-permute-start.11) | collective-permute-done | bytes 98336 | tf_op jit(solution)/shard_map/ppermute | solution.py:188
  109.0 3.0 %collective-permute-done.9.a = bf16[48,1024]{1,0:T(8,128)(2,1)S(1)} collective-permute-done((bf16[48,1024]{1,0:T(8,128)(2,1)}, bf16[48,1024]{1,0:T(8,128)(2,1)S(1)}, u32[]{:S(2)}, u32[]{:S(2)}) %collective-permute-start.9) | collective-permute-done | bytes 98336 | tf_op jit(solution)/shard_map/ppermute | solution.py:188
  112.0 4.5 %backward.1 = (bf16[8,112,256]{2,1,0:T(8,128)(2,1)}, bf16[112,1024]{1,0:T(8,128)(2,1)}, f32[1,384]{1,0:T(1,128)}, f32[1,1]{1,0:T(1,128)}) custom-call(s32[11]{0:T(128)} %stack.77.idx, f32[1]{0:T(128)} %bitcast.25.scale, f32[64,2,384]{2,1,0:T(2,128)} %copy-done.4, f32[112,384]{1,0:T(8,128)} %get-tuple-element.40.me, f32[112,1024]{1,0:T(8,128)} %get-tuple-element.49.slope1, ...), custom_call_target="tpu_custom_call" | custom-call | flops 500000000 | bytes 4194304 | tf_op jit(solution)/shard_map/backward/pallas_call | solution.py:38
  116.6 13.8 %all_to_all.26.joined = bf16[8,112,256]{2,1,0:T(8,128)(2,1)} all-to-all(bf16[8,112,256]{2,1,0:T(8,128)(2,1)} %get-tuple-element.55), channel_id=1, replica_groups=mesh['z'=8,'y'=8,'x'=4,'core'=2] {'x','core'}, dimensions={0} | all-to-all | bytes 917504 | tf_op jit(solution)/shard_map/all_to_all | solution.py:262
  130.4 4.1 %weight.1 = bf16[64,16,384]{2,1,0:T(8,128)(2,1)} custom-call(bf16[896,1024]{1,0:T(8,128)(2,1)} %all-gather.9.cloned.1.call-done.hidden1, bf16[896,1024]{1,0:T(8,128)(2,1)} %all-gather.11.cloned.1.call-done.tokens, bf16[8,112,256]{2,1,0:T(8,128)(2,1)} %all_to_all.26.joined, bf16[48,1024]{1,0:T(8,128)(2,1)} %get-tuple-element.56.own, ...), custom_call_target="tpu_custom_call" | custom-call | flops 500000000 | bytes 4194304 | tf_op jit(solution)/shard_map/weight/pallas_call | solution.py:38
  134.5 12.7 %all-to-all-start.4 = ((bf16[64,16,384]{2,1,0:T(8,128)(2,1)}), bf16[64,16,384]{2,1,0:T(8,128)(2,1)S(1)}, u32[]{:S(2)}, u32[]{:S(2)}) async-start(bf16[64,16,384]{2,1,0:T(8,128)(2,1)} %weight.1), calls=%async_computation.4 | async-start | bytes 1572864 | tf_op jit(solution)/shard_map/all_to_all | solution.py:268
  148.1 3.5 %token_.1 = f32[896,128]{1,0:T(8,128)} custom-call(s32[11]{0:T(128)} %stack.77.idx, bf16[896,1024]{1,0:T(8,128)(2,1)} %all-gather.7.cloned.1.call-done.grad1, bf16[4,1024,128]{2,1,0:T(8,128)(2,1)} %copy-done, bf16[4,1024,128]{2,1,0:T(8,128)(2,1)} %copy-done.2), custom_call_target="tpu_custom_call" | custom-call | flops 300000000 | bytes 4194304 | tf_op jit(solution)/shard_map/token/pallas_call | solution.py:38
  151.6 19.3 %all-to-all-done.4 = bf16[64,16,384]{2,1,0:T(8,128)(2,1)S(1)} async-done(((bf16[64,16,384]{2,1,0:T(8,128)(2,1)}), bf16[64,16,384]{2,1,0:T(8,128)(2,1)S(1)}, u32[]{:S(2)}, u32[]{:S(2)}) %all-to-all-start.4) | async-done | bytes 786464 | tf_op jit(solution)/shard_map/all_to_all | solution.py:268
  (63 shorter events, 24.4 us)
Async XLA Ops:
  7.2 8.8 %copy-start.7 = (bf16[1024,128]{1,0:T(8,128)(2,1)S(1)}, bf16[1024,128]{1,0:T(8,128)(2,1)}, u32[]{:S(2)}) copy-start(bf16[1024,128]{1,0:T(8,128)(2,1)} %param.9) | copy-start | bytes 786436
  7.2 12.7 %copy-start.6 = (bf16[1024,128]{1,0:T(8,128)(2,1)S(1)}, bf16[1024,128]{1,0:T(8,128)(2,1)}, u32[]{:S(2)}) copy-start(bf16[1024,128]{1,0:T(8,128)(2,1)} %param.10) | copy-start | bytes 786436
  7.2 47.4 %all-gather.5.cloned.1.call-start = ((), (), s32[]{:S(2)}) async-start(), calls=%async_computation.5 | async-start | bytes 1179648 | tf_op jit(solution)/shard_map/all_gather | solution.py:205
  8.9 121.6 %all-gather.11.cloned.1.call-start = ((), (), s32[]{:S(2)}) async-start(), calls=%async_computation.8 | async-start | bytes 2064384 | tf_op jit(solution)/shard_map/all_gather | solution.py:203
  11.6 20.3 %all-to-all-start = ((bf16[8,256,128]{2,1,0:T(8,128)(2,1)}), bf16[8,256,128]{2,1,0:T(8,128)(2,1)S(1)}, u32[]{:S(2)}, u32[]{:S(2)}) async-start(bf16[8,256,128]{2,1,0:T(8,128)(2,1)} %prep.1), calls=%async_computation | async-start | bytes 1048576 | tf_op jit(solution)/shard_map/all_to_all | solution.py:210
  15.9 114.5 %all-gather.9.cloned.1.call-start = ((), (), s32[]{:S(2)}) async-start(), calls=%async_computation.7 | async-start | bytes 2064384 | tf_op jit(solution)/shard_map/all_gather | solution.py:238
  16.0 15.9 %collective-permute-start = (bf16[1024,128]{1,0:T(8,128)(2,1)S(1)}, bf16[1024,128]{1,0:T(8,128)(2,1)S(1)}, u32[]{:S(2)}, u32[]{:S(2)}) collective-permute-start(bf16[1024,128]{1,0:T(8,128)(2,1)S(1)} %copy-done.7), channel_id=1, source_target_pairs={{0,2},{2,4},{4,6},{6,0},{1,3},{3,5},{5,7},{7,1},{8,10},{10,12},{12... | collective-permute-start | bytes 786440 | tf_op jit(solution)/shard_map/ppermute | solution.py:188
  19.9 12.0 %collective-permute-start.1 = (bf16[1024,128]{1,0:T(8,128)(2,1)S(1)}, bf16[1024,128]{1,0:T(8,128)(2,1)S(1)}, u32[]{:S(2)}, u32[]{:S(2)}) collective-permute-start(bf16[1024,128]{1,0:T(8,128)(2,1)S(1)} %copy-done.6), channel_id=1, source_target_pairs={{0,6},{2,0},{4,2},{6,4},{1,7},{3,1},{5,3},{7,5},{8,14},{10,8},{12,... | collective-permute-start | bytes 786440 | tf_op jit(solution)/shard_map/ppermute | solution.py:188
  23.0 17.8 %collective-permute-start.5 = (bf16[1024,128]{1,0:T(8,128)(2,1)S(1)}, bf16[1024,128]{1,0:T(8,128)(2,1)S(1)}, u32[]{:S(2)}, u32[]{:S(2)}) collective-permute-start(bf16[1024,128]{1,0:T(8,128)(2,1)S(1)} %copy-done.6), channel_id=1, source_target_pairs={{0,2},{2,4},{4,6},{6,0},{1,3},{3,5},{5,7},{7,1},{8,10},{10,12},{12... | collective-permute-start | bytes 786440 | tf_op jit(solution)/shard_map/ppermute | solution.py:188
  31.9 12.9 %copy-start.3 = (bf16[8,256,128]{2,1,0:T(8,128)(2,1)}, bf16[8,256,128]{2,1,0:T(8,128)(2,1)S(1)}, u32[]{:S(2)}) copy-start(bf16[8,256,128]{2,1,0:T(8,128)(2,1)S(1)} %all-to-all-done.given) | copy-start | bytes 1572868
  31.9 12.9 %collective-permute-start.6 = (bf16[1024,128]{1,0:T(8,128)(2,1)S(1)}, bf16[1024,128]{1,0:T(8,128)(2,1)S(1)}, u32[]{:S(2)}, u32[]{:S(2)}) collective-permute-start(bf16[1024,128]{1,0:T(8,128)(2,1)S(1)} %collective-permute-done.1), channel_id=1, source_target_pairs={{0,6},{2,0},{4,2},{6,4},{1,7},{3,1},{5,3},{7,5},{8,14},{10,8},{12,... | collective-permute-start | bytes 786440 | tf_op jit(solution)/shard_map/ppermute | solution.py:188
  35.0 14.8 %collective-permute-start.2 = (bf16[1024,128]{1,0:T(8,128)(2,1)S(1)}, bf16[1024,128]{1,0:T(8,128)(2,1)S(1)}, u32[]{:S(2)}, u32[]{:S(2)}) collective-permute-start(bf16[1024,128]{1,0:T(8,128)(2,1)S(1)} %copy-done.7), channel_id=1, source_target_pairs={{0,6},{2,0},{4,2},{6,4},{1,7},{3,1},{5,3},{7,5},{8,14},{10,8},{12,... | collective-permute-start | bytes 786440 | tf_op jit(solution)/shard_map/ppermute | solution.py:188
  37.4 12.3 %collective-permute-start.3 = (bf16[1024,128]{1,0:T(8,128)(2,1)S(1)}, bf16[1024,128]{1,0:T(8,128)(2,1)S(1)}, u32[]{:S(2)}, u32[]{:S(2)}) collective-permute-start(bf16[1024,128]{1,0:T(8,128)(2,1)S(1)} %collective-permute-done), channel_id=1, source_target_pairs={{0,2},{2,4},{4,6},{6,0},{1,3},{3,5},{5,7},{7,1},{8,10},{10,12},{12... | collective-permute-start | bytes 786440 | tf_op jit(solution)/shard_map/ppermute | solution.py:188
  45.0 9.6 %copy-start.1 = (bf16[4,1024,128]{2,1,0:T(8,128)(2,1)}, bf16[4,1024,128]{2,1,0:T(8,128)(2,1)S(1)}, u32[]{:S(2)}) copy-start(bf16[4,1024,128]{2,1,0:T(8,128)(2,1)S(1)} %pad_maximum_fusion.1.w2n) | copy-start | bytes 3145732
  45.0 9.5 %collective-permute-start.7 = (bf16[4,1024,128]{2,1,0:T(8,128)(2,1)S(1)}, bf16[4,1024,128]{2,1,0:T(8,128)(2,1)}, u32[]{:S(2)}, u32[]{:S(2)}) collective-permute-start(bf16[4,1024,128]{2,1,0:T(8,128)(2,1)S(1)} %pad_maximum_fusion.1.w2n), channel_id=1, source_target_pairs={{0,1},{1,0},{2,3},{3,2},{4,5},{5,4},{6,7},{7,6},{8,9},{9,8},{10,11... | collective-permute-start | bytes 3145736 | tf_op jit(solution)/shard_map/ppermute | solution.py:192
  49.9 4.6 %collective-permute-start.4 = (bf16[4,1024,128]{2,1,0:T(8,128)(2,1)S(1)}, bf16[4,1024,128]{2,1,0:T(8,128)(2,1)S(1)}, u32[]{:S(2)}, u32[]{:S(2)}) collective-permute-start(bf16[4,1024,128]{2,1,0:T(8,128)(2,1)S(1)} %pad_maximum_fusion.w1n), channel_id=1, source_target_pairs={{0,1},{1,0},{2,3},{3,2},{4,5},{5,4},{6,7},{7,6},{8,9},{9,8},{10,11... | collective-permute-start | bytes 3145736 | tf_op jit(solution)/shard_map/ppermute | solution.py:192
  73.2 18.9 %collective-permute-start.8 = (bf16[4,48,1024]{2,1,0:T(8,128)(2,1)}, bf16[4,48,1024]{2,1,0:T(8,128)(2,1)S(1)}, u32[]{:S(2)}, u32[]{:S(2)}) collective-permute-start(bf16[4,48,1024]{2,1,0:T(8,128)(2,1)} %get-tuple-element.43), channel_id=1, source_target_pairs={{0,1},{1,0},{2,3},{3,2},{4,5},{5,4},{6,7},{7,6},{8,9},{9,8},{10,11... | collective-permute-start | bytes 1179656 | tf_op jit(solution)/shard_map/ppermute | solution.py:192
  75.8 29.9 %all-to-all-start.2 = ((f32[64,2,384]{2,1,0:T(2,128)}), f32[64,2,384]{2,1,0:T(2,128)S(1)}, u32[]{:S(2)}, u32[]{:S(2)}) async-start(f32[64,2,384]{2,1,0:T(2,128)} %broadcast_in_dim.13), calls=%async_computation.2 | async-start | bytes 393216 | tf_op jit(solution)/shard_map/all_to_all | solution.py:244
  92.0 56.1 %all-gather.7.cloned.1.call-start = ((), (), s32[]{:S(2)}) async-start(), calls=%async_computation.6 | async-start | bytes 2064384 | tf_op jit(solution)/shard_map/all_gather | solution.py:263
  94.7 11.1 %collective-permute-start.10 = (bf16[48,1024]{1,0:T(8,128)(2,1)}, bf16[48,1024]{1,0:T(8,128)(2,1)S(1)}, u32[]{:S(2)}, u32[]{:S(2)}) collective-permute-start(bf16[48,1024]{1,0:T(8,128)(2,1)} %get-tuple-element.46), channel_id=1, source_target_pairs={{0,6},{2,0},{4,2},{6,4},{1,7},{3,1},{5,3},{7,5},{8,14},{10,8},{12,... | collective-permute-start | bytes 294920 | tf_op jit(solution)/shard_map/ppermute | solution.py:188
  97.7 11.3 %collective-permute-start.11 = (bf16[48,1024]{1,0:T(8,128)(2,1)}, bf16[48,1024]{1,0:T(8,128)(2,1)S(1)}, u32[]{:S(2)}, u32[]{:S(2)}) collective-permute-start(bf16[48,1024]{1,0:T(8,128)(2,1)} %get-tuple-element.47), channel_id=1, source_target_pairs={{0,4},{2,6},{4,0},{6,2},{1,5},{3,7},{5,1},{7,3},{8,12},{10,14},{12... | collective-permute-start | bytes 294920 | tf_op jit(solution)/shard_map/ppermute | solution.py:188
  101.1 10.9 %collective-permute-start.9 = (bf16[48,1024]{1,0:T(8,128)(2,1)}, bf16[48,1024]{1,0:T(8,128)(2,1)S(1)}, u32[]{:S(2)}, u32[]{:S(2)}) collective-permute-start(bf16[48,1024]{1,0:T(8,128)(2,1)} %get-tuple-element.45), channel_id=1, source_target_pairs={{0,2},{2,4},{4,6},{6,0},{1,3},{3,5},{5,7},{7,1},{8,10},{10,12},{12... | collective-permute-start | bytes 294920 | tf_op jit(solution)/shard_map/ppermute | solution.py:188
  105.7 10.8 %copy-start.8 = (bf16[48,1024]{1,0:T(8,128)(2,1)}, bf16[48,1024]{1,0:T(8,128)(2,1)S(1)}, u32[]{:S(2)}) copy-start(bf16[48,1024]{1,0:T(8,128)(2,1)S(1)} %collective-permute-done.10.b) | copy-start | bytes 294916
  134.5 36.5 %all-to-all-start.4 = ((bf16[64,16,384]{2,1,0:T(8,128)(2,1)}), bf16[64,16,384]{2,1,0:T(8,128)(2,1)S(1)}, u32[]{:S(2)}, u32[]{:S(2)}) async-start(bf16[64,16,384]{2,1,0:T(8,128)(2,1)} %weight.1), calls=%async_computation.4 | async-start | bytes 1572864 | tf_op jit(solution)/shard_map/all_to_all | solution.py:268
  (6 other events, 24.8 us)
Sparse Core Ops, SparseCore 0:
  10.7 35.2 all-gather.4
  48.2 31.2 all-gather.10
  81.6 33.0 all-gather.8
  116.7 31.3 all-gather.6

commit v3 on v2

v3 whole, which is shorter than its diff:
```python
import math

import jax
import jax.numpy as jnp
from jax import lax
from jax.experimental import pallas as pl
from jax.experimental.pallas import tpu as pltpu
from jax.sharding import Mesh
from jax.sharding import PartitionSpec as P

V = 88
PP = 4
LONP = 224
D = 1024
OWN = 112
HEAD = 48
COLS = 8 * HEAD
BF = jnp.bfloat16
F32 = jnp.float32
SPACE = ("z", "ya", "yb")
NEAR = ("yb", "x", "core")
FAR = ("z", "ya")
TENSOR = ("x", "core")
OFFS = (0, 3, 1, 2)


def dot(a, b, da, db):
    return lax.dot_general(a, b, (((da,), (db,)), ((), ())), preferred_element_type=F32)


def lanes(j):
    return pl.ds(pl.multiple_of(j * 128, 128), 128)


def call(body, name, outs, args, smem=(), scratch=(), flops=0, vmem=56):
    specs = [
        pl.BlockSpec(memory_space=pltpu.SMEM if i in smem else pltpu.VMEM) for i in range(len(args))
    ]
    return pl.pallas_call(
        body,
        name=name,
        out_shape=tuple(jax.ShapeDtypeStruct(s, t) for s, t in outs),
        in_specs=specs,
        out_specs=tuple(pl.BlockSpec(memory_space=pltpu.VMEM) for _ in outs),
        scratch_shapes=list(scratch),
        compiler_params=pltpu.CompilerParams(vmem_limit_bytes=vmem * 2**20),
        cost_estimate=pl.CostEstimate(flops=flops, bytes_accessed=4 * 2**20, transcendentals=0),
    )(*args)


def prep_body(kinds, tokens, targets, second, head, out, packed):
    real = V * PP // 8
    row = lax.broadcasted_iota(jnp.int32, (HEAD, 128 - OWN), 0)
    kind = jnp.zeros(row.shape, F32)
    for v in range(V // 8):
        kind = jnp.where(row // PP == v, kinds[v].astype(F32), kind)
    blank = jnp.zeros((HEAD - real, 128), F32)
    packed[:D, :] = second[...]
    for i in range(8):
        out[i, :OWN, :] = tokens[OWN * i : OWN * (i + 1), :]
        rest = jnp.concatenate([targets[:, OWN * i : OWN * (i + 1)], kind[:real]], axis=1)
        rest = jnp.concatenate([rest, blank], axis=0)
        for piece in range(3):
            at = OWN + HEAD * piece
            part = rest.astype(BF)
            out[i, at : at + HEAD, :] = part
            rest = rest - part.astype(F32)
        rows = jnp.concatenate([head[:, 128 * i : 128 * (i + 1)].astype(F32), blank], axis=0)
        packed[D + HEAD * i : D + HEAD * (i + 1), :] = rows.astype(BF)


def gelu_parts(z):
    cdf = 0.5 * (1.0 + lax.erf(z * (1.0 / math.sqrt(2.0))))
    return z * cdf, cdf + z * jnp.exp(-0.5 * z * z) * (1.0 / math.sqrt(2.0 * math.pi))


def block(refs, a, s, rows):
    three, last = refs[2 * a], refs[2 * a + 1]
    return three[s, rows, :] if s < 3 else last[rows, :]


def pairs(refs, rows=slice(0, D)):
    for a in range(2):
        for s in (0, 2):
            both = [block(refs, a, s, rows), block(refs, a, s + 1, rows)]
            yield jnp.concatenate(both, axis=1), 4 * a + s


def layer(idx, value, refs, pre):
    for both, at in pairs(refs):
        z = dot(value, both, 1, 0)
        pre[:, lanes(idx[at])] = z[:, :128]
        pre[:, lanes(idx[at + 1])] = z[:, 128:]
    return gelu_parts(pre[...])


def back_through(idx, grad, refs, rows=slice(0, D)):
    total = None
    for both, at in pairs(refs, rows):
        left = jnp.concatenate([grad[:, lanes(idx[at])], grad[:, lanes(idx[at + 1])]], axis=1)
        term = dot(left, both, 1, 1)
        total = term if total is None else total + term
    return total


def first_body(idx, given, n3, n1, f3, f1, hidden1, slope1, own, pre):
    for j in range(8):
        own[:, 128 * j : 128 * (j + 1)] = given[j, :OWN, :]
    hidden, slope = layer(idx, own[...], (n3, n1, f3, f1), pre)
    hidden1[...] = hidden.astype(BF)
    slope1[...] = slope


def second_body(
    idx, given, hidden1, n3, n1, f3, f1, land, weights, slope2, hidden2, me, sums, head, pre
):
    refs = (n3, n1, f3, f1)
    for a in range(2):
        for s in range(4):
            rows = pl.ds(pl.multiple_of(idx[4 * a + s] * HEAD, HEAD), HEAD)
            for i in range(8):
                piece = block(refs, a, s, slice(D + HEAD * i, D + HEAD * (i + 1)))
                head[rows, 128 * i : 128 * (i + 1)] = piece
    hidden, slope = layer(idx, hidden1[...], refs, pre)
    hidden2[...] = hidden.astype(BF)
    slope2[...] = slope
    predicted = dot(hidden2[...], head[...], 1, 1)
    pieces = [given[:, OWN + HEAD * p : OWN + HEAD * (p + 1), :].astype(F32) for p in range(3)]
    flipped = (pieces[0] + (pieces[1] + pieces[2])).reshape(COLS, 128).T
    kind = flipped[OWN : OWN + 1, :]
    column = lax.broadcasted_iota(jnp.int32, (8, COLS), 1)
    picks = (column % PP == lax.broadcasted_iota(jnp.int32, (8, COLS), 0)).astype(BF)
    on_land = dot(land[...], picks, 0, 0)[:OWN, :]
    valid = jnp.where(kind == 0.0, 1.0, jnp.where(kind == 1.0, on_land, 1.0 - on_land))
    masked = weights[...] * valid
    error = predicted - flipped[:OWN, :]
    product = masked * error
    me[...] = product
    pair = [jnp.sum(product * error, axis=0, keepdims=True), jnp.sum(masked, axis=0, keepdims=True)]
    sums[...] = jnp.broadcast_to(jnp.concatenate(pair, axis=0)[None], sums.shape)


def spread_body(came, out):
    out[...] = jnp.broadcast_to(jnp.sum(came[...], axis=0, keepdims=True), out.shape)


def head_body(idx, me, hidden2, keep, send, full):
    full[...] = dot(me[...].astype(BF), hidden2[...], 0, 0)
    core = idx[8]
    for k in range(4):
        for ref, c in ((keep, core), (send, 1 - core)):
            rows = pl.ds(pl.multiple_of((2 * k + c) * HEAD, HEAD), HEAD)
            ref[k] = full[rows, :].astype(BF)


def pair_body(idx, keep, came, own, up, down, across):
    x = idx[9]
    for ref, off in ((own, 0), (up, 1), (down, 3), (across, 2)):
        k = lax.rem(x + off, 4)
        ref[...] = (keep[k].astype(F32) + came[k].astype(F32)).astype(BF)


def over_cells(v):
    column = lax.broadcasted_iota(jnp.int32, v.shape, 1)
    n = v.shape[1]
    for step in (1, 2):
        ahead = pltpu.roll(v, n - step, 1)
        behind = pltpu.roll(v, step, 1)
        v = v + jnp.where((column // step) % 2 == 0, ahead, behind)
    return v


def backward_body(
    idx, scale, sums, me, slope1, slope2, head, n3, n1, f3, f1, joined, grad1, coefs, loss, g2
):
    total = over_cells(jnp.sum(sums[...], axis=0))
    column = lax.broadcasted_iota(jnp.int32, (1, COLS), 1)
    real = column % HEAD < V * PP // 8
    weight = jnp.where(real, total[1:2, :], 1.0)
    root = jnp.sqrt(total[0:1, :] / weight + 1e-06)
    loss[...] = jnp.sum(jnp.where(real, root, 0.0), axis=1, keepdims=True) / (V * PP)
    coef = jnp.where(real, scale[0] / (V * root * weight), 0.0)
    coefs[...] = coef
    grad_pred = (coef * me[...]).astype(BF)
    g2[...] = (dot(grad_pred, head[...], 1, 0) * slope2[...]).astype(BF)
    back = back_through(idx, g2, (n3, n1, f3, f1))
    grad1[...] = (back * slope1[...]).astype(BF)
    for j in range(8):
        joined[j, :, :128] = g2[:, 128 * j : 128 * (j + 1)]
        joined[j, :, 128:] = grad1[:, 128 * j : 128 * (j + 1)]


def token_body(idx, grad1, n3, n1, f3, f1, out):
    out[...] = back_through(idx, grad1, (n3, n1, f3, f1), lanes(idx[10]))


def weight_body(hidden1, tokens, joined, own, a, b, c, out):
    grads = joined[...].reshape(8 * OWN, 256)
    second = dot(grads[:, :128], hidden1[...], 0, 0).T.reshape(64, 16, 128)
    first = dot(grads[:, 128:], tokens[...], 0, 0).T.reshape(64, 16, 128)
    part = own[...].astype(F32) + a[...].astype(F32) + b[...].astype(F32) + c[...].astype(F32)
    part = jnp.concatenate([part, jnp.zeros((128 - HEAD, D), F32)], axis=0).T
    part = part.reshape(64, 2, 8, 128)
    high = pltpu.roll(part[:, 1].reshape(512, 128), HEAD, 1).reshape(64, 8, 128)
    out[...] = jnp.concatenate([second, first, part[:, 0] + high], axis=1).astype(BF)


def shift(v, by):
    return lax.ppermute(v, "x", [(i, (i + by) % 4) for i in range(4)])


def flip(v):
    return lax.ppermute(v, "core", [(0, 1), (1, 0)])


def per_device(
    tokens, first_weight, second_weight, head_weight, targets, land_mask, variable_kind, loss_scale
):
    x, core = lax.axis_index("x"), lax.axis_index("core")
    mine = lax.axis_index(TENSOR)
    places = [2 * ((x + off) % 4) + c for c in (core, 1 - core) for off in OFFS]
    idx = jnp.stack([*places, core, x, mine]).astype(jnp.int32)

    given, packed = call(
        prep_body, "prep", [((8, OWN + 3 * HEAD, 128), BF), ((D + COLS, 128), BF)],
        [variable_kind, tokens, targets, second_weight, head_weight], smem=(0,),
    )
    given = lax.all_to_all(given, TENSOR, 0, 0, tiled=True)
    w1_m1, w1_p1 = shift(first_weight, 1), shift(first_weight, 3)
    w2_m1, w2_p1 = shift(packed, 1), shift(packed, 3)
    w1_m1, w1_p1, w2_m1, w2_p1, given = lax.optimization_barrier((w1_m1, w1_p1, w2_m1, w2_p1, given))
    w1_last, w2_last = shift(w1_m1, 1), shift(w2_p1, 3)
    w1_three = jnp.stack([first_weight, w1_m1, w1_p1])
    w2_three = jnp.stack([packed, w2_m1, w2_p1])
    w1 = (w1_three, w1_last, flip(w1_three), flip(w1_last))
    w2 = (w2_three, w2_last, flip(w2_three), flip(w2_last))
    full_tokens = lax.all_gather(tokens, TENSOR, axis=1, tiled=True)

    land = lax.dynamic_slice(land_mask, (0, mine * OWN), (PP, OWN))
    land = jnp.pad(land.astype(BF), ((0, 8 - PP), (0, 128 - OWN)))
    space = lax.axis_index(SPACE)
    patch_row = (space * 8 * OWN + mine * OWN) // LONP
    nlat = 2 * (64 * 8 * OWN // LONP)
    col = jnp.arange(COLS, dtype=jnp.int32)
    lat_row = 2 * patch_row + (col % PP) // 2
    weights = jnp.cos(math.pi / 2.0 * (lat_row.astype(F32) + 0.5) / nlat)
    weights = jnp.where(col % HEAD < 44, weights, 0.0)[None, :]

    hidden1, slope1 = call(
        first_body, "first", [((OWN, D), BF), ((OWN, D), F32)], [idx, given, *w1], smem=(0,),
        scratch=[pltpu.VMEM((OWN, D), BF), pltpu.VMEM((OWN, D), F32)], flops=3 * 10**8,
    )
    full_hidden1 = lax.all_gather(hidden1, TENSOR, axis=0, tiled=True)
    slope2, hidden2, me, sums, head = call(
        second_body, "second",
        [((OWN, D), F32), ((OWN, D), BF), ((OWN, COLS), F32), ((16, 2, COLS), F32), ((COLS, D), BF)],
        [idx, given, hidden1, *w2, land, weights],
        smem=(0,), scratch=[pltpu.VMEM((OWN, D), F32)], flops=5 * 10**8,
    )

    sums = lax.all_to_all(sums, NEAR, 0, 0, tiled=True)
    sums, me, hidden2 = lax.optimization_barrier((sums, me, hidden2))
    (sums,) = call(spread_body, "spread", [((32, 2, COLS), F32)], [sums])
    sums = lax.all_to_all(sums, FAR, 0, 0, tiled=True)

    keep, send = call(
        head_body, "head_part", [((4, HEAD, D), BF)] * 2, [idx, me, hidden2],
        smem=(0,), scratch=[pltpu.VMEM((COLS, D), F32)], flops=10**8,
    )
    own, up, down, across = call(
        pair_body, "pair", [((HEAD, D), BF)] * 4, [idx, keep, flip(send)], smem=(0,)
    )
    sums, own, up, down, across = lax.optimization_barrier((sums, own, up, down, across))
    head_parts = [own, shift(up, 1), shift(down, 3), shift(across, 2)]

    joined, grad1, coefs, loss = call(
        backward_body, "backward",
        [((8, OWN, 256), BF), ((OWN, D), BF), ((1, COLS), F32), ((1, 1), F32)],
        [idx, loss_scale.reshape(1), sums, me, slope1, slope2, head, *w2],
        smem=(0, 1), scratch=[pltpu.VMEM((OWN, D), BF)], flops=5 * 10**8,
    )
    joined = lax.all_to_all(joined, TENSOR, 0, 0, tiled=True)
    full_grad1 = lax.all_gather(grad1, TENSOR, axis=0, tiled=True)
    (out,) = call(
        weight_body, "weight", [((64, 40, 128), BF)],
        [full_hidden1, full_tokens, joined, *head_parts], flops=5 * 10**8,
    )
    out = lax.all_to_all(out, SPACE, 0, 0, tiled=True)
    (token_grad,) = call(
        token_body, "token", [((8 * OWN, 128), F32)], [idx, full_grad1, *w1],
        smem=(0,), flops=3 * 10**8,
    )
    out = jnp.sum(out.astype(F32), axis=0)
    local = lax.dynamic_slice(coefs, (0, mine * HEAD), (1, 44))
    halves = jnp.concatenate([out[32:, :44], out[32:, HEAD : HEAD + 44]], axis=0)
    return loss.reshape(()), token_grad, out[16:32], out[:16], (halves * local).T


def solution(mesh):
    inner = Mesh(mesh.devices.reshape(8, 4, 2, 4, 2), ("z", "ya", "yb", "x", "core"))
    return jax.shard_map(
        per_device,
        mesh=inner,
        in_specs=(
            P(SPACE, TENSOR),
            P(None, TENSOR),
            P(None, TENSOR),
            P(TENSOR, None),
            P(TENSOR, SPACE),
            P(None, SPACE),
            P(TENSOR),
            P(),
        ),
        out_specs=(
            P(),
            P(SPACE, TENSOR),
            P(SPACE, TENSOR),
            P(SPACE, TENSOR),
            P(TENSOR, SPACE),
        ),
        check_vma=False,
    )
```

time: 180 us -> 209 us (1.16)
  waiting for transfers between devices: 41.6 us -> 69 us
  blocking collectives: 23.2 us -> 16.2 us
  Pallas kernels: 23.6 us -> 27.3 us
    ppermute x9, waiting for transfers between devices: 19.3 us -> 40.7 us  [shift(): return lax.ppermute(v, 'x', [(i, (i + by) % 4) for i in range(4)])]
    all_to_all x1 -> x2, waiting for transfers between devices: 2.05 us -> 9.05 us  [the longest x1 9.05 us: per_device(): sums = lax.all_to_all(sums, FAR, 0, 0, tiled=True)]
    all_to_all x2 -> x1, blocking collectives: 23.2 us -> 16.2 us  [per_device(): sums = lax.all_to_all(sums, NEAR, 0, 0, tiled=True)]
    all_to_all x1, starting transfers between devices: 12.7 us -> 5.9 us  [per_device(): out = lax.all_to_all(out, SPACE, 0, 0, tiled=True)]
    unnamed x22 -> x42, local copies, waits for them, and re-layouts: 1.69 us -> 6.21 us
    ppermute x3 -> x5, starting transfers between devices: 5.75 us -> 9.8 us  [flip(): return lax.ppermute(v, 'core', [(0, 1), (1, 0)])]
    pallas_call x7 -> x9, Pallas kernels: 23.6 us -> 27.3 us  [call(): pl.pallas_call(body, name=name, out_shape=tuple((jax.ShapeDtypeStruct(s,...]
    ppermute x9, starting transfers between devices: 26.9 us -> 30.2 us  [shift(): return lax.ppermute(v, 'x', [(i, (i + by) % 4) for i in range(4)])]
  transfers between devices with their start and end apart: 19 -> 21, of which waited for: 8 -> 9; matrix products, arithmetic and copies ran while one was open for 3% -> 2% of each run, Pallas kernels for 13% -> 13%
where the time goes in v3:
time: 209 us; the launch traced here: 208 us
  waiting for transfers between devices  69 us (33%)
  starting transfers between devices  67.9 us (32%)
  Pallas kernels  27.3 us (13%)
  blocking collectives  16.2 us (8%)
  between operations  14.8 us (7%)
  local copies, waits for them, and re-layouts  8.93 us (4%)
  other arithmetic  3.32 us (2%)
    ppermute x9, waiting for transfers between devices, shift(): return lax.ppermute(v, 'x', [(i, (i + by) % 4) for i in range(4)])  40.7 us
    ppermute x9, starting transfers between devices, shift(): return lax.ppermute(v, 'x', [(i, (i + by) % 4) for i in range(4)])  30.2 us
    pallas_call x9, Pallas kernels, call(): pl.pallas_call(body, name=name, out_shape=tuple((jax.ShapeDtypeStruct(s,...  27.3 us
    all_to_all x1, waiting for transfers between devices, per_device(): out = lax.all_to_all(out, SPACE, 0, 0, tiled=True)  17.7 us
    all_to_all x1, blocking collectives, per_device(): sums = lax.all_to_all(sums, NEAR, 0, 0, tiled=True)  16.2 us
    all_to_all x1, starting transfers between devices, per_device(): sums = lax.all_to_all(sums, FAR, 0, 0, tiled=True)  14 us
    ppermute x5, starting transfers between devices, flip(): return lax.ppermute(v, 'core', [(0, 1), (1, 0)])  9.8 us
    all_to_all x1, waiting for transfers between devices, per_device(): sums = lax.all_to_all(sums, FAR, 0, 0, tiled=True)  9.05 us
  transfers between devices with their start and end apart: 21, of which 9 were waited for; matrix products, arithmetic and copies ran while one was open for 2% of the time, Pallas kernels for 13%

profile of v3, /device:TPU:8, one launch (start us, length us, event | category | flops | bytes accessed | tf_op | source)
XLA Modules:
  0.0 207.5 jit_solution(16176268710710978728)
XLA Ops:
  10.1 4.3 %all-to-all-start = ((bf16[8,256,128]{2,1,0:T(8,128)(2,1)}), bf16[8,256,128]{2,1,0:T(8,128)(2,1)S(1)}, u32[]{:S(2)}, u32[]{:S(2)}) async-start(bf16[8,256,128]{2,1,0:T(8,128)(2,1)} %get-tuple-element.38), calls=%async_computation | async-start | bytes 1048576 | tf_op jit(solution)/shard_map/all_to_all | solution.py:228
  14.5 3.9 %collective-permute-start.2 = (bf16[1408,128]{1,0:T(8,128)(2,1)}, bf16[1408,128]{1,0:T(8,128)(2,1)S(1)}, u32[]{:S(2)}, u32[]{:S(2)}) collective-permute-start(bf16[1408,128]{1,0:T(8,128)(2,1)} %get-tuple-element.37), channel_id=1, source_target_pairs={{0,2},{2,4},{4,6},{6,0},{1,3},{3,5},{5,7},{7,1},{8,10},{10,12},{12... | collective-permute-start | bytes 1081352 | tf_op jit(solution)/shard_map/ppermute | solution.py:209
  18.4 3.2 %collective-permute-start.3 = (bf16[1408,128]{1,0:T(8,128)(2,1)}, bf16[1408,128]{1,0:T(8,128)(2,1)S(1)}, u32[]{:S(2)}, u32[]{:S(2)}) collective-permute-start(bf16[1408,128]{1,0:T(8,128)(2,1)} %get-tuple-element.37), channel_id=1, source_target_pairs={{0,6},{2,0},{4,2},{6,4},{1,7},{3,1},{5,3},{7,5},{8,14},{10,8},{12,... | collective-permute-start | bytes 1081352 | tf_op jit(solution)/shard_map/ppermute | solution.py:209
  24.2 4.4 %collective-permute-start.1 = (bf16[1024,128]{1,0:T(8,128)(2,1)S(1)}, bf16[1024,128]{1,0:T(8,128)(2,1)S(1)}, u32[]{:S(2)}, u32[]{:S(2)}) collective-permute-start(bf16[1024,128]{1,0:T(8,128)(2,1)S(1)} %copy-done.14), channel_id=1, source_target_pairs={{0,6},{2,0},{4,2},{6,4},{1,7},{3,1},{5,3},{7,5},{8,14},{10,8},{12,... | collective-permute-start | bytes 786440 | tf_op jit(solution)/shard_map/ppermute | solution.py:209
  28.6 11.7 %collective-permute-done = bf16[1024,128]{1,0:T(8,128)(2,1)S(1)} collective-permute-done((bf16[1024,128]{1,0:T(8,128)(2,1)S(1)}, bf16[1024,128]{1,0:T(8,128)(2,1)S(1)}, u32[]{:S(2)}, u32[]{:S(2)}) %collective-permute-start) | collective-permute-done | bytes 262176 | tf_op jit(solution)/shard_map/ppermute | solution.py:209
  43.1 2.8 %collective-permute-start.4 = (bf16[1024,128]{1,0:T(8,128)(2,1)S(1)}, bf16[1024,128]{1,0:T(8,128)(2,1)S(1)}, u32[]{:S(2)}, u32[]{:S(2)}) collective-permute-start(bf16[1024,128]{1,0:T(8,128)(2,1)S(1)} %collective-permute-done), channel_id=1, source_target_pairs={{0,2},{2,4},{4,6},{6,0},{1,3},{3,5},{5,7},{7,1},{8,10},{10,12},{12... | collective-permute-start | bytes 786440 | tf_op jit(solution)/shard_map/ppermute | solution.py:209
  45.8 9.0 %collective-permute-done.4.n1 = bf16[1024,128]{1,0:T(8,128)(2,1)S(1)} collective-permute-done((bf16[1024,128]{1,0:T(8,128)(2,1)S(1)}, bf16[1024,128]{1,0:T(8,128)(2,1)S(1)}, u32[]{:S(2)}, u32[]{:S(2)}) %collective-permute-start.4) | collective-permute-done | bytes 262176 | tf_op jit(solution)/shard_map/ppermute | solution.py:209
  59.9 3.3 %first.1 = (bf16[112,1024]{1,0:T(8,128)(2,1)}, f32[112,1024]{1,0:T(8,128)}) custom-call(s32[11]{0:T(128)} %stack.71.idx, bf16[8,256,128]{2,1,0:T(8,128)(2,1)} %copy-done.2, bf16[3,1024,128]{2,1,0:T(8,128)(2,1)} %copy-done.1, bf16[1024,128]{1,0:T(8,128)(2,1)} %copy-done.8, bf16[3,1024,128]{2,1,0:T(8,128)(2,1)} %copy-done.4, bf16[1024,128]{1,0:T(8,128)(2,1)} %copy-done.9), custom_call_target="tpu_custom_call" | custom-call | flops 300000000 | bytes 4194304 | tf_op jit(solution)/shard_map/first/pallas_call | solution.py:39
  68.6 10.4 %collective-permute-done.7.n1 = bf16[1408,128]{1,0:T(8,128)(2,1)S(1)} collective-permute-done((bf16[1408,128]{1,0:T(8,128)(2,1)S(1)}, bf16[1408,128]{1,0:T(8,128)(2,1)S(1)}, u32[]{:S(2)}, u32[]{:S(2)}) %collective-permute-start.7) | collective-permute-done | bytes 360480 | tf_op jit(solution)/shard_map/ppermute | solution.py:209
  84.8 4.1 %second.3 = (f32[112,1024]{1,0:T(8,128)}, bf16[112,1024]{1,0:T(8,128)(2,1)}, f32[112,384]{1,0:T(8,128)}, f32[16,2,384]{2,1,0:T(2,128)}, bf16[384,1024]{1,0:T(8,128)(2,1)}) custom-call(s32[11]{0:T(128)} %stack.71.idx, bf16[8,256,128]{2,1,0:T(8,128)(2,1)} %copy-done.2, bf16[112,1024]{1,0:T(8,128)(2,1)} %get-tuple-element.42.hidden1, ...), custom_call_target="tpu_custom_call" | custom-call | flops 500000000 | bytes 4194304 | tf_op jit(solution)/shard_map/second/pallas_call | solution.py:39
  88.8 16.2 %all_to_all.25.came = f32[16,2,384]{2,1,0:T(2,128)} all-to-all(f32[16,2,384]{2,1,0:T(2,128)} %get-tuple-element.45), channel_id=1, replica_groups=mesh['z'=8,'ya'=4,'yb'=2,'x'=4,'core'=2] {'yb','x','core'}, dimensions={0} | all-to-all | bytes 98304 | tf_op jit(solution)/shard_map/all_to_all | solution.py:261
  110.9 14.0 %all-to-all-start.2 = ((f32[32,2,384]{2,1,0:T(2,128)}), f32[32,2,384]{2,1,0:T(2,128)S(1)}, u32[]{:S(2)}, u32[]{:S(2)}) async-start(f32[32,2,384]{2,1,0:T(2,128)} %spread.1), calls=%async_computation.2 | async-start | bytes 196608 | tf_op jit(solution)/shard_map/all_to_all | solution.py:264
  128.2 9.0 %all-to-all-done.2.sums = f32[32,2,384]{2,1,0:T(2,128)S(1)} async-done(((f32[32,2,384]{2,1,0:T(2,128)}), f32[32,2,384]{2,1,0:T(2,128)S(1)}, u32[]{:S(2)}, u32[]{:S(2)}) %all-to-all-start.2) | async-done | bytes 98336 | tf_op jit(solution)/shard_map/all_to_all | solution.py:264
  137.9 4.5 %backward.1 = (bf16[8,112,256]{2,1,0:T(8,128)(2,1)}, bf16[112,1024]{1,0:T(8,128)(2,1)}, f32[1,384]{1,0:T(1,128)}, f32[1,1]{1,0:T(1,128)}) custom-call(s32[11]{0:T(128)} %stack.71.idx, f32[1]{0:T(128)} %bitcast.23.scale, f32[32,2,384]{2,1,0:T(2,128)} %copy-done.11, f32[112,384]{1,0:T(8,128)} %get-tuple-element.49.me, f32[112,1024]{1,0:T(8,128)} %get-tuple-element.58.slope1, ...), custom_call_target="tpu_custom_call" | custom-call | flops 500000000 | bytes 4194304 | tf_op jit(solution)/shard_map/backward/pallas_call | solution.py:39
  142.5 3.6 %all-to-all-start.3 = ((bf16[8,112,256]{2,1,0:T(8,128)(2,1)}), bf16[8,112,256]{2,1,0:T(8,128)(2,1)S(1)}, u32[]{:S(2)}, u32[]{:S(2)}) async-start(bf16[8,112,256]{2,1,0:T(8,128)(2,1)} %get-tuple-element.63), calls=%async_computation.3 | async-start | bytes 917504 | tf_op jit(solution)/shard_map/all_to_all | solution.py:282
  146.2 3.8 %collective-permute-start.11 = (bf16[48,1024]{1,0:T(8,128)(2,1)S(1)}, bf16[48,1024]{1,0:T(8,128)(2,1)S(1)}, u32[]{:S(2)}, u32[]{:S(2)}) collective-permute-start(bf16[48,1024]{1,0:T(8,128)(2,1)S(1)} %copy-done.20), channel_id=1, source_target_pairs={{0,2},{2,4},{4,6},{6,0},{1,3},{3,5},{5,7},{7,1},{8,10},{10,12},{12... | collective-permute-start | bytes 294920 | tf_op jit(solution)/shard_map/ppermute | solution.py:209
  150.0 3.3 %collective-permute-start.12 = (bf16[48,1024]{1,0:T(8,128)(2,1)S(1)}, bf16[48,1024]{1,0:T(8,128)(2,1)S(1)}, u32[]{:S(2)}, u32[]{:S(2)}) collective-permute-start(bf16[48,1024]{1,0:T(8,128)(2,1)S(1)} %copy-done.19), channel_id=1, source_target_pairs={{0,6},{2,0},{4,2},{6,4},{1,7},{3,1},{5,3},{7,5},{8,14},{10,8},{12,... | collective-permute-start | bytes 294920 | tf_op jit(solution)/shard_map/ppermute | solution.py:209
  153.3 4.1 %collective-permute-start.13 = (bf16[48,1024]{1,0:T(8,128)(2,1)S(1)}, bf16[48,1024]{1,0:T(8,128)(2,1)S(1)}, u32[]{:S(2)}, u32[]{:S(2)}) collective-permute-start(bf16[48,1024]{1,0:T(8,128)(2,1)S(1)} %copy-done.18), channel_id=1, source_target_pairs={{0,4},{2,6},{4,0},{6,2},{1,5},{3,7},{5,1},{7,3},{8,12},{10,14},{12... | collective-permute-start | bytes 294920 | tf_op jit(solution)/shard_map/ppermute | solution.py:209
  157.4 3.6 %collective-permute-done.11.a = bf16[48,1024]{1,0:T(8,128)(2,1)S(1)} collective-permute-done((bf16[48,1024]{1,0:T(8,128)(2,1)S(1)}, bf16[48,1024]{1,0:T(8,128)(2,1)S(1)}, u32[]{:S(2)}, u32[]{:S(2)}) %collective-permute-start.11) | collective-permute-done | bytes 98336 | tf_op jit(solution)/shard_map/ppermute | solution.py:209
  162.0 5.0 %collective-permute-done.13.c = bf16[48,1024]{1,0:T(8,128)(2,1)S(1)} collective-permute-done((bf16[48,1024]{1,0:T(8,128)(2,1)S(1)}, bf16[48,1024]{1,0:T(8,128)(2,1)S(1)}, u32[]{:S(2)}, u32[]{:S(2)}) %collective-permute-start.13) | collective-permute-done | bytes 98336 | tf_op jit(solution)/shard_map/ppermute | solution.py:209
  167.7 3.9 %weight.1 = bf16[64,40,128]{2,1,0:T(8,128)(2,1)} custom-call(bf16[896,1024]{1,0:T(8,128)(2,1)} %all-gather.6.cloned.1.call-done.hidden1, bf16[896,1024]{1,0:T(8,128)(2,1)} %all-gather.8.cloned.1.call-done.tokens, bf16[8,112,256]{2,1,0:T(8,128)(2,1)} %copy-done.5, bf16[48,1024]{1,0:T(8,128)(2,1)} %get-tuple-element.64.own, bf16[48,1024]{1,0:T(8,128)(2,1)} %copy-done.15, ...), custom_call_target="tpu_custom_call" | custom-call | flops 500000000 | bytes 4194304 | tf_op jit(solution)/shard_map/weight/pallas_call | solution.py:39
  171.7 5.9 %all-to-all-start.4 = ((bf16[64,40,128]{2,1,0:T(8,128)(2,1)}), bf16[64,40,128]{2,1,0:T(8,128)(2,1)S(1)}, u32[]{:S(2)}, u32[]{:S(2)}) async-start(bf16[64,40,128]{2,1,0:T(8,128)(2,1)} %weight.1), calls=%async_computation.4 | async-start | bytes 1310720 | tf_op jit(solution)/shard_map/all_to_all | solution.py:288
  178.4 3.5 %token_.1 = f32[896,128]{1,0:T(8,128)} custom-call(s32[11]{0:T(128)} %stack.71.idx, bf16[896,1024]{1,0:T(8,128)(2,1)} %all-gather.4.cloned.1.call-done.grad1, bf16[3,1024,128]{2,1,0:T(8,128)(2,1)} %copy-done.1, bf16[1024,128]{1,0:T(8,128)(2,1)} %copy-done.8, bf16[3,1024,128]{2,1,0:T(8,128)(2,1)} %copy-done.4, bf16[1024,128]{1,0:T(8,128)(2,1)} %copy-done.9), custom_call_target="tpu_custom_call" | custom-call | flops 300000000 | bytes 4194304 | tf_op jit(solution)/shard_map/token/pallas_call | solution.py:39
  181.8 17.7 %all-to-all-done.4 = bf16[64,40,128]{2,1,0:T(8,128)(2,1)S(1)} async-done(((bf16[64,40,128]{2,1,0:T(8,128)(2,1)}), bf16[64,40,128]{2,1,0:T(8,128)(2,1)S(1)}, u32[]{:S(2)}, u32[]{:S(2)}) %all-to-all-start.4) | async-done | bytes 655392 | tf_op jit(solution)/shard_map/all_to_all | solution.py:288
  (84 shorter events, 37.4 us)
Async XLA Ops:
  7.2 159.8 %all-gather.8.cloned.1.call-start = ((), (), s32[]{:S(2)}) async-start(), calls=%async_computation.7 | async-start | bytes 2064384 | tf_op jit(solution)/shard_map/all_gather | solution.py:237
  10.1 30.2 %all-to-all-start = ((bf16[8,256,128]{2,1,0:T(8,128)(2,1)}), bf16[8,256,128]{2,1,0:T(8,128)(2,1)S(1)}, u32[]{:S(2)}, u32[]{:S(2)}) async-start(bf16[8,256,128]{2,1,0:T(8,128)(2,1)} %get-tuple-element.38), calls=%async_computation | async-start | bytes 1048576 | tf_op jit(solution)/shard_map/all_to_all | solution.py:228
  14.4 152.6 %all-gather.6.cloned.1.call-start = ((), (), s32[]{:S(2)}) async-start(), calls=%async_computation.6 | async-start | bytes 2064384 | tf_op jit(solution)/shard_map/all_gather | solution.py:253
  14.5 25.8 %collective-permute-start.2 = (bf16[1408,128]{1,0:T(8,128)(2,1)}, bf16[1408,128]{1,0:T(8,128)(2,1)S(1)}, u32[]{:S(2)}, u32[]{:S(2)}) collective-permute-start(bf16[1408,128]{1,0:T(8,128)(2,1)} %get-tuple-element.37), channel_id=1, source_target_pairs={{0,2},{2,4},{4,6},{6,0},{1,3},{3,5},{5,7},{7,1},{8,10},{10,12},{12... | collective-permute-start | bytes 1081352 | tf_op jit(solution)/shard_map/ppermute | solution.py:209
  18.4 21.9 %collective-permute-start.3 = (bf16[1408,128]{1,0:T(8,128)(2,1)}, bf16[1408,128]{1,0:T(8,128)(2,1)S(1)}, u32[]{:S(2)}, u32[]{:S(2)}) collective-permute-start(bf16[1408,128]{1,0:T(8,128)(2,1)} %get-tuple-element.37), channel_id=1, source_target_pairs={{0,6},{2,0},{4,2},{6,4},{1,7},{3,1},{5,3},{7,5},{8,14},{10,8},{12,... | collective-permute-start | bytes 1081352 | tf_op jit(solution)/shard_map/ppermute | solution.py:209
  21.6 18.7 %collective-permute-start = (bf16[1024,128]{1,0:T(8,128)(2,1)S(1)}, bf16[1024,128]{1,0:T(8,128)(2,1)S(1)}, u32[]{:S(2)}, u32[]{:S(2)}) collective-permute-start(bf16[1024,128]{1,0:T(8,128)(2,1)S(1)} %copy-done.14), channel_id=1, source_target_pairs={{0,2},{2,4},{4,6},{6,0},{1,3},{3,5},{5,7},{7,1},{8,10},{10,12},{12... | collective-permute-start | bytes 786440 | tf_op jit(solution)/shard_map/ppermute | solution.py:209
  24.2 16.1 %collective-permute-start.1 = (bf16[1024,128]{1,0:T(8,128)(2,1)S(1)}, bf16[1024,128]{1,0:T(8,128)(2,1)S(1)}, u32[]{:S(2)}, u32[]{:S(2)}) collective-permute-start(bf16[1024,128]{1,0:T(8,128)(2,1)S(1)} %copy-done.14), channel_id=1, source_target_pairs={{0,6},{2,0},{4,2},{6,4},{1,7},{3,1},{5,3},{7,5},{8,14},{10,8},{12,... | collective-permute-start | bytes 786440 | tf_op jit(solution)/shard_map/ppermute | solution.py:209
  40.3 18.0 %copy-start.2 = (bf16[8,256,128]{2,1,0:T(8,128)(2,1)}, bf16[8,256,128]{2,1,0:T(8,128)(2,1)S(1)}, u32[]{:S(2)}) copy-start(bf16[8,256,128]{2,1,0:T(8,128)(2,1)S(1)} %all-to-all-done.given) | copy-start | bytes 1572868
  41.1 17.2 %copy-start.1 = (bf16[3,1024,128]{2,1,0:T(8,128)(2,1)}, bf16[3,1024,128]{2,1,0:T(8,128)(2,1)S(1)}, u32[]{:S(2)}) copy-start(bf16[3,1024,128]{2,1,0:T(8,128)(2,1)S(1)} %pad_maximum_fusion.1.n3) | copy-start | bytes 2359300
  41.2 17.2 %collective-permute-start.5 = (bf16[3,1024,128]{2,1,0:T(8,128)(2,1)S(1)}, bf16[3,1024,128]{2,1,0:T(8,128)(2,1)S(1)}, u32[]{:S(2)}, u32[]{:S(2)}) collective-permute-start(bf16[3,1024,128]{2,1,0:T(8,128)(2,1)S(1)} %pad_maximum_fusion.1.n3), channel_id=1, source_target_pairs={{0,1},{1,0},{2,3},{3,2},{4,5},{5,4},{6,7},{7,6},{8,9},{9,8},{10,11... | collective-permute-start | bytes 2359304 | tf_op jit(solution)/shard_map/ppermute | solution.py:213
  43.1 11.8 %collective-permute-start.4 = (bf16[1024,128]{1,0:T(8,128)(2,1)S(1)}, bf16[1024,128]{1,0:T(8,128)(2,1)S(1)}, u32[]{:S(2)}, u32[]{:S(2)}) collective-permute-start(bf16[1024,128]{1,0:T(8,128)(2,1)S(1)} %collective-permute-done), channel_id=1, source_target_pairs={{0,2},{2,4},{4,6},{6,0},{1,3},{3,5},{5,7},{7,1},{8,10},{10,12},{12... | collective-permute-start | bytes 786440 | tf_op jit(solution)/shard_map/ppermute | solution.py:209
  54.9 3.4 %collective-permute-start.6 = (bf16[1024,128]{1,0:T(8,128)(2,1)S(1)}, bf16[1024,128]{1,0:T(8,128)(2,1)S(1)}, u32[]{:S(2)}, u32[]{:S(2)}) collective-permute-start(bf16[1024,128]{1,0:T(8,128)(2,1)S(1)} %collective-permute-done.4.n1), channel_id=1, source_target_pairs={{0,1},{1,0},{2,3},{3,2},{4,5},{5,4},{6,7},{7,6},{8,9},{9,8},{10,11... | collective-permute-start | bytes 786440 | tf_op jit(solution)/shard_map/ppermute | solution.py:213
  64.4 18.6 %copy-start = (bf16[3,1408,128]{2,1,0:T(8,128)(2,1)}, bf16[3,1408,128]{2,1,0:T(8,128)(2,1)S(1)}, u32[]{:S(2)}) copy-start(bf16[3,1408,128]{2,1,0:T(8,128)(2,1)S(1)} %pad_maximum_fusion.n3) | copy-start | bytes 3244036
  64.4 18.6 %collective-permute-start.8 = (bf16[3,1408,128]{2,1,0:T(8,128)(2,1)S(1)}, bf16[3,1408,128]{2,1,0:T(8,128)(2,1)S(1)}, u32[]{:S(2)}, u32[]{:S(2)}) collective-permute-start(bf16[3,1408,128]{2,1,0:T(8,128)(2,1)S(1)} %pad_maximum_fusion.n3), channel_id=1, source_target_pairs={{0,1},{1,0},{2,3},{3,2},{4,5},{5,4},{6,7},{7,6},{8,9},{9,8},{10,11... | collective-permute-start | bytes 3244040 | tf_op jit(solution)/shard_map/ppermute | solution.py:213
  66.4 12.6 %collective-permute-start.7 = (bf16[1408,128]{1,0:T(8,128)(2,1)S(1)}, bf16[1408,128]{1,0:T(8,128)(2,1)S(1)}, u32[]{:S(2)}, u32[]{:S(2)}) collective-permute-start(bf16[1408,128]{1,0:T(8,128)(2,1)S(1)} %collective-permute-done.3), channel_id=1, source_target_pairs={{0,6},{2,0},{4,2},{6,4},{1,7},{3,1},{5,3},{7,5},{8,14},{10,8},{12,... | collective-permute-start | bytes 1081352 | tf_op jit(solution)/shard_map/ppermute | solution.py:209
  79.0 3.9 %collective-permute-start.9 = (bf16[1408,128]{1,0:T(8,128)(2,1)S(1)}, bf16[1408,128]{1,0:T(8,128)(2,1)S(1)}, u32[]{:S(2)}, u32[]{:S(2)}) collective-permute-start(bf16[1408,128]{1,0:T(8,128)(2,1)S(1)} %collective-permute-done.7.n1), channel_id=1, source_target_pairs={{0,1},{1,0},{2,3},{3,2},{4,5},{5,4},{6,7},{7,6},{8,9},{9,8},{10,11... | collective-permute-start | bytes 1081352 | tf_op jit(solution)/shard_map/ppermute | solution.py:213
  107.4 18.2 %collective-permute-start.10 = (bf16[4,48,1024]{2,1,0:T(8,128)(2,1)}, bf16[4,48,1024]{2,1,0:T(8,128)(2,1)S(1)}, u32[]{:S(2)}, u32[]{:S(2)}) collective-permute-start(bf16[4,48,1024]{2,1,0:T(8,128)(2,1)} %get-tuple-element.52), channel_id=1, source_target_pairs={{0,1},{1,0},{2,3},{3,2},{4,5},{5,4},{6,7},{7,6},{8,9},{9,8},{10,11... | collective-permute-start | bytes 1179656 | tf_op jit(solution)/shard_map/ppermute | solution.py:213
  110.9 26.4 %all-to-all-start.2 = ((f32[32,2,384]{2,1,0:T(2,128)}), f32[32,2,384]{2,1,0:T(2,128)S(1)}, u32[]{:S(2)}, u32[]{:S(2)}) async-start(f32[32,2,384]{2,1,0:T(2,128)} %spread.1), calls=%async_computation.2 | async-start | bytes 196608 | tf_op jit(solution)/shard_map/all_to_all | solution.py:264
  124.9 53.5 %all-gather.4.cloned.1.call-start = ((), (), s32[]{:S(2)}) async-start(), calls=%async_computation.5 | async-start | bytes 2064384 | tf_op jit(solution)/shard_map/all_gather | solution.py:283
  142.5 24.4 %all-to-all-start.3 = ((bf16[8,112,256]{2,1,0:T(8,128)(2,1)}), bf16[8,112,256]{2,1,0:T(8,128)(2,1)S(1)}, u32[]{:S(2)}, u32[]{:S(2)}) async-start(bf16[8,112,256]{2,1,0:T(8,128)(2,1)} %get-tuple-element.63), calls=%async_computation.3 | async-start | bytes 917504 | tf_op jit(solution)/shard_map/all_to_all | solution.py:282
  146.2 14.9 %collective-permute-start.11 = (bf16[48,1024]{1,0:T(8,128)(2,1)S(1)}, bf16[48,1024]{1,0:T(8,128)(2,1)S(1)}, u32[]{:S(2)}, u32[]{:S(2)}) collective-permute-start(bf16[48,1024]{1,0:T(8,128)(2,1)S(1)} %copy-done.20), channel_id=1, source_target_pairs={{0,2},{2,4},{4,6},{6,0},{1,3},{3,5},{5,7},{7,1},{8,10},{10,12},{12... | collective-permute-start | bytes 294920 | tf_op jit(solution)/shard_map/ppermute | solution.py:209
  150.0 12.0 %collective-permute-start.12 = (bf16[48,1024]{1,0:T(8,128)(2,1)S(1)}, bf16[48,1024]{1,0:T(8,128)(2,1)S(1)}, u32[]{:S(2)}, u32[]{:S(2)}) collective-permute-start(bf16[48,1024]{1,0:T(8,128)(2,1)S(1)} %copy-done.19), channel_id=1, source_target_pairs={{0,6},{2,0},{4,2},{6,4},{1,7},{3,1},{5,3},{7,5},{8,14},{10,8},{12,... | collective-permute-start | bytes 294920 | tf_op jit(solution)/shard_map/ppermute | solution.py:209
  153.3 13.7 %collective-permute-start.13 = (bf16[48,1024]{1,0:T(8,128)(2,1)S(1)}, bf16[48,1024]{1,0:T(8,128)(2,1)S(1)}, u32[]{:S(2)}, u32[]{:S(2)}) collective-permute-start(bf16[48,1024]{1,0:T(8,128)(2,1)S(1)} %copy-done.18), channel_id=1, source_target_pairs={{0,4},{2,6},{4,0},{6,2},{1,5},{3,7},{5,1},{7,3},{8,12},{10,14},{12... | collective-permute-start | bytes 294920 | tf_op jit(solution)/shard_map/ppermute | solution.py:209
  171.7 27.9 %all-to-all-start.4 = ((bf16[64,40,128]{2,1,0:T(8,128)(2,1)}), bf16[64,40,128]{2,1,0:T(8,128)(2,1)S(1)}, u32[]{:S(2)}, u32[]{:S(2)}) async-start(bf16[64,40,128]{2,1,0:T(8,128)(2,1)} %weight.1), calls=%async_computation.4 | async-start | bytes 1310720 | tf_op jit(solution)/shard_map/all_to_all | solution.py:288
  (18 other events, 67.4 us)
Sparse Core Ops, SparseCore 0:
  10.1 39.0 all-gather.7
  63.4 35.4 all-gather.5
  142.7 25.9 all-gather.3

commit v4 on v3

v4 whole, which is shorter than its diff:
```python
import math

import jax
import jax.numpy as jnp
from jax import lax
from jax.experimental import pallas as pl
from jax.experimental.pallas import tpu as pltpu
from jax.sharding import Mesh
from jax.sharding import PartitionSpec as P

V = 88
PP = 4
LONP = 224
D = 1024
OWN = 112
HEAD = 48
COLS = 8 * HEAD
HALF = 3 * D // 2
PIECE = OWN + 3 * HEAD
BF = jnp.bfloat16
F32 = jnp.float32
SPACE = ("z", "y")
TENSOR = ("x", "core")
OFFS = (0, 3, 1, 2)
PACK = 10**8
BACK = 3 * 10**10
TOKEN = 3 * 10**10


def dot(a, b, da, db):
    return lax.dot_general(a, b, (((da,), (db,)), ((), ())), preferred_element_type=F32)


def lanes(j):
    return pl.ds(pl.multiple_of(j * 128, 128), 128)


def call(body, name, outs, args, smem=(), scratch=(), flops=0, vmem=56, loose=()):
    specs = [
        pl.BlockSpec(
            memory_space=pltpu.SMEM if i in smem else pl.ANY if i in loose else pltpu.VMEM
        )
        for i in range(len(args))
    ]
    return pl.pallas_call(
        body,
        name=name,
        out_shape=tuple(jax.ShapeDtypeStruct(s, t) for s, t in outs),
        in_specs=specs,
        out_specs=tuple(pl.BlockSpec(memory_space=pltpu.VMEM) for _ in outs),
        scratch_shapes=list(scratch),
        compiler_params=pltpu.CompilerParams(vmem_limit_bytes=vmem * 2**20),
        cost_estimate=pl.CostEstimate(flops=flops, bytes_accessed=4 * 2**20, transcendentals=0),
    )(*args)


def prep_body(kinds, tokens, targets, second, head, out, packed):
    real = V * PP // 8
    row = lax.broadcasted_iota(jnp.int32, (HEAD, 128 - OWN), 0)
    kind = jnp.zeros(row.shape, F32)
    for v in range(V // 8):
        kind = jnp.where(row // PP == v, kinds[v].astype(F32), kind)
    blank = jnp.zeros((HEAD - real, 128), F32)
    packed[:D, :] = second[...]
    for i in range(8):
        out[i, :OWN, :] = tokens[OWN * i : OWN * (i + 1), :]
        rest = jnp.concatenate([targets[:, OWN * i : OWN * (i + 1)], kind[:real]], axis=1)
        rest = jnp.concatenate([rest, blank], axis=0)
        for piece in range(3):
            at = OWN + HEAD * piece
            part = rest.astype(BF)
            out[i, at : at + HEAD, :] = part
            rest = rest - part.astype(F32)
        rows = jnp.concatenate([head[:, 128 * i : 128 * (i + 1)].astype(F32), blank], axis=0)
        packed[D + HEAD * i : D + HEAD * (i + 1), :] = rows.astype(BF)


def gelu_parts(z):
    cdf = 0.5 * (1.0 + lax.erf(z * (1.0 / math.sqrt(2.0))))
    return z * cdf, cdf + z * jnp.exp(-0.5 * z * z) * (1.0 / math.sqrt(2.0 * math.pi))


def pairs(refs, rows=slice(0, D)):
    for a in range(2):
        for k in (0, 2):
            both = [refs[a][k, rows, :], refs[a][k + 1, rows, :]]
            yield jnp.concatenate(both, axis=1), 4 * a + k


def layer(idx, value, refs, pre):
    for both, at in pairs(refs):
        z = dot(value, both, 1, 0)
        pre[:, lanes(idx[at])] = z[:, :128]
        pre[:, lanes(idx[at + 1])] = z[:, 128:]
    return gelu_parts(pre[...])


def back_through(idx, grad, refs, rows=slice(0, D)):
    total = None
    for both, at in pairs(refs, rows):
        left = jnp.concatenate([grad[:, lanes(idx[at])], grad[:, lanes(idx[at + 1])]], axis=1)
        term = dot(left, both, 1, 1)
        total = term if total is None else total + term
    return total


def first_body(idx, given, near, far, tokhid, slope1, pre):
    for j in range(8):
        tokhid[:, 128 * j : 128 * (j + 1)] = given[j, :OWN, :]
    hidden, slope = layer(idx, tokhid[:, :D], (near, far), pre)
    tokhid[:, D:] = hidden.astype(BF)
    slope1[...] = slope


def second_body(
    idx, tokhid, given, near, far, land, weights, hidden2, slope2, me, sums, head, pre, goal
):
    for j in range(8):
        parts = [
            given[j, OWN + HEAD * p : OWN + HEAD * (p + 1), :].astype(F32) for p in range(3)
        ]
        goal[HEAD * j : HEAD * (j + 1), :] = parts[0] + (parts[1] + parts[2])
    for a, ref in enumerate((near, far)):
        for s in range(4):
            rows = pl.ds(pl.multiple_of(idx[4 * a + s] * HEAD, HEAD), HEAD)
            for i in range(8):
                piece = ref[s, D + HEAD * i : D + HEAD * (i + 1), :]
                head[rows, 128 * i : 128 * (i + 1)] = piece
    hidden, slope = layer(idx, tokhid[:, D:], (near, far), pre)
    hidden2[...] = hidden.astype(BF)
    slope2[...] = slope
    predicted = dot(hidden2[...], head[...], 1, 1)
    flipped = goal[...].T
    kind = flipped[OWN : OWN + 1, :]
    column = lax.broadcasted_iota(jnp.int32, (8, COLS), 1)
    picks = (column % PP == lax.broadcasted_iota(jnp.int32, (8, COLS), 0)).astype(BF)
    on_land = dot(land[...], picks, 0, 0)[:OWN, :]
    valid = jnp.where(kind == 0.0, 1.0, jnp.where(kind == 1.0, on_land, 1.0 - on_land))
    masked = weights[...] * valid
    error = predicted - flipped[:OWN, :]
    product = masked * error
    me[...] = product
    pair = [jnp.sum(product * error, axis=0, keepdims=True), jnp.sum(masked, axis=0, keepdims=True)]
    sums[...] = jnp.broadcast_to(jnp.concatenate(pair, axis=0)[None], sums.shape)


def spread_body(came, out):
    out[...] = jnp.broadcast_to(jnp.sum(came[...], axis=0, keepdims=True), out.shape)


def pack_body(tokhid, hidden2, came, xh):
    xh[0] = tokhid[:, :HALF]
    xh[1, :, : 2 * D - HALF] = tokhid[:, HALF:]
    xh[1, :, 2 * D - HALF :] = hidden2[...]


def over_cells(v):
    column = lax.broadcasted_iota(jnp.int32, v.shape, 1)
    n = v.shape[1]
    for step in (1, 2):
        ahead = pltpu.roll(v, n - step, 1)
        behind = pltpu.roll(v, step, 1)
        v = v + jnp.where((column // step) % 2 == 0, ahead, behind)
    return v


def backward_body(
    idx, scale, sums, me, slope1, slope2, head, near, far, joined, grad1, loss, g2
):
    total = over_cells(jnp.sum(sums[...], axis=0))
    column = lax.broadcasted_iota(jnp.int32, (1, COLS), 1)
    real = column % HEAD < V * PP // 8
    weight = jnp.where(real, total[1:2, :], 1.0)
    root = jnp.sqrt(total[0:1, :] / weight + 1e-06)
    loss[...] = jnp.sum(jnp.where(real, root, 0.0), axis=1, keepdims=True) / (V * PP)
    coef = jnp.where(real, scale[0] / (V * root * weight), 0.0)
    grad_pred = (coef * me[...]).astype(BF)
    g2[...] = (dot(grad_pred, head[...], 1, 0) * slope2[...]).astype(BF)
    back = back_through(idx, g2, (near, far))
    grad1[...] = (back * slope1[...]).astype(BF)
    for j in range(8):
        joined[j, :, :128] = g2[:, 128 * j : 128 * (j + 1)]
        joined[j, :, 128:256] = grad1[:, 128 * j : 128 * (j + 1)]
        tail = grad_pred[:, HEAD * j : HEAD * (j + 1)].astype(F32)
        tail = jnp.concatenate([tail, jnp.zeros((OWN, 128 - HEAD), F32)], axis=1)
        joined[j, :, 256:] = tail.astype(BF)


def token_body(idx, grad1, near, far, keep, send):
    grad = None
    for both, at in pairs((near, far)):
        left = jnp.concatenate([grad1[:, lanes(idx[at])], grad1[:, lanes(idx[at + 1])]], axis=1)
        term = dot(left, both, 1, 1)
        grad = term if grad is None else grad + term
    mine = idx[8] == 0
    for k in range(4):
        even, odd = grad[:, 256 * k : 256 * k + 128], grad[:, 256 * k + 128 : 256 * (k + 1)]
        keep[k] = jnp.where(mine, even, odd)
        send[k] = jnp.where(mine, odd, even)


def split_body(idx, keep, came, own, up, down, across):
    for ref, off in ((own, 0), (up, 1), (down, 3), (across, 2)):
        k = lax.rem(idx[9] + off, 4)
        ref[0] = keep[k]
        ref[1] = came[k]


def place_body(idx, own, left, right, across, out):
    for s, ref in enumerate((own, left, right, across)):
        for a in range(2):
            rows = pl.ds(pl.multiple_of(idx[4 * a + s] * OWN, OWN), OWN)
            out[rows, :] = ref[a]


def weight_body(idx, near, far, joined, out, order):
    for at in range(8):
        order[OWN * at : OWN * (at + 1), :] = joined[idx[at]]
    half = 4 * OWN
    sums = []
    places = (((1, 0, 512), (0, D, HALF)), ((0, 0, D),), ((1, 512, HALF),))
    for to, cuts in zip((0, 128, 256), (places[0][::-1], places[1], places[2])):
        found = []
        for h, lo, hi in cuts:
            term = dot(order[:half, to : to + 128], near[:, h, :, lo:hi].reshape(half, hi - lo), 0, 0)
            term += dot(order[half:, to : to + 128], far[:, h, :, lo:hi].reshape(half, hi - lo), 0, 0)
            found.append(term.T)
        sums.append(found[0] if len(found) == 1 else jnp.concatenate(found, axis=0))
    part = sums[2].reshape(64, 2, 8, 128)
    high = pltpu.roll(part[:, 1].reshape(512, 128), HEAD, 1).reshape(64, 8, 128)
    wide = [sums[0].reshape(64, 16, 128), sums[1].reshape(64, 16, 128), part[:, 0] + high]
    out[...] = jnp.concatenate(wide, axis=1).astype(BF)


def shift(v, by):
    return lax.ppermute(v, "x", [(i, (i + by) % 4) for i in range(4)])


def flip(v):
    return lax.ppermute(v, "core", [(0, 1), (1, 0)])


def per_device(
    tokens, first_weight, second_weight, head_weight, targets, land_mask, variable_kind, loss_scale
):
    x, core = lax.axis_index("x"), lax.axis_index("core")
    mine = lax.axis_index(TENSOR)
    places = [2 * ((x + off) % 4) + c for c in (core, 1 - core) for off in OFFS]
    idx = jnp.stack([*places, core, x]).astype(jnp.int32)

    given, packed = call(
        prep_body, "prep", [((8, PIECE, 128), BF), ((D + COLS, 128), BF)],
        [variable_kind, tokens, targets, second_weight, head_weight], smem=(0,),
    )
    given = lax.all_to_all(given, TENSOR, 0, 0, tiled=True)
    w1_m1, w1_p1 = shift(first_weight, 1), shift(first_weight, 3)
    w2_m1, w2_p1 = shift(packed, 1), shift(packed, 3)
    w1_m1, w1_p1, w2_m1, w2_p1, given = lax.optimization_barrier((w1_m1, w1_p1, w2_m1, w2_p1, given))
    w1_last, w2_last = shift(w1_m1, 1), shift(w2_p1, 3)
    w1_last, w2_last = lax.optimization_barrier((w1_last, w2_last))
    near1 = jnp.stack([first_weight, w1_m1, w1_p1, w1_last])
    near2 = jnp.stack([packed, w2_m1, w2_p1, w2_last])
    far1, far2 = flip(near1), flip(near2)

    land = lax.dynamic_slice(land_mask, (0, mine * OWN), (PP, OWN))
    land = jnp.pad(land.astype(BF), ((0, 8 - PP), (0, 128 - OWN)))
    space = lax.axis_index(SPACE)
    patch_row = (space * 8 * OWN + mine * OWN) // LONP
    nlat = 2 * (64 * 8 * OWN // LONP)
    col = jnp.arange(COLS, dtype=jnp.int32)
    lat_row = 2 * patch_row + (col % PP) // 2
    weights = jnp.cos(math.pi / 2.0 * (lat_row.astype(F32) + 0.5) / nlat)
    weights = jnp.where(col % HEAD < 44, weights, 0.0)[None, :]

    tokhid, slope1 = call(
        first_body, "first", [((OWN, 2 * D), BF), ((OWN, D), F32)], [idx, given, near1, far1],
        smem=(0,), scratch=[pltpu.VMEM((OWN, D), F32)], flops=3 * 10**8,
    )
    hidden2, slope2, me, sums, head = call(
        second_body, "second",
        [((OWN, D), BF), ((OWN, D), F32), ((OWN, COLS), F32), ((8, 2, COLS), F32), ((COLS, D), BF)],
        [idx, tokhid, given, near2, far2, land, weights], smem=(0,),
        scratch=[pltpu.VMEM((OWN, D), F32), pltpu.VMEM((COLS, 128), F32)], flops=5 * 10**8,
    )

    sums = lax.all_to_all(sums, TENSOR, 0, 0, tiled=True)
    (spread,) = call(spread_body, "spread", [((64, 2, COLS), F32)], [sums])
    (xh,) = call(
        pack_body, "pack", [((2, OWN, HALF), BF)], [tokhid, hidden2, sums], loose=(2,),
        flops=PACK,
    )
    sums = lax.all_to_all(spread, SPACE, 0, 0, tiled=True)

    xh_m1, xh_p1 = shift(xh, 1), shift(xh, 3)
    xh_last = jnp.stack([shift(xh_m1[0], 1), shift(xh_p1[1], 3)])
    xhn = jnp.stack([xh, xh_m1, xh_p1, xh_last])
    xhf = flip(xhn)

    joined, grad1, loss = call(
        backward_body, "backward",
        [((8, OWN, 384), BF), ((OWN, D), BF), ((1, 1), F32)],
        [idx, loss_scale.reshape(1), sums, me, slope1, slope2, head, near2, far2],
        smem=(0, 1), scratch=[pltpu.VMEM((OWN, D), BF)], flops=BACK,
    )
    joined = lax.all_to_all(joined, TENSOR, 0, 0, tiled=True)
    (out,) = call(
        weight_body, "weight", [((64, 40, 128), BF)], [idx, xhn, xhf, joined], smem=(0,),
        scratch=[pltpu.VMEM((8 * OWN, 384), BF)], flops=8 * 10**8,
    )
    keep, send = call(
        token_body, "token", [((4, OWN, 128), F32)] * 2, [idx, grad1, near1, far1], smem=(0,),
        flops=TOKEN,
    )
    came, keep, out = lax.optimization_barrier((flip(send), keep, out))
    out = lax.all_to_all(out, SPACE, 0, 0, tiled=True)
    own, up, down, across = call(
        split_body, "split", [((2, OWN, 128), F32)] * 4, [idx, keep, came], smem=(0,)
    )
    (token_grad,) = call(
        place_body, "place", [((8 * OWN, 128), F32)],
        [idx, own, shift(up, 1), shift(down, 3), shift(across, 2)], smem=(0,),
    )
    out = jnp.sum(out.astype(F32), axis=0)
    halves = jnp.concatenate([out[32:, :44], out[32:, HEAD : HEAD + 44]], axis=0)
    return loss.reshape(()), token_grad, out[16:32], out[:16], halves.T


def solution(mesh):
    inner = Mesh(mesh.devices.reshape(8, 8, 4, 2), ("z", "y", "x", "core"))
    return jax.shard_map(
        per_device,
        mesh=inner,
        in_specs=(
            P(SPACE, TENSOR),
            P(None, TENSOR),
            P(None, TENSOR),
            P(TENSOR, None),
            P(TENSOR, SPACE),
            P(None, SPACE),
            P(TENSOR),
            P(),
        ),
        out_specs=(
            P(),
            P(SPACE, TENSOR),
            P(SPACE, TENSOR),
            P(SPACE, TENSOR),
            P(TENSOR, SPACE),
        ),
        check_vma=False,
    )
```

time: 209 us -> 168 us (0.80)
  waiting for transfers between devices: 69 us -> 34.9 us
  starting transfers between devices: 67.9 us -> 81.8 us
  between operations: 14.8 us -> 1.77 us
  blocking collectives: 16.2 us -> 9.33 us
  local copies, waits for them, and re-layouts: 8.93 us -> 5.44 us
  Pallas kernels: 27.3 us -> 29.8 us
    ppermute x9 -> x13, waiting for transfers between devices: 40.7 us -> 23.9 us  [shift(): return lax.ppermute(v, 'x', [(i, (i + by) % 4) for i in range(4)])]
    all_to_all x1, waiting for transfers between devices: 17.7 us -> 1.97 us  [per_device(): out = lax.all_to_all(out, SPACE, 0, 0, tiled=True)]
    ppermute x9 -> x13, starting transfers between devices: 30.2 us -> 40.9 us  [shift(): return lax.ppermute(v, 'x', [(i, (i + by) % 4) for i in range(4)])]
    all_to_all x1, blocking collectives: 16.2 us -> 9.33 us  [per_device(): sums = lax.all_to_all(sums, TENSOR, 0, 0, tiled=True)]
    all_to_all x1, waiting for transfers between devices: 9.05 us -> 6.16 us  [per_device(): sums = lax.all_to_all(spread, SPACE, 0, 0, tiled=True)]
    all_to_all x1, waiting for transfers between devices: 0.01 us -> 2.86 us  [per_device(): joined = lax.all_to_all(joined, TENSOR, 0, 0, tiled=True)]
    unnamed x42 -> x32, local copies, waits for them, and re-layouts: 6.21 us -> 3.52 us
    all_to_all x1, starting transfers between devices: 14 us -> 16.6 us  [per_device(): sums = lax.all_to_all(spread, SPACE, 0, 0, tiled=True)]
  transfers between devices with their start and end apart: 21 -> 21, of which waited for: 9 -> 7; matrix products, arithmetic and copies ran while one was open for 2% -> 2% of each run, Pallas kernels for 13% -> 13%
where the time goes in v4:
time: 168 us; the launch traced here: 167 us
  starting transfers between devices  81.8 us (49%)
  waiting for transfers between devices  34.9 us (21%)
  Pallas kernels  29.8 us (18%)
  blocking collectives  9.33 us (6%)
  local copies, waits for them, and re-layouts  5.44 us (3%)
  other arithmetic  3.86 us (2%)
  between operations  1.77 us (1%)
    ppermute x13, starting transfers between devices, shift(): return lax.ppermute(v, 'x', [(i, (i + by) % 4) for i in range(4)])  40.9 us
    pallas_call x10, Pallas kernels, call(): pl.pallas_call(body, name=name, out_shape=tuple((jax.ShapeDtypeStruct(s,...  29.8 us
    ppermute x13, waiting for transfers between devices, shift(): return lax.ppermute(v, 'x', [(i, (i + by) % 4) for i in range(4)])  23.9 us
    all_to_all x1, starting transfers between devices, per_device(): sums = lax.all_to_all(spread, SPACE, 0, 0, tiled=True)  16.6 us
    all_to_all x1, blocking collectives, per_device(): sums = lax.all_to_all(sums, TENSOR, 0, 0, tiled=True)  9.33 us
    ppermute x4, starting transfers between devices, flip(): return lax.ppermute(v, 'core', [(0, 1), (1, 0)])  8.64 us
    all_to_all x1, starting transfers between devices, per_device(): out = lax.all_to_all(out, SPACE, 0, 0, tiled=True)  6.96 us
    all_to_all x1, waiting for transfers between devices, per_device(): sums = lax.all_to_all(spread, SPACE, 0, 0, tiled=True)  6.16 us
  transfers between devices with their start and end apart: 21, of which 7 were waited for; matrix products, arithmetic and copies ran while one was open for 2% of the time, Pallas kernels for 13%

profile of v4, /device:TPU:8, one launch (start us, length us, event | category | flops | bytes accessed | tf_op | source)
XLA Modules:
  0.0 166.9 jit_solution(8223210244967945062)
XLA Ops:
  2.9 4.3 %all-to-all-start = ((bf16[8,256,128]{2,1,0:T(8,128)(2,1)}), bf16[8,256,128]{2,1,0:T(8,128)(2,1)S(1)}, u32[]{:S(2)}, u32[]{:S(2)}) async-start(bf16[8,256,128]{2,1,0:T(8,128)(2,1)} %get-tuple-element.34), calls=%async_computation | async-start | bytes 1048576 | tf_op jit(solution)/shard_map/all_to_all | solution.py:255
  7.2 5.1 %collective-permute-start.3 = (bf16[1408,128]{1,0:T(8,128)(2,1)}, bf16[1408,128]{1,0:T(8,128)(2,1)S(1)}, u32[]{:S(2)}, u32[]{:S(2)}) collective-permute-start(bf16[1408,128]{1,0:T(8,128)(2,1)} %get-tuple-element.33), channel_id=1, source_target_pairs={{0,6},{2,0},{4,2},{6,4},{1,7},{3,1},{5,3},{7,5},{8,14},{10,8},{12,... | collective-permute-start | bytes 1081352 | tf_op jit(solution)/shard_map/ppermute | solution.py:236
  14.3 2.7 %collective-permute-start = (bf16[1024,128]{1,0:T(8,128)(2,1)S(1)}, bf16[1024,128]{1,0:T(8,128)(2,1)S(1)}, u32[]{:S(2)}, u32[]{:S(2)}) collective-permute-start(bf16[1024,128]{1,0:T(8,128)(2,1)S(1)} %copy-done.10), channel_id=1, source_target_pairs={{0,2},{2,4},{4,6},{6,0},{1,3},{3,5},{5,7},{7,1},{8,10},{10,12},{12... | collective-permute-start | bytes 786440 | tf_op jit(solution)/shard_map/ppermute | solution.py:236
  17.0 4.3 %collective-permute-start.1 = (bf16[1024,128]{1,0:T(8,128)(2,1)S(1)}, bf16[1024,128]{1,0:T(8,128)(2,1)S(1)}, u32[]{:S(2)}, u32[]{:S(2)}) collective-permute-start(bf16[1024,128]{1,0:T(8,128)(2,1)S(1)} %copy-done.10), channel_id=1, source_target_pairs={{0,6},{2,0},{4,2},{6,4},{1,7},{3,1},{5,3},{7,5},{8,14},{10,8},{12,... | collective-permute-start | bytes 786440 | tf_op jit(solution)/shard_map/ppermute | solution.py:236
  21.4 10.1 %collective-permute-done = bf16[1024,128]{1,0:T(8,128)(2,1)S(1)} collective-permute-done((bf16[1024,128]{1,0:T(8,128)(2,1)S(1)}, bf16[1024,128]{1,0:T(8,128)(2,1)S(1)}, u32[]{:S(2)}, u32[]{:S(2)}) %collective-permute-start) | collective-permute-done | bytes 262176 | tf_op jit(solution)/shard_map/ppermute | solution.py:236
  33.8 3.5 %collective-permute-start.4 = (bf16[1024,128]{1,0:T(8,128)(2,1)S(1)}, bf16[1024,128]{1,0:T(8,128)(2,1)S(1)}, u32[]{:S(2)}, u32[]{:S(2)}) collective-permute-start(bf16[1024,128]{1,0:T(8,128)(2,1)S(1)} %collective-permute-done), channel_id=1, source_target_pairs={{0,2},{2,4},{4,6},{6,0},{1,3},{3,5},{5,7},{7,1},{8,10},{10,12},{12... | collective-permute-start | bytes 786440 | tf_op jit(solution)/shard_map/ppermute | solution.py:236
  37.4 7.3 %collective-permute-done.4 = bf16[1024,128]{1,0:T(8,128)(2,1)S(1)} collective-permute-done((bf16[1024,128]{1,0:T(8,128)(2,1)S(1)}, bf16[1024,128]{1,0:T(8,128)(2,1)S(1)}, u32[]{:S(2)}, u32[]{:S(2)}) %collective-permute-start.4) | collective-permute-done | bytes 262176 | tf_op jit(solution)/shard_map/ppermute | solution.py:236
  54.1 3.3 %first.1 = (bf16[112,2048]{1,0:T(8,128)(2,1)}, f32[112,1024]{1,0:T(8,128)}) custom-call(s32[10]{0:T(128)} %stack.97.idx, bf16[8,256,128]{2,1,0:T(8,128)(2,1)} %copy-done.2, bf16[4,1024,128]{2,1,0:T(8,128)(2,1)} %copy-done.3, bf16[4,1024,128]{2,1,0:T(8,128)(2,1)} %copy-done.9), custom_call_target="tpu_custom_call" | custom-call | flops 300000000 | bytes 4194304 | tf_op jit(solution)/shard_map/first/pallas_call | solution.py:45
  57.4 4.1 %second.3 = (bf16[112,1024]{1,0:T(8,128)(2,1)}, f32[112,1024]{1,0:T(8,128)}, f32[112,384]{1,0:T(8,128)}, f32[8,2,384]{2,1,0:T(2,128)}, bf16[384,1024]{1,0:T(8,128)(2,1)}) custom-call(s32[10]{0:T(128)} %stack.97.idx, bf16[112,2048]{1,0:T(8,128)(2,1)} %get-tuple-element.40.tokhid, bf16[8,256,128]{2,1,0:T(8,128)(2,1)} %copy-done.2, ...), custom_call_target="tpu_custom_call" | custom-call | flops 500000000 | bytes 4194304 | tf_op jit(solution)/shard_map/second/pallas_call | solution.py:45
  61.4 9.3 %all_to_all.25.came = f32[8,2,384]{2,1,0:T(2,128)} all-to-all(f32[8,2,384]{2,1,0:T(2,128)} %get-tuple-element.43), channel_id=1, replica_groups=mesh['z'=8,'y'=8,'x'=4,'core'=2] {'x','core'}, dimensions={0} | all-to-all | bytes 49152 | tf_op jit(solution)/shard_map/all_to_all | solution.py:286
  72.8 3.1 %collective-permute-start.10 = (bf16[2,112,1536]{2,1,0:T(8,128)(2,1)}, bf16[2,112,1536]{2,1,0:T(8,128)(2,1)S(1)}, u32[]{:S(2)}, u32[]{:S(2)}) collective-permute-start(bf16[2,112,1536]{2,1,0:T(8,128)(2,1)} %pack.1), channel_id=1, source_target_pairs={{0,6},{2,0},{4,2},{6,4},{1,7},{3,1},{5,3},{7,5},{8,14},{10,8},{12,... | collective-permute-start | bytes 2064392 | tf_op jit(solution)/shard_map/ppermute | solution.py:236
  75.8 2.8 %collective-permute-start.9 = (bf16[2,112,1536]{2,1,0:T(8,128)(2,1)}, bf16[2,112,1536]{2,1,0:T(8,128)(2,1)S(1)}, u32[]{:S(2)}, u32[]{:S(2)}) collective-permute-start(bf16[2,112,1536]{2,1,0:T(8,128)(2,1)} %pack.1), channel_id=1, source_target_pairs={{0,2},{2,4},{4,6},{6,0},{1,3},{3,5},{5,7},{7,1},{8,10},{10,12},{12... | collective-permute-start | bytes 2064392 | tf_op jit(solution)/shard_map/ppermute | solution.py:236
  80.7 16.6 %all-to-all-start.2 = ((f32[64,2,384]{2,1,0:T(2,128)}), f32[64,2,384]{2,1,0:T(2,128)S(1)}, u32[]{:S(2)}, u32[]{:S(2)}) async-start(f32[64,2,384]{2,1,0:T(2,128)} %spread.1), calls=%async_computation.2 | async-start | bytes 393216 | tf_op jit(solution)/shard_map/all_to_all | solution.py:292
  97.4 4.3 %collective-permute-start.12 = (bf16[112,1536]{1,0:T(8,128)(2,1)S(1)}, bf16[112,1536]{1,0:T(8,128)(2,1)S(1)}, u32[]{:S(2)}, u32[]{:S(2)}) collective-permute-start(bf16[112,1536]{1,0:T(8,128)(2,1)S(1)} %slice_bitcast_fusion), channel_id=1, source_target_pairs={{0,6},{2,0},{4,2},{6,4},{1,7},{3,1},{5,3},{7,5},{8,14},{10,8},{12,... | collective-permute-start | bytes 1032200 | tf_op jit(solution)/shard_map/ppermute | solution.py:236
  103.6 6.2 %all-to-all-done.2.sums = f32[64,2,384]{2,1,0:T(2,128)S(1)} async-done(((f32[64,2,384]{2,1,0:T(2,128)}), f32[64,2,384]{2,1,0:T(2,128)S(1)}, u32[]{:S(2)}, u32[]{:S(2)}) %all-to-all-start.2) | async-done | bytes 196640 | tf_op jit(solution)/shard_map/all_to_all | solution.py:292
  110.5 4.8 %backward.1 = (bf16[8,112,384]{2,1,0:T(8,128)(2,1)}, bf16[112,1024]{1,0:T(8,128)(2,1)}, f32[1,1]{1,0:T(1,128)}) custom-call(s32[10]{0:T(128)} %stack.97.idx, f32[1]{0:T(128)} %bitcast.33.scale, f32[64,2,384]{2,1,0:T(2,128)} %copy-done.12, f32[112,384]{1,0:T(8,128)} %get-tuple-element.44.me, f32[112,1024]{1,0:T(8,128)} %get-tuple-element.45.slope1, ...), custom_call_target="tpu_custom_call" | custom-call | flops 30000001024 | bytes 4194304 | tf_op jit(solution)/shard_map/backward/pallas_call | solution.py:45
  115.3 4.3 %all-to-all-start.3 = ((bf16[8,112,384]{2,1,0:T(8,128)(2,1)}), bf16[8,112,384]{2,1,0:T(8,128)(2,1)}, u32[]{:S(2)}, u32[]{:S(2)}) async-start(bf16[8,112,384]{2,1,0:T(8,128)(2,1)} %get-tuple-element.53), calls=%async_computation.3 | async-start | bytes 1376256 | tf_op jit(solution)/shard_map/all_to_all | solution.py:305
  123.7 3.2 %token_.1 = (f32[4,112,128]{2,1,0:T(8,128)}, f32[4,112,128]{2,1,0:T(8,128)}) custom-call(s32[10]{0:T(128)} %stack.97.idx, bf16[112,1024]{1,0:T(8,128)(2,1)} %get-tuple-element.49.grad1, bf16[4,1024,128]{2,1,0:T(8,128)(2,1)} %copy-done.3, bf16[4,1024,128]{2,1,0:T(8,128)(2,1)} %copy-done.9), custom_call_target="tpu_custom_call" | custom-call | flops 30000001024 | bytes 4194304 | tf_op jit(solution)/shard_map/token/pallas_call | solution.py:45
  128.9 2.9 %all-to-all-done.3.joined = bf16[8,112,384]{2,1,0:T(8,128)(2,1)} async-done(((bf16[8,112,384]{2,1,0:T(8,128)(2,1)}), bf16[8,112,384]{2,1,0:T(8,128)(2,1)}, u32[]{:S(2)}, u32[]{:S(2)}) %all-to-all-start.3) | async-done | bytes 688160 | tf_op jit(solution)/shard_map/all_to_all | solution.py:305
  131.8 4.9 %weight.1 = bf16[64,40,128]{2,1,0:T(8,128)(2,1)} custom-call(s32[10]{0:T(128)} %stack.97.idx, bf16[4,2,112,1536]{3,2,1,0:T(8,128)(2,1)} %copy-done, bf16[4,2,112,1536]{3,2,1,0:T(8,128)(2,1)} %collective-permute-done.13.far, bf16[8,112,384]{2,1,0:T(8,128)(2,1)} %all-to-all-done.3.joined), custom_call_target="tpu_custom_call" | custom-call | flops 800000000 | bytes 4194304 | tf_op jit(solution)/shard_map/weight/pallas_call | solution.py:45
  136.7 7.0 %all-to-all-start.4 = ((bf16[64,40,128]{2,1,0:T(8,128)(2,1)}), bf16[64,40,128]{2,1,0:T(8,128)(2,1)S(1)}, u32[]{:S(2)}, u32[]{:S(2)}) async-start(bf16[64,40,128]{2,1,0:T(8,128)(2,1)} %weight.1), calls=%async_computation.4 | async-start | bytes 1310720 | tf_op jit(solution)/shard_map/all_to_all | solution.py:315
  148.0 4.6 %collective-permute-start.15 = (f32[2,112,128]{2,1,0:T(8,128)}, f32[2,112,128]{2,1,0:T(8,128)S(1)}, u32[]{:S(2)}, u32[]{:S(2)}) collective-permute-start(f32[2,112,128]{2,1,0:T(8,128)} %get-tuple-element.58), channel_id=1, source_target_pairs={{0,6},{2,0},{4,2},{6,4},{1,7},{3,1},{5,3},{7,5},{8,14},{10,8},{12,... | collective-permute-start | bytes 344072 | tf_op jit(solution)/shard_map/ppermute | solution.py:236
  154.6 3.1 %collective-permute-done.15.right = f32[2,112,128]{2,1,0:T(8,128)S(1)} collective-permute-done((f32[2,112,128]{2,1,0:T(8,128)}, f32[2,112,128]{2,1,0:T(8,128)S(1)}, u32[]{:S(2)}, u32[]{:S(2)}) %collective-permute-start.15) | collective-permute-done | bytes 114720 | tf_op jit(solution)/shard_map/ppermute | solution.py:236
  157.7 3.3 %collective-permute-done.16.across = f32[2,112,128]{2,1,0:T(8,128)S(1)} collective-permute-done((f32[2,112,128]{2,1,0:T(8,128)}, f32[2,112,128]{2,1,0:T(8,128)S(1)}, u32[]{:S(2)}, u32[]{:S(2)}) %collective-permute-start.16) | collective-permute-done | bytes 114720 | tf_op jit(solution)/shard_map/ppermute | solution.py:236
  (75 shorter events, 39.9 us)
Async XLA Ops:
  2.9 28.6 %all-to-all-start = ((bf16[8,256,128]{2,1,0:T(8,128)(2,1)}), bf16[8,256,128]{2,1,0:T(8,128)(2,1)S(1)}, u32[]{:S(2)}, u32[]{:S(2)}) async-start(bf16[8,256,128]{2,1,0:T(8,128)(2,1)} %get-tuple-element.34), calls=%async_computation | async-start | bytes 1048576 | tf_op jit(solution)/shard_map/all_to_all | solution.py:255
  7.2 24.3 %collective-permute-start.3 = (bf16[1408,128]{1,0:T(8,128)(2,1)}, bf16[1408,128]{1,0:T(8,128)(2,1)S(1)}, u32[]{:S(2)}, u32[]{:S(2)}) collective-permute-start(bf16[1408,128]{1,0:T(8,128)(2,1)} %get-tuple-element.33), channel_id=1, source_target_pairs={{0,6},{2,0},{4,2},{6,4},{1,7},{3,1},{5,3},{7,5},{8,14},{10,8},{12,... | collective-permute-start | bytes 1081352 | tf_op jit(solution)/shard_map/ppermute | solution.py:236
  12.3 19.1 %collective-permute-start.2 = (bf16[1408,128]{1,0:T(8,128)(2,1)}, bf16[1408,128]{1,0:T(8,128)(2,1)S(1)}, u32[]{:S(2)}, u32[]{:S(2)}) collective-permute-start(bf16[1408,128]{1,0:T(8,128)(2,1)} %get-tuple-element.33), channel_id=1, source_target_pairs={{0,2},{2,4},{4,6},{6,0},{1,3},{3,5},{5,7},{7,1},{8,10},{10,12},{12... | collective-permute-start | bytes 1081352 | tf_op jit(solution)/shard_map/ppermute | solution.py:236
  14.3 17.2 %collective-permute-start = (bf16[1024,128]{1,0:T(8,128)(2,1)S(1)}, bf16[1024,128]{1,0:T(8,128)(2,1)S(1)}, u32[]{:S(2)}, u32[]{:S(2)}) collective-permute-start(bf16[1024,128]{1,0:T(8,128)(2,1)S(1)} %copy-done.10), channel_id=1, source_target_pairs={{0,2},{2,4},{4,6},{6,0},{1,3},{3,5},{5,7},{7,1},{8,10},{10,12},{12... | collective-permute-start | bytes 786440 | tf_op jit(solution)/shard_map/ppermute | solution.py:236
  17.0 14.5 %collective-permute-start.1 = (bf16[1024,128]{1,0:T(8,128)(2,1)S(1)}, bf16[1024,128]{1,0:T(8,128)(2,1)S(1)}, u32[]{:S(2)}, u32[]{:S(2)}) collective-permute-start(bf16[1024,128]{1,0:T(8,128)(2,1)S(1)} %copy-done.10), channel_id=1, source_target_pairs={{0,6},{2,0},{4,2},{6,4},{1,7},{3,1},{5,3},{7,5},{8,14},{10,8},{12,... | collective-permute-start | bytes 786440 | tf_op jit(solution)/shard_map/ppermute | solution.py:236
  31.5 14.4 %copy-start.2 = (bf16[8,256,128]{2,1,0:T(8,128)(2,1)}, bf16[8,256,128]{2,1,0:T(8,128)(2,1)S(1)}, u32[]{:S(2)}) copy-start(bf16[8,256,128]{2,1,0:T(8,128)(2,1)S(1)} %all-to-all-done.given) | copy-start | bytes 1572868
  31.5 13.2 %collective-permute-start.5 = (bf16[1408,128]{1,0:T(8,128)(2,1)S(1)}, bf16[1408,128]{1,0:T(8,128)(2,1)S(1)}, u32[]{:S(2)}, u32[]{:S(2)}) collective-permute-start(bf16[1408,128]{1,0:T(8,128)(2,1)S(1)} %collective-permute-done.3), channel_id=1, source_target_pairs={{0,6},{2,0},{4,2},{6,4},{1,7},{3,1},{5,3},{7,5},{8,14},{10,8},{12,... | collective-permute-start | bytes 1081352 | tf_op jit(solution)/shard_map/ppermute | solution.py:236
  33.8 10.9 %collective-permute-start.4 = (bf16[1024,128]{1,0:T(8,128)(2,1)S(1)}, bf16[1024,128]{1,0:T(8,128)(2,1)S(1)}, u32[]{:S(2)}, u32[]{:S(2)}) collective-permute-start(bf16[1024,128]{1,0:T(8,128)(2,1)S(1)} %collective-permute-done), channel_id=1, source_target_pairs={{0,2},{2,4},{4,6},{6,0},{1,3},{3,5},{5,7},{7,1},{8,10},{10,12},{12... | collective-permute-start | bytes 786440 | tf_op jit(solution)/shard_map/ppermute | solution.py:236
  45.9 11.5 %collective-permute-start.7 = (bf16[4,1408,128]{2,1,0:T(8,128)(2,1)S(1)}, bf16[4,1408,128]{2,1,0:T(8,128)(2,1)}, u32[]{:S(2)}, u32[]{:S(2)}) collective-permute-start(bf16[4,1408,128]{2,1,0:T(8,128)(2,1)S(1)} %pad_maximum_fusion.1.near), channel_id=1, source_target_pairs={{0,1},{1,0},{2,3},{3,2},{4,5},{5,4},{6,7},{7,6},{8,9},{9,8},{10,11... | collective-permute-start | bytes 4325384 | tf_op jit(solution)/shard_map/ppermute | solution.py:240
  48.0 5.1 %collective-permute-start.6 = (bf16[4,1024,128]{2,1,0:T(8,128)(2,1)S(1)}, bf16[4,1024,128]{2,1,0:T(8,128)(2,1)S(1)}, u32[]{:S(2)}, u32[]{:S(2)}) collective-permute-start(bf16[4,1024,128]{2,1,0:T(8,128)(2,1)S(1)} %pad_maximum_fusion.2.near), channel_id=1, source_target_pairs={{0,1},{1,0},{2,3},{3,2},{4,5},{5,4},{6,7},{7,6},{8,9},{9,8},{10,11... | collective-permute-start | bytes 3145736 | tf_op jit(solution)/shard_map/ppermute | solution.py:240
  72.8 24.6 %collective-permute-start.10 = (bf16[2,112,1536]{2,1,0:T(8,128)(2,1)}, bf16[2,112,1536]{2,1,0:T(8,128)(2,1)S(1)}, u32[]{:S(2)}, u32[]{:S(2)}) collective-permute-start(bf16[2,112,1536]{2,1,0:T(8,128)(2,1)} %pack.1), channel_id=1, source_target_pairs={{0,6},{2,0},{4,2},{6,4},{1,7},{3,1},{5,3},{7,5},{8,14},{10,8},{12,... | collective-permute-start | bytes 2064392 | tf_op jit(solution)/shard_map/ppermute | solution.py:236
  75.8 25.8 %collective-permute-start.9 = (bf16[2,112,1536]{2,1,0:T(8,128)(2,1)}, bf16[2,112,1536]{2,1,0:T(8,128)(2,1)S(1)}, u32[]{:S(2)}, u32[]{:S(2)}) collective-permute-start(bf16[2,112,1536]{2,1,0:T(8,128)(2,1)} %pack.1), channel_id=1, source_target_pairs={{0,2},{2,4},{4,6},{6,0},{1,3},{3,5},{5,7},{7,1},{8,10},{10,12},{12... | collective-permute-start | bytes 2064392 | tf_op jit(solution)/shard_map/ppermute | solution.py:236
  80.7 29.1 %all-to-all-start.2 = ((f32[64,2,384]{2,1,0:T(2,128)}), f32[64,2,384]{2,1,0:T(2,128)S(1)}, u32[]{:S(2)}, u32[]{:S(2)}) async-start(f32[64,2,384]{2,1,0:T(2,128)} %spread.1), calls=%async_computation.2 | async-start | bytes 393216 | tf_op jit(solution)/shard_map/all_to_all | solution.py:292
  97.3 18.0 %copy-start.5 = (bf16[2,112,1536]{2,1,0:T(8,128)(2,1)}, bf16[2,112,1536]{2,1,0:T(8,128)(2,1)S(1)}, u32[]{:S(2)}) copy-start(bf16[2,112,1536]{2,1,0:T(8,128)(2,1)S(1)} %collective-permute-done.10) | copy-start | bytes 2064388
  97.4 22.3 %collective-permute-start.12 = (bf16[112,1536]{1,0:T(8,128)(2,1)S(1)}, bf16[112,1536]{1,0:T(8,128)(2,1)S(1)}, u32[]{:S(2)}, u32[]{:S(2)}) collective-permute-start(bf16[112,1536]{1,0:T(8,128)(2,1)S(1)} %slice_bitcast_fusion), channel_id=1, source_target_pairs={{0,6},{2,0},{4,2},{6,4},{1,7},{3,1},{5,3},{7,5},{8,14},{10,8},{12,... | collective-permute-start | bytes 1032200 | tf_op jit(solution)/shard_map/ppermute | solution.py:236
  101.7 13.7 %copy-start.7 = (bf16[2,112,1536]{2,1,0:T(8,128)(2,1)}, bf16[2,112,1536]{2,1,0:T(8,128)(2,1)S(1)}, u32[]{:S(2)}) copy-start(bf16[2,112,1536]{2,1,0:T(8,128)(2,1)S(1)} %collective-permute-done.9) | copy-start | bytes 2064388
  101.7 18.0 %collective-permute-start.11 = (bf16[112,1536]{1,0:T(8,128)(2,1)S(1)}, bf16[112,1536]{1,0:T(8,128)(2,1)S(1)}, u32[]{:S(2)}, u32[]{:S(2)}) collective-permute-start(bf16[112,1536]{1,0:T(8,128)(2,1)S(1)} %slice_bitcast_fusion.1), channel_id=1, source_target_pairs={{0,2},{2,4},{4,6},{6,0},{1,3},{3,5},{5,7},{7,1},{8,10},{10,12},{12... | collective-permute-start | bytes 1032200 | tf_op jit(solution)/shard_map/ppermute | solution.py:236
  115.3 16.4 %all-to-all-start.3 = ((bf16[8,112,384]{2,1,0:T(8,128)(2,1)}), bf16[8,112,384]{2,1,0:T(8,128)(2,1)}, u32[]{:S(2)}, u32[]{:S(2)}) async-start(bf16[8,112,384]{2,1,0:T(8,128)(2,1)} %get-tuple-element.53), calls=%async_computation.3 | async-start | bytes 1376256 | tf_op jit(solution)/shard_map/all_to_all | solution.py:305
  121.4 10.4 %collective-permute-start.13 = (bf16[4,2,112,1536]{3,2,1,0:T(8,128)(2,1)S(1)}, bf16[4,2,112,1536]{3,2,1,0:T(8,128)(2,1)}, u32[]{:S(2)}, u32[]{:S(2)}) collective-permute-start(bf16[4,2,112,1536]{3,2,1,0:T(8,128)(2,1)S(1)} %pad_maximum_fusion.near), channel_id=1, source_target_pairs={{0,1},{1,0},{2,3},{3,2},{4,5},{5,4},{6,7},{7,6},{8,9},{9,8},{10,11... | collective-permute-start | bytes 8257544 | tf_op jit(solution)/shard_map/ppermute | solution.py:240
  126.9 9.8 %collective-permute-start.8 = (f32[4,112,128]{2,1,0:T(8,128)}, f32[4,112,128]{2,1,0:T(8,128)S(1)}, u32[]{:S(2)}, u32[]{:S(2)}) collective-permute-start(f32[4,112,128]{2,1,0:T(8,128)} %get-tuple-element.50), channel_id=1, source_target_pairs={{0,1},{1,0},{2,3},{3,2},{4,5},{5,4},{6,7},{7,6},{8,9},{9,8},{10,11... | collective-permute-start | bytes 688136 | tf_op jit(solution)/shard_map/ppermute | solution.py:240
  136.7 28.8 %all-to-all-start.4 = ((bf16[64,40,128]{2,1,0:T(8,128)(2,1)}), bf16[64,40,128]{2,1,0:T(8,128)(2,1)S(1)}, u32[]{:S(2)}, u32[]{:S(2)}) async-start(bf16[64,40,128]{2,1,0:T(8,128)(2,1)} %weight.1), calls=%async_computation.4 | async-start | bytes 1310720 | tf_op jit(solution)/shard_map/all_to_all | solution.py:315
  145.6 9.0 %collective-permute-start.14 = (f32[2,112,128]{2,1,0:T(8,128)}, f32[2,112,128]{2,1,0:T(8,128)S(1)}, u32[]{:S(2)}, u32[]{:S(2)}) collective-permute-start(f32[2,112,128]{2,1,0:T(8,128)} %get-tuple-element.57), channel_id=1, source_target_pairs={{0,2},{2,4},{4,6},{6,0},{1,3},{3,5},{5,7},{7,1},{8,10},{10,12},{12... | collective-permute-start | bytes 344072 | tf_op jit(solution)/shard_map/ppermute | solution.py:236
  148.0 9.7 %collective-permute-start.15 = (f32[2,112,128]{2,1,0:T(8,128)}, f32[2,112,128]{2,1,0:T(8,128)S(1)}, u32[]{:S(2)}, u32[]{:S(2)}) collective-permute-start(f32[2,112,128]{2,1,0:T(8,128)} %get-tuple-element.58), channel_id=1, source_target_pairs={{0,6},{2,0},{4,2},{6,4},{1,7},{3,1},{5,3},{7,5},{8,14},{10,8},{12,... | collective-permute-start | bytes 344072 | tf_op jit(solution)/shard_map/ppermute | solution.py:236
  152.6 8.4 %collective-permute-start.16 = (f32[2,112,128]{2,1,0:T(8,128)}, f32[2,112,128]{2,1,0:T(8,128)S(1)}, u32[]{:S(2)}, u32[]{:S(2)}) collective-permute-start(f32[2,112,128]{2,1,0:T(8,128)} %get-tuple-element.59), channel_id=1, source_target_pairs={{0,4},{2,6},{4,0},{6,2},{1,5},{3,7},{5,1},{7,3},{8,12},{10,14},{12... | collective-permute-start | bytes 344072 | tf_op jit(solution)/shard_map/ppermute | solution.py:236
  (13 other events, 61.7 us)

commit v5 on v4

--- a/solution.py
+++ b/solution.py
@@ -23,6 +23,7 @@
 TENSOR = ("x", "core")
 OFFS = (0, 3, 1, 2)
 PACK = 10**8
+FIRST = 2 * 10**10
 BACK = 3 * 10**10
 TOKEN = 3 * 10**10
 
@@ -274,7 +275,7 @@
 
     tokhid, slope1 = call(
         first_body, "first", [((OWN, 2 * D), BF), ((OWN, D), F32)], [idx, given, near1, far1],
-        smem=(0,), scratch=[pltpu.VMEM((OWN, D), F32)], flops=3 * 10**8,
+        smem=(0,), scratch=[pltpu.VMEM((OWN, D), F32)], flops=FIRST,
     )
     hidden2, slope2, me, sums, head = call(
         second_body, "second",
@@ -286,14 +287,12 @@
     sums = lax.all_to_all(sums, TENSOR, 0, 0, tiled=True)
     (spread,) = call(spread_body, "spread", [((64, 2, COLS), F32)], [sums])
     (xh,) = call(
-        pack_body, "pack", [((2, OWN, HALF), BF)], [tokhid, hidden2, sums], loose=(2,),
+        pack_body, "pack", [((2, OWN, HALF), BF)], [tokhid, hidden2, spread], loose=(2,),
         flops=PACK,
     )
     sums = lax.all_to_all(spread, SPACE, 0, 0, tiled=True)
 
-    xh_m1, xh_p1 = shift(xh, 1), shift(xh, 3)
-    xh_last = jnp.stack([shift(xh_m1[0], 1), shift(xh_p1[1], 3)])
-    xhn = jnp.stack([xh, xh_m1, xh_p1, xh_last])
+    xhn = jnp.stack([xh, shift(xh, 1), shift(xh, 3), shift(xh, 2)])
     xhf = flip(xhn)
 
     joined, grad1, loss = call(

time: 168 us -> 181 us (1.077)
  waiting for transfers between devices: 34.9 us -> 42.1 us
  starting transfers between devices: 81.8 us -> 85.6 us
    ppermute x13 -> x12, waiting for transfers between devices: 23.9 us -> 38.5 us  [shift(): return lax.ppermute(v, 'x', [(i, (i + by) % 4) for i in range(4)])]
    all_to_all x1, starting transfers between devices: 6.96 us -> 12.7 us  [per_device(): out = lax.all_to_all(out, SPACE, 0, 0, tiled=True)]
    all_to_all x1, waiting for transfers between devices: 6.16 us -> 1.46 us  [per_device(): sums = lax.all_to_all(spread, SPACE, 0, 0, tiled=True)]
    all_to_all x1, waiting for transfers between devices: 2.86 us -> 0.01 us  [per_device(): joined = lax.all_to_all(joined, TENSOR, 0, 0, tiled=True)]
    ppermute x13 -> x12, starting transfers between devices: 40.9 us -> 38.9 us  [shift(): return lax.ppermute(v, 'x', [(i, (i + by) % 4) for i in range(4)])]
    unnamed x32 -> x34, local copies, waits for them, and re-layouts: 3.52 us -> 4 us
  transfers between devices with their start and end apart: 21 -> 20, of which waited for: 7 -> 9; matrix products, arithmetic and copies ran while one was open for 2% -> 3% of each run, Pallas kernels for 13% -> 12%
where the time goes in v5:
time: 181 us; the launch traced here: 180 us
  starting transfers between devices  85.6 us (47%)
  waiting for transfers between devices  42.1 us (23%)
  Pallas kernels  29.9 us (17%)
  blocking collectives  9.34 us (5%)
  local copies, waits for them, and re-layouts  5.95 us (3%)
  other arithmetic  5.08 us (3%)
    ppermute x12, starting transfers between devices, shift(): return lax.ppermute(v, 'x', [(i, (i + by) % 4) for i in range(4)])  38.9 us
    ppermute x12, waiting for transfers between devices, shift(): return lax.ppermute(v, 'x', [(i, (i + by) % 4) for i in range(4)])  38.5 us
    pallas_call x10, Pallas kernels, call(): pl.pallas_call(body, name=name, out_shape=tuple((jax.ShapeDtypeStruct(s,...  29.9 us
    all_to_all x1, starting transfers between devices, per_device(): sums = lax.all_to_all(spread, SPACE, 0, 0, tiled=True)  16.6 us
    all_to_all x1, starting transfers between devices, per_device(): out = lax.all_to_all(out, SPACE, 0, 0, tiled=True)  12.7 us
    all_to_all x1, blocking collectives, per_device(): sums = lax.all_to_all(sums, TENSOR, 0, 0, tiled=True)  9.34 us
    ppermute x4, starting transfers between devices, flip(): return lax.ppermute(v, 'core', [(0, 1), (1, 0)])  8.64 us
    all_to_all x1, starting transfers between devices, per_device(): given = lax.all_to_all(given, TENSOR, 0, 0, tiled=True)  4.43 us
  transfers between devices with their start and end apart: 20, of which 9 were waited for; matrix products, arithmetic and copies ran while one was open for 3% of the time, Pallas kernels for 12%

profile of v5, /device:TPU:8, one launch (start us, length us, event | category | flops | bytes accessed | tf_op | source)
XLA Modules:
  0.0 179.6 jit_solution(13870603949458519287)
XLA Ops:
  2.9 4.4 %all-to-all-start = ((bf16[8,256,128]{2,1,0:T(8,128)(2,1)}), bf16[8,256,128]{2,1,0:T(8,128)(2,1)S(1)}, u32[]{:S(2)}, u32[]{:S(2)}) async-start(bf16[8,256,128]{2,1,0:T(8,128)(2,1)} %get-tuple-element.34), calls=%async_computation | async-start | bytes 1048576 | tf_op jit(solution)/shard_map/all_to_all | solution.py:256
  7.3 5.1 %collective-permute-start.3 = (bf16[1408,128]{1,0:T(8,128)(2,1)}, bf16[1408,128]{1,0:T(8,128)(2,1)S(1)}, u32[]{:S(2)}, u32[]{:S(2)}) collective-permute-start(bf16[1408,128]{1,0:T(8,128)(2,1)} %get-tuple-element.33), channel_id=1, source_target_pairs={{0,6},{2,0},{4,2},{6,4},{1,7},{3,1},{5,3},{7,5},{8,14},{10,8},{12,... | collective-permute-start | bytes 1081352 | tf_op jit(solution)/shard_map/ppermute | solution.py:237
  14.4 2.7 %collective-permute-start = (bf16[1024,128]{1,0:T(8,128)(2,1)S(1)}, bf16[1024,128]{1,0:T(8,128)(2,1)S(1)}, u32[]{:S(2)}, u32[]{:S(2)}) collective-permute-start(bf16[1024,128]{1,0:T(8,128)(2,1)S(1)} %copy-done.10), channel_id=1, source_target_pairs={{0,2},{2,4},{4,6},{6,0},{1,3},{3,5},{5,7},{7,1},{8,10},{10,12},{12... | collective-permute-start | bytes 786440 | tf_op jit(solution)/shard_map/ppermute | solution.py:237
  17.1 4.3 %collective-permute-start.1 = (bf16[1024,128]{1,0:T(8,128)(2,1)S(1)}, bf16[1024,128]{1,0:T(8,128)(2,1)S(1)}, u32[]{:S(2)}, u32[]{:S(2)}) collective-permute-start(bf16[1024,128]{1,0:T(8,128)(2,1)S(1)} %copy-done.10), channel_id=1, source_target_pairs={{0,6},{2,0},{4,2},{6,4},{1,7},{3,1},{5,3},{7,5},{8,14},{10,8},{12,... | collective-permute-start | bytes 786440 | tf_op jit(solution)/shard_map/ppermute | solution.py:237
  21.5 10.1 %collective-permute-done = bf16[1024,128]{1,0:T(8,128)(2,1)S(1)} collective-permute-done((bf16[1024,128]{1,0:T(8,128)(2,1)S(1)}, bf16[1024,128]{1,0:T(8,128)(2,1)S(1)}, u32[]{:S(2)}, u32[]{:S(2)}) %collective-permute-start) | collective-permute-done | bytes 262176 | tf_op jit(solution)/shard_map/ppermute | solution.py:237
  34.0 3.5 %collective-permute-start.4 = (bf16[1024,128]{1,0:T(8,128)(2,1)S(1)}, bf16[1024,128]{1,0:T(8,128)(2,1)S(1)}, u32[]{:S(2)}, u32[]{:S(2)}) collective-permute-start(bf16[1024,128]{1,0:T(8,128)(2,1)S(1)} %collective-permute-done), channel_id=1, source_target_pairs={{0,2},{2,4},{4,6},{6,0},{1,3},{3,5},{5,7},{7,1},{8,10},{10,12},{12... | collective-permute-start | bytes 786440 | tf_op jit(solution)/shard_map/ppermute | solution.py:237
  37.5 7.3 %collective-permute-done.4 = bf16[1024,128]{1,0:T(8,128)(2,1)S(1)} collective-permute-done((bf16[1024,128]{1,0:T(8,128)(2,1)S(1)}, bf16[1024,128]{1,0:T(8,128)(2,1)S(1)}, u32[]{:S(2)}, u32[]{:S(2)}) %collective-permute-start.4) | collective-permute-done | bytes 262176 | tf_op jit(solution)/shard_map/ppermute | solution.py:237
  50.9 2.4 %collective-permute-start.7 = (bf16[4,1408,128]{2,1,0:T(8,128)(2,1)S(1)}, bf16[4,1408,128]{2,1,0:T(8,128)(2,1)S(1)}, u32[]{:S(2)}, u32[]{:S(2)}) collective-permute-start(bf16[4,1408,128]{2,1,0:T(8,128)(2,1)S(1)} %pad_maximum_fusion.1.near), channel_id=1, source_target_pairs={{0,1},{1,0},{2,3},{3,2},{4,5},{5,4},{6,7},{7,6},{8,9},{9,8},{10,11... | collective-permute-start | bytes 4325384 | tf_op jit(solution)/shard_map/ppermute | solution.py:241
  53.3 3.3 %first.1 = (bf16[112,2048]{1,0:T(8,128)(2,1)}, f32[112,1024]{1,0:T(8,128)}) custom-call(s32[10]{0:T(128)} %stack.88.idx, bf16[8,256,128]{2,1,0:T(8,128)(2,1)} %copy-done.3, bf16[4,1024,128]{2,1,0:T(8,128)(2,1)} %copy-done.5, bf16[4,1024,128]{2,1,0:T(8,128)(2,1)} %collective-permute-done.6.far), custom_call_target="tpu_custom_call" | custom-call | flops 20000000000 | bytes 4194304 | tf_op jit(solution)/shard_map/first/pallas_call | solution.py:46
  57.7 4.1 %second.3 = (bf16[112,1024]{1,0:T(8,128)(2,1)}, f32[112,1024]{1,0:T(8,128)}, f32[112,384]{1,0:T(8,128)}, f32[8,2,384]{2,1,0:T(2,128)}, bf16[384,1024]{1,0:T(8,128)(2,1)}) custom-call(s32[10]{0:T(128)} %stack.88.idx, bf16[112,2048]{1,0:T(8,128)(2,1)} %get-tuple-element.40.tokhid, bf16[8,256,128]{2,1,0:T(8,128)(2,1)} %copy-done.3, ...), custom_call_target="tpu_custom_call" | custom-call | flops 500000000 | bytes 4194304 | tf_op jit(solution)/shard_map/second/pallas_call | solution.py:46
  61.8 9.3 %all_to_all.25.came = f32[8,2,384]{2,1,0:T(2,128)} all-to-all(f32[8,2,384]{2,1,0:T(2,128)} %get-tuple-element.43), channel_id=1, replica_groups=mesh['z'=8,'y'=8,'x'=4,'core'=2] {'x','core'}, dimensions={0} | all-to-all | bytes 49152 | tf_op jit(solution)/shard_map/all_to_all | solution.py:287
  72.7 16.6 %all-to-all-start.2 = ((f32[64,2,384]{2,1,0:T(2,128)}), f32[64,2,384]{2,1,0:T(2,128)S(1)}, u32[]{:S(2)}, u32[]{:S(2)}) async-start(f32[64,2,384]{2,1,0:T(2,128)} %spread.1.came), calls=%async_computation.2 | async-start | bytes 393216 | tf_op jit(solution)/shard_map/all_to_all | solution.py:293
  91.9 3.0 %collective-permute-start.11 = (bf16[2,112,1536]{2,1,0:T(8,128)(2,1)}, bf16[2,112,1536]{2,1,0:T(8,128)(2,1)S(1)}, u32[]{:S(2)}, u32[]{:S(2)}) collective-permute-start(bf16[2,112,1536]{2,1,0:T(8,128)(2,1)} %pack.1), channel_id=1, source_target_pairs={{0,4},{2,6},{4,0},{6,2},{1,5},{3,7},{5,1},{7,3},{8,12},{10,14},{12... | collective-permute-start | bytes 2064392 | tf_op jit(solution)/shard_map/ppermute | solution.py:237
  94.9 4.0 %collective-permute-start.10 = (bf16[2,112,1536]{2,1,0:T(8,128)(2,1)}, bf16[2,112,1536]{2,1,0:T(8,128)(2,1)S(1)}, u32[]{:S(2)}, u32[]{:S(2)}) collective-permute-start(bf16[2,112,1536]{2,1,0:T(8,128)(2,1)} %pack.1), channel_id=1, source_target_pairs={{0,6},{2,0},{4,2},{6,4},{1,7},{3,1},{5,3},{7,5},{8,14},{10,8},{12,... | collective-permute-start | bytes 2064392 | tf_op jit(solution)/shard_map/ppermute | solution.py:237
  103.0 4.8 %backward.1 = (bf16[8,112,384]{2,1,0:T(8,128)(2,1)}, bf16[112,1024]{1,0:T(8,128)(2,1)}, f32[1,1]{1,0:T(1,128)}) custom-call(s32[10]{0:T(128)} %stack.88.idx, f32[1]{0:T(128)} %bitcast.26.scale, f32[64,2,384]{2,1,0:T(2,128)} %copy-done.13, f32[112,384]{1,0:T(8,128)} %get-tuple-element.44.me, f32[112,1024]{1,0:T(8,128)} %get-tuple-element.45.slope1, ...), custom_call_target="tpu_custom_call" | custom-call | flops 30000001024 | bytes 4194304 | tf_op jit(solution)/shard_map/backward/pallas_call | solution.py:46
  107.9 4.3 %all-to-all-start.3 = ((bf16[8,112,384]{2,1,0:T(8,128)(2,1)}), bf16[8,112,384]{2,1,0:T(8,128)(2,1)}, u32[]{:S(2)}, u32[]{:S(2)}) async-start(bf16[8,112,384]{2,1,0:T(8,128)(2,1)} %get-tuple-element.53), calls=%async_computation.3 | async-start | bytes 1376256 | tf_op jit(solution)/shard_map/all_to_all | solution.py:304
  113.9 13.2 %collective-permute-done.10 = bf16[2,112,1536]{2,1,0:T(8,128)(2,1)S(1)} collective-permute-done((bf16[2,112,1536]{2,1,0:T(8,128)(2,1)}, bf16[2,112,1536]{2,1,0:T(8,128)(2,1)S(1)}, u32[]{:S(2)}, u32[]{:S(2)}) %collective-permute-start.10) | collective-permute-done | bytes 688160 | tf_op jit(solution)/shard_map/ppermute | solution.py:237
  132.3 3.2 %token_.1 = (f32[4,112,128]{2,1,0:T(8,128)}, f32[4,112,128]{2,1,0:T(8,128)}) custom-call(s32[10]{0:T(128)} %stack.88.idx, bf16[112,1024]{1,0:T(8,128)(2,1)} %get-tuple-element.49.grad1, bf16[4,1024,128]{2,1,0:T(8,128)(2,1)} %copy-done.5, bf16[4,1024,128]{2,1,0:T(8,128)(2,1)} %collective-permute-done.6.far), custom_call_target="tpu_custom_call" | custom-call | flops 30000001024 | bytes 4194304 | tf_op jit(solution)/shard_map/token/pallas_call | solution.py:46
  137.9 4.9 %weight.1 = bf16[64,40,128]{2,1,0:T(8,128)(2,1)} custom-call(s32[10]{0:T(128)} %stack.88.idx, bf16[4,2,112,1536]{3,2,1,0:T(8,128)(2,1)} %copy-done, bf16[4,2,112,1536]{3,2,1,0:T(8,128)(2,1)} %collective-permute-done.12.far, bf16[8,112,384]{2,1,0:T(8,128)(2,1)} %all-to-all-done.3.joined), custom_call_target="tpu_custom_call" | custom-call | flops 800000000 | bytes 4194304 | tf_op jit(solution)/shard_map/weight/pallas_call | solution.py:46
  143.5 12.7 %all-to-all-start.4 = ((bf16[64,40,128]{2,1,0:T(8,128)(2,1)}), bf16[64,40,128]{2,1,0:T(8,128)(2,1)S(1)}, u32[]{:S(2)}, u32[]{:S(2)}) async-start(bf16[64,40,128]{2,1,0:T(8,128)(2,1)} %weight.1), calls=%async_computation.4 | async-start | bytes 1310720 | tf_op jit(solution)/shard_map/all_to_all | solution.py:314
  158.1 2.7 %collective-permute-start.13 = (f32[2,112,128]{2,1,0:T(8,128)}, f32[2,112,128]{2,1,0:T(8,128)S(1)}, u32[]{:S(2)}, u32[]{:S(2)}) collective-permute-start(f32[2,112,128]{2,1,0:T(8,128)} %get-tuple-element.57), channel_id=1, source_target_pairs={{0,2},{2,4},{4,6},{6,0},{1,3},{3,5},{5,7},{7,1},{8,10},{10,12},{12... | collective-permute-start | bytes 344072 | tf_op jit(solution)/shard_map/ppermute | solution.py:237
  160.9 4.3 %collective-permute-start.14 = (f32[2,112,128]{2,1,0:T(8,128)}, f32[2,112,128]{2,1,0:T(8,128)S(1)}, u32[]{:S(2)}, u32[]{:S(2)}) collective-permute-start(f32[2,112,128]{2,1,0:T(8,128)} %get-tuple-element.58), channel_id=1, source_target_pairs={{0,6},{2,0},{4,2},{6,4},{1,7},{3,1},{5,3},{7,5},{8,14},{10,8},{12,... | collective-permute-start | bytes 344072 | tf_op jit(solution)/shard_map/ppermute | solution.py:237
  165.2 3.0 %collective-permute-start.15 = (f32[2,112,128]{2,1,0:T(8,128)}, f32[2,112,128]{2,1,0:T(8,128)S(1)}, u32[]{:S(2)}, u32[]{:S(2)}) collective-permute-start(f32[2,112,128]{2,1,0:T(8,128)} %get-tuple-element.59), channel_id=1, source_target_pairs={{0,4},{2,6},{4,0},{6,2},{1,5},{3,7},{5,1},{7,3},{8,12},{10,14},{12... | collective-permute-start | bytes 344072 | tf_op jit(solution)/shard_map/ppermute | solution.py:237
  169.0 4.5 %collective-permute-done.15.across = f32[2,112,128]{2,1,0:T(8,128)S(1)} collective-permute-done((f32[2,112,128]{2,1,0:T(8,128)}, f32[2,112,128]{2,1,0:T(8,128)S(1)}, u32[]{:S(2)}, u32[]{:S(2)}) %collective-permute-start.15) | collective-permute-done | bytes 114720 | tf_op jit(solution)/shard_map/ppermute | solution.py:237
  (72 shorter events, 39.8 us)
Async XLA Ops:
  2.9 47.7 %copy-start.9 = (bf16[1408,128]{1,0:T(8,128)(2,1)S(1)}, bf16[1408,128]{1,0:T(8,128)(2,1)}, u32[]{:S(2)}) copy-start(bf16[1408,128]{1,0:T(8,128)(2,1)} %get-tuple-element.33) | copy-start | bytes 1081348
  2.9 28.7 %all-to-all-start = ((bf16[8,256,128]{2,1,0:T(8,128)(2,1)}), bf16[8,256,128]{2,1,0:T(8,128)(2,1)S(1)}, u32[]{:S(2)}, u32[]{:S(2)}) async-start(bf16[8,256,128]{2,1,0:T(8,128)(2,1)} %get-tuple-element.34), calls=%async_computation | async-start | bytes 1048576 | tf_op jit(solution)/shard_map/all_to_all | solution.py:256
  7.3 24.3 %collective-permute-start.3 = (bf16[1408,128]{1,0:T(8,128)(2,1)}, bf16[1408,128]{1,0:T(8,128)(2,1)S(1)}, u32[]{:S(2)}, u32[]{:S(2)}) collective-permute-start(bf16[1408,128]{1,0:T(8,128)(2,1)} %get-tuple-element.33), channel_id=1, source_target_pairs={{0,6},{2,0},{4,2},{6,4},{1,7},{3,1},{5,3},{7,5},{8,14},{10,8},{12,... | collective-permute-start | bytes 1081352 | tf_op jit(solution)/shard_map/ppermute | solution.py:237
  12.5 19.1 %collective-permute-start.2 = (bf16[1408,128]{1,0:T(8,128)(2,1)}, bf16[1408,128]{1,0:T(8,128)(2,1)S(1)}, u32[]{:S(2)}, u32[]{:S(2)}) collective-permute-start(bf16[1408,128]{1,0:T(8,128)(2,1)} %get-tuple-element.33), channel_id=1, source_target_pairs={{0,2},{2,4},{4,6},{6,0},{1,3},{3,5},{5,7},{7,1},{8,10},{10,12},{12... | collective-permute-start | bytes 1081352 | tf_op jit(solution)/shard_map/ppermute | solution.py:237
  14.4 17.2 %collective-permute-start = (bf16[1024,128]{1,0:T(8,128)(2,1)S(1)}, bf16[1024,128]{1,0:T(8,128)(2,1)S(1)}, u32[]{:S(2)}, u32[]{:S(2)}) collective-permute-start(bf16[1024,128]{1,0:T(8,128)(2,1)S(1)} %copy-done.10), channel_id=1, source_target_pairs={{0,2},{2,4},{4,6},{6,0},{1,3},{3,5},{5,7},{7,1},{8,10},{10,12},{12... | collective-permute-start | bytes 786440 | tf_op jit(solution)/shard_map/ppermute | solution.py:237
  17.1 14.5 %collective-permute-start.1 = (bf16[1024,128]{1,0:T(8,128)(2,1)S(1)}, bf16[1024,128]{1,0:T(8,128)(2,1)S(1)}, u32[]{:S(2)}, u32[]{:S(2)}) collective-permute-start(bf16[1024,128]{1,0:T(8,128)(2,1)S(1)} %copy-done.10), channel_id=1, source_target_pairs={{0,6},{2,0},{4,2},{6,4},{1,7},{3,1},{5,3},{7,5},{8,14},{10,8},{12,... | collective-permute-start | bytes 786440 | tf_op jit(solution)/shard_map/ppermute | solution.py:237
  31.6 19.2 %copy-start.3 = (bf16[8,256,128]{2,1,0:T(8,128)(2,1)}, bf16[8,256,128]{2,1,0:T(8,128)(2,1)S(1)}, u32[]{:S(2)}) copy-start(bf16[8,256,128]{2,1,0:T(8,128)(2,1)S(1)} %all-to-all-done.given) | copy-start | bytes 1572868
  31.6 13.2 %collective-permute-start.5 = (bf16[1408,128]{1,0:T(8,128)(2,1)S(1)}, bf16[1408,128]{1,0:T(8,128)(2,1)S(1)}, u32[]{:S(2)}, u32[]{:S(2)}) collective-permute-start(bf16[1408,128]{1,0:T(8,128)(2,1)S(1)} %collective-permute-done.3), channel_id=1, source_target_pairs={{0,6},{2,0},{4,2},{6,4},{1,7},{3,1},{5,3},{7,5},{8,14},{10,8},{12,... | collective-permute-start | bytes 1081352 | tf_op jit(solution)/shard_map/ppermute | solution.py:237
  34.0 10.9 %collective-permute-start.4 = (bf16[1024,128]{1,0:T(8,128)(2,1)S(1)}, bf16[1024,128]{1,0:T(8,128)(2,1)S(1)}, u32[]{:S(2)}, u32[]{:S(2)}) collective-permute-start(bf16[1024,128]{1,0:T(8,128)(2,1)S(1)} %collective-permute-done), channel_id=1, source_target_pairs={{0,2},{2,4},{4,6},{6,0},{1,3},{3,5},{5,7},{7,1},{8,10},{10,12},{12... | collective-permute-start | bytes 786440 | tf_op jit(solution)/shard_map/ppermute | solution.py:237
  45.9 7.3 %collective-permute-start.6 = (bf16[4,1024,128]{2,1,0:T(8,128)(2,1)S(1)}, bf16[4,1024,128]{2,1,0:T(8,128)(2,1)}, u32[]{:S(2)}, u32[]{:S(2)}) collective-permute-start(bf16[4,1024,128]{2,1,0:T(8,128)(2,1)S(1)} %pad_maximum_fusion.2.near), channel_id=1, source_target_pairs={{0,1},{1,0},{2,3},{3,2},{4,5},{5,4},{6,7},{7,6},{8,9},{9,8},{10,11... | collective-permute-start | bytes 3145736 | tf_op jit(solution)/shard_map/ppermute | solution.py:241
  50.9 5.7 %collective-permute-start.7 = (bf16[4,1408,128]{2,1,0:T(8,128)(2,1)S(1)}, bf16[4,1408,128]{2,1,0:T(8,128)(2,1)S(1)}, u32[]{:S(2)}, u32[]{:S(2)}) collective-permute-start(bf16[4,1408,128]{2,1,0:T(8,128)(2,1)S(1)} %pad_maximum_fusion.1.near), channel_id=1, source_target_pairs={{0,1},{1,0},{2,3},{3,2},{4,5},{5,4},{6,7},{7,6},{8,9},{9,8},{10,11... | collective-permute-start | bytes 4325384 | tf_op jit(solution)/shard_map/ppermute | solution.py:241
  72.7 29.7 %all-to-all-start.2 = ((f32[64,2,384]{2,1,0:T(2,128)}), f32[64,2,384]{2,1,0:T(2,128)S(1)}, u32[]{:S(2)}, u32[]{:S(2)}) async-start(f32[64,2,384]{2,1,0:T(2,128)} %spread.1.came), calls=%async_computation.2 | async-start | bytes 393216 | tf_op jit(solution)/shard_map/all_to_all | solution.py:293
  91.9 22.0 %collective-permute-start.11 = (bf16[2,112,1536]{2,1,0:T(8,128)(2,1)}, bf16[2,112,1536]{2,1,0:T(8,128)(2,1)S(1)}, u32[]{:S(2)}, u32[]{:S(2)}) collective-permute-start(bf16[2,112,1536]{2,1,0:T(8,128)(2,1)} %pack.1), channel_id=1, source_target_pairs={{0,4},{2,6},{4,0},{6,2},{1,5},{3,7},{5,1},{7,3},{8,12},{10,14},{12... | collective-permute-start | bytes 2064392 | tf_op jit(solution)/shard_map/ppermute | solution.py:237
  94.9 32.2 %collective-permute-start.10 = (bf16[2,112,1536]{2,1,0:T(8,128)(2,1)}, bf16[2,112,1536]{2,1,0:T(8,128)(2,1)S(1)}, u32[]{:S(2)}, u32[]{:S(2)}) collective-permute-start(bf16[2,112,1536]{2,1,0:T(8,128)(2,1)} %pack.1), channel_id=1, source_target_pairs={{0,6},{2,0},{4,2},{6,4},{1,7},{3,1},{5,3},{7,5},{8,14},{10,8},{12,... | collective-permute-start | bytes 2064392 | tf_op jit(solution)/shard_map/ppermute | solution.py:237
  98.9 28.9 %collective-permute-start.9 = (bf16[2,112,1536]{2,1,0:T(8,128)(2,1)}, bf16[2,112,1536]{2,1,0:T(8,128)(2,1)S(1)}, u32[]{:S(2)}, u32[]{:S(2)}) collective-permute-start(bf16[2,112,1536]{2,1,0:T(8,128)(2,1)} %pack.1), channel_id=1, source_target_pairs={{0,2},{2,4},{4,6},{6,0},{1,3},{3,5},{5,7},{7,1},{8,10},{10,12},{12... | collective-permute-start | bytes 2064392 | tf_op jit(solution)/shard_map/ppermute | solution.py:237
  107.9 20.8 %copy-start.2 = (bf16[2,112,1536]{2,1,0:T(8,128)(2,1)S(1)}, bf16[2,112,1536]{2,1,0:T(8,128)(2,1)}, u32[]{:S(2)}) copy-start(bf16[2,112,1536]{2,1,0:T(8,128)(2,1)} %pack.1) | copy-start | bytes 2064388
  107.9 30.0 %all-to-all-start.3 = ((bf16[8,112,384]{2,1,0:T(8,128)(2,1)}), bf16[8,112,384]{2,1,0:T(8,128)(2,1)}, u32[]{:S(2)}, u32[]{:S(2)}) async-start(bf16[8,112,384]{2,1,0:T(8,128)(2,1)} %get-tuple-element.53), calls=%async_computation.3 | async-start | bytes 1376256 | tf_op jit(solution)/shard_map/all_to_all | solution.py:304
  113.9 13.9 %copy-start.6 = (bf16[2,112,1536]{2,1,0:T(8,128)(2,1)}, bf16[2,112,1536]{2,1,0:T(8,128)(2,1)S(1)}, u32[]{:S(2)}) copy-start(bf16[2,112,1536]{2,1,0:T(8,128)(2,1)S(1)} %collective-permute-done.11) | copy-start | bytes 2064388
  130.4 7.5 %collective-permute-start.12 = (bf16[4,2,112,1536]{3,2,1,0:T(8,128)(2,1)S(1)}, bf16[4,2,112,1536]{3,2,1,0:T(8,128)(2,1)}, u32[]{:S(2)}, u32[]{:S(2)}) collective-permute-start(bf16[4,2,112,1536]{3,2,1,0:T(8,128)(2,1)S(1)} %pad_maximum_fusion.near), channel_id=1, source_target_pairs={{0,1},{1,0},{2,3},{3,2},{4,5},{5,4},{6,7},{7,6},{8,9},{9,8},{10,11... | collective-permute-start | bytes 8257544 | tf_op jit(solution)/shard_map/ppermute | solution.py:241
  135.5 7.3 %collective-permute-start.8 = (f32[4,112,128]{2,1,0:T(8,128)}, f32[4,112,128]{2,1,0:T(8,128)S(1)}, u32[]{:S(2)}, u32[]{:S(2)}) collective-permute-start(f32[4,112,128]{2,1,0:T(8,128)} %get-tuple-element.50), channel_id=1, source_target_pairs={{0,1},{1,0},{2,3},{3,2},{4,5},{5,4},{6,7},{7,6},{8,9},{9,8},{10,11... | collective-permute-start | bytes 688136 | tf_op jit(solution)/shard_map/ppermute | solution.py:241
  143.5 34.7 %all-to-all-start.4 = ((bf16[64,40,128]{2,1,0:T(8,128)(2,1)}), bf16[64,40,128]{2,1,0:T(8,128)(2,1)S(1)}, u32[]{:S(2)}, u32[]{:S(2)}) async-start(bf16[64,40,128]{2,1,0:T(8,128)(2,1)} %weight.1), calls=%async_computation.4 | async-start | bytes 1310720 | tf_op jit(solution)/shard_map/all_to_all | solution.py:314
  158.1 10.0 %collective-permute-start.13 = (f32[2,112,128]{2,1,0:T(8,128)}, f32[2,112,128]{2,1,0:T(8,128)S(1)}, u32[]{:S(2)}, u32[]{:S(2)}) collective-permute-start(f32[2,112,128]{2,1,0:T(8,128)} %get-tuple-element.57), channel_id=1, source_target_pairs={{0,2},{2,4},{4,6},{6,0},{1,3},{3,5},{5,7},{7,1},{8,10},{10,12},{12... | collective-permute-start | bytes 344072 | tf_op jit(solution)/shard_map/ppermute | solution.py:237
  160.9 8.2 %collective-permute-start.14 = (f32[2,112,128]{2,1,0:T(8,128)}, f32[2,112,128]{2,1,0:T(8,128)S(1)}, u32[]{:S(2)}, u32[]{:S(2)}) collective-permute-start(f32[2,112,128]{2,1,0:T(8,128)} %get-tuple-element.58), channel_id=1, source_target_pairs={{0,6},{2,0},{4,2},{6,4},{1,7},{3,1},{5,3},{7,5},{8,14},{10,8},{12,... | collective-permute-start | bytes 344072 | tf_op jit(solution)/shard_map/ppermute | solution.py:237
  165.2 8.4 %collective-permute-start.15 = (f32[2,112,128]{2,1,0:T(8,128)}, f32[2,112,128]{2,1,0:T(8,128)S(1)}, u32[]{:S(2)}, u32[]{:S(2)}) collective-permute-start(f32[2,112,128]{2,1,0:T(8,128)} %get-tuple-element.59), channel_id=1, source_target_pairs={{0,4},{2,6},{4,0},{6,2},{1,5},{3,7},{5,1},{7,3},{8,12},{10,14},{12... | collective-permute-start | bytes 344072 | tf_op jit(solution)/shard_map/ppermute | solution.py:237
  (13 other events, 57.6 us)

commit v6 on v4

--- a/solution.py
+++ b/solution.py
@@ -22,7 +22,7 @@
 SPACE = ("z", "y")
 TENSOR = ("x", "core")
 OFFS = (0, 3, 1, 2)
-PACK = 10**8
+FIRST = 2 * 10**10
 BACK = 3 * 10**10
 TOKEN = 3 * 10**10
 
@@ -113,7 +113,7 @@
 
 
 def second_body(
-    idx, tokhid, given, near, far, land, weights, hidden2, slope2, me, sums, head, pre, goal
+    idx, tokhid, given, near, far, land, weights, xh, slope2, me, sums, head, pre, goal
 ):
     for j in range(8):
         parts = [
@@ -127,9 +127,12 @@
                 piece = ref[s, D + HEAD * i : D + HEAD * (i + 1), :]
                 head[rows, 128 * i : 128 * (i + 1)] = piece
     hidden, slope = layer(idx, tokhid[:, D:], (near, far), pre)
-    hidden2[...] = hidden.astype(BF)
+    hidden2 = hidden.astype(BF)
+    xh[0] = tokhid[:, :HALF]
+    xh[1, :, : 2 * D - HALF] = tokhid[:, HALF:]
+    xh[1, :, 2 * D - HALF :] = hidden2
     slope2[...] = slope
-    predicted = dot(hidden2[...], head[...], 1, 1)
+    predicted = dot(hidden2, head[...], 1, 1)
     flipped = goal[...].T
     kind = flipped[OWN : OWN + 1, :]
     column = lax.broadcasted_iota(jnp.int32, (8, COLS), 1)
@@ -142,16 +145,6 @@
     me[...] = product
     pair = [jnp.sum(product * error, axis=0, keepdims=True), jnp.sum(masked, axis=0, keepdims=True)]
     sums[...] = jnp.broadcast_to(jnp.concatenate(pair, axis=0)[None], sums.shape)
-
-
-def spread_body(came, out):
-    out[...] = jnp.broadcast_to(jnp.sum(came[...], axis=0, keepdims=True), out.shape)
-
-
-def pack_body(tokhid, hidden2, came, xh):
-    xh[0] = tokhid[:, :HALF]
-    xh[1, :, : 2 * D - HALF] = tokhid[:, HALF:]
-    xh[1, :, 2 * D - HALF :] = hidden2[...]
 
 
 def over_cells(v):
@@ -248,20 +241,6 @@
     places = [2 * ((x + off) % 4) + c for c in (core, 1 - core) for off in OFFS]
     idx = jnp.stack([*places, core, x]).astype(jnp.int32)
 
-    given, packed = call(
-        prep_body, "prep", [((8, PIECE, 128), BF), ((D + COLS, 128), BF)],
-        [variable_kind, tokens, targets, second_weight, head_weight], smem=(0,),
-    )
-    given = lax.all_to_all(given, TENSOR, 0, 0, tiled=True)
-    w1_m1, w1_p1 = shift(first_weight, 1), shift(first_weight, 3)
-    w2_m1, w2_p1 = shift(packed, 1), shift(packed, 3)
-    w1_m1, w1_p1, w2_m1, w2_p1, given = lax.optimization_barrier((w1_m1, w1_p1, w2_m1, w2_p1, given))
-    w1_last, w2_last = shift(w1_m1, 1), shift(w2_p1, 3)
-    w1_last, w2_last = lax.optimization_barrier((w1_last, w2_last))
-    near1 = jnp.stack([first_weight, w1_m1, w1_p1, w1_last])
-    near2 = jnp.stack([packed, w2_m1, w2_p1, w2_last])
-    far1, far2 = flip(near1), flip(near2)
-
     land = lax.dynamic_slice(land_mask, (0, mine * OWN), (PP, OWN))
     land = jnp.pad(land.astype(BF), ((0, 8 - PP), (0, 128 - OWN)))
     space = lax.axis_index(SPACE)
@@ -272,23 +251,37 @@
     weights = jnp.cos(math.pi / 2.0 * (lat_row.astype(F32) + 0.5) / nlat)
     weights = jnp.where(col % HEAD < 44, weights, 0.0)[None, :]
 
+    given, packed = call(
+        prep_body, "prep", [((8, PIECE, 128), BF), ((D + COLS, 128), BF)],
+        [variable_kind, tokens, targets, second_weight, head_weight], smem=(0,),
+    )
+    given = lax.all_to_all(given, TENSOR, 0, 0, tiled=True)
+    w1_m1, w1_p1 = shift(first_weight, 1), shift(first_weight, 3)
+    w2_m1, w2_p1 = shift(packed, 1), shift(packed, 3)
+    w1_m1, w1_p1, w2_m1, w2_p1, given, idx, land, weights = lax.optimization_barrier(
+        (w1_m1, w1_p1, w2_m1, w2_p1, given, idx, land, weights)
+    )
+    w1_last, w2_last = shift(w1_m1, 1), shift(w2_p1, 3)
+    w1_last, w2_last = lax.optimization_barrier((w1_last, w2_last))
+    near1 = jnp.stack([first_weight, w1_m1, w1_p1, w1_last])
+    near2 = jnp.stack([packed, w2_m1, w2_p1, w2_last])
+    far1, far2 = flip(near1), flip(near2)
+
     tokhid, slope1 = call(
         first_body, "first", [((OWN, 2 * D), BF), ((OWN, D), F32)], [idx, given, near1, far1],
-        smem=(0,), scratch=[pltpu.VMEM((OWN, D), F32)], flops=3 * 10**8,
-    )
-    hidden2, slope2, me, sums, head = call(
+        smem=(0,), scratch=[pltpu.VMEM((OWN, D), F32)], flops=FIRST,
+    )
+    xh, slope2, me, sums, head = call(
         second_body, "second",
-        [((OWN, D), BF), ((OWN, D), F32), ((OWN, COLS), F32), ((8, 2, COLS), F32), ((COLS, D), BF)],
+        [((2, OWN, HALF), BF), ((OWN, D), F32), ((OWN, COLS), F32), ((8, 2, COLS), F32),
+         ((COLS, D), BF)],
         [idx, tokhid, given, near2, far2, land, weights], smem=(0,),
         scratch=[pltpu.VMEM((OWN, D), F32), pltpu.VMEM((COLS, 128), F32)], flops=5 * 10**8,
     )
 
     sums = lax.all_to_all(sums, TENSOR, 0, 0, tiled=True)
-    (spread,) = call(spread_body, "spread", [((64, 2, COLS), F32)], [sums])
-    (xh,) = call(
-        pack_body, "pack", [((2, OWN, HALF), BF)], [tokhid, hidden2, sums], loose=(2,),
-        flops=PACK,
-    )
+    sums, xh = lax.optimization_barrier((sums, xh))
+    spread = jnp.broadcast_to(jnp.sum(sums, axis=0), (64, 2, COLS))
     sums = lax.all_to_all(spread, SPACE, 0, 0, tiled=True)
 
     xh_m1, xh_p1 = shift(xh, 1), shift(xh, 3)

time: 168 us -> 163 us (0.970)
  waiting for transfers between devices: 34.9 us -> 30.8 us
  Pallas kernels: 29.8 us -> 26.6 us
  local copies, waits for them, and re-layouts: 5.44 us -> 8.18 us
    pallas_call x10 -> x8, Pallas kernels: 29.8 us -> 26.6 us  [call(): pl.pallas_call(body, name=name, out_shape=tuple((jax.ShapeDtypeStruct(s,...]
    ppermute x13, waiting for transfers between devices: 23.9 us -> 20.8 us  [shift(): return lax.ppermute(v, 'x', [(i, (i + by) % 4) for i in range(4)])]
    unnamed x32 -> x34, local copies, waits for them, and re-layouts: 3.52 us -> 5.51 us
  transfers between devices with their start and end apart: 21 -> 21, of which waited for: 7 -> 7; matrix products, arithmetic and copies ran while one was open for 2% -> 3% of each run, Pallas kernels for 13% -> 12%
where the time goes in v6:
time: 163 us; the launch traced here: 162 us
  starting transfers between devices  82.1 us (50%)
  waiting for transfers between devices  30.8 us (19%)
  Pallas kernels  26.6 us (16%)
  blocking collectives  8.63 us (5%)
  local copies, waits for them, and re-layouts  8.18 us (5%)
  other arithmetic  3.88 us (2%)
  between operations  1.78 us (1%)
    ppermute x13, starting transfers between devices, shift(): return lax.ppermute(v, 'x', [(i, (i + by) % 4) for i in range(4)])  41.4 us
    pallas_call x8, Pallas kernels, call(): pl.pallas_call(body, name=name, out_shape=tuple((jax.ShapeDtypeStruct(s,...  26.6 us
    ppermute x13, waiting for transfers between devices, shift(): return lax.ppermute(v, 'x', [(i, (i + by) % 4) for i in range(4)])  20.8 us
    all_to_all x1, starting transfers between devices, per_device(): sums = lax.all_to_all(spread, SPACE, 0, 0, tiled=True)  16.6 us
    ppermute x4, starting transfers between devices, flip(): return lax.ppermute(v, 'core', [(0, 1), (1, 0)])  8.65 us
    all_to_all x1, blocking collectives, per_device(): sums = lax.all_to_all(sums, TENSOR, 0, 0, tiled=True)  8.63 us
    all_to_all x1, starting transfers between devices, per_device(): out = lax.all_to_all(out, SPACE, 0, 0, tiled=True)  7.4 us
    all_to_all x1, waiting for transfers between devices, per_device(): sums = lax.all_to_all(spread, SPACE, 0, 0, tiled=True)  6.16 us
  transfers between devices with their start and end apart: 21, of which 7 were waited for; matrix products, arithmetic and copies ran while one was open for 3% of the time, Pallas kernels for 12%

profile of v6, /device:TPU:8, one launch (start us, length us, event | category | flops | bytes accessed | tf_op | source)
XLA Modules:
  0.0 161.9 jit_solution(3315834516597991492)
XLA Ops:
  2.9 4.4 %all-to-all-start = ((bf16[8,256,128]{2,1,0:T(8,128)(2,1)}), bf16[8,256,128]{2,1,0:T(8,128)(2,1)S(1)}, u32[]{:S(2)}, u32[]{:S(2)}) async-start(bf16[8,256,128]{2,1,0:T(8,128)(2,1)} %get-tuple-element.39), calls=%async_computation | async-start | bytes 1048576 | tf_op jit(solution)/shard_map/all_to_all | solution.py:258
  7.3 5.1 %collective-permute-start.3 = (bf16[1408,128]{1,0:T(8,128)(2,1)}, bf16[1408,128]{1,0:T(8,128)(2,1)S(1)}, u32[]{:S(2)}, u32[]{:S(2)}) collective-permute-start(bf16[1408,128]{1,0:T(8,128)(2,1)} %get-tuple-element.38), channel_id=1, source_target_pairs={{0,6},{2,0},{4,2},{6,4},{1,7},{3,1},{5,3},{7,5},{8,14},{10,8},{12,... | collective-permute-start | bytes 1081352 | tf_op jit(solution)/shard_map/ppermute | solution.py:229
  14.4 2.7 %collective-permute-start = (bf16[1024,128]{1,0:T(8,128)(2,1)S(1)}, bf16[1024,128]{1,0:T(8,128)(2,1)S(1)}, u32[]{:S(2)}, u32[]{:S(2)}) collective-permute-start(bf16[1024,128]{1,0:T(8,128)(2,1)S(1)} %copy-done.11), channel_id=1, source_target_pairs={{0,2},{2,4},{4,6},{6,0},{1,3},{3,5},{5,7},{7,1},{8,10},{10,12},{12... | collective-permute-start | bytes 786440 | tf_op jit(solution)/shard_map/ppermute | solution.py:229
  17.1 4.3 %collective-permute-start.1 = (bf16[1024,128]{1,0:T(8,128)(2,1)S(1)}, bf16[1024,128]{1,0:T(8,128)(2,1)S(1)}, u32[]{:S(2)}, u32[]{:S(2)}) collective-permute-start(bf16[1024,128]{1,0:T(8,128)(2,1)S(1)} %copy-done.11), channel_id=1, source_target_pairs={{0,6},{2,0},{4,2},{6,4},{1,7},{3,1},{5,3},{7,5},{8,14},{10,8},{12,... | collective-permute-start | bytes 786440 | tf_op jit(solution)/shard_map/ppermute | solution.py:229
  24.2 7.4 %collective-permute-done = bf16[1024,128]{1,0:T(8,128)(2,1)S(1)} collective-permute-done((bf16[1024,128]{1,0:T(8,128)(2,1)S(1)}, bf16[1024,128]{1,0:T(8,128)(2,1)S(1)}, u32[]{:S(2)}, u32[]{:S(2)}) %collective-permute-start) | collective-permute-done | bytes 262176 | tf_op jit(solution)/shard_map/ppermute | solution.py:229
  34.0 3.5 %collective-permute-start.4 = (bf16[1024,128]{1,0:T(8,128)(2,1)S(1)}, bf16[1024,128]{1,0:T(8,128)(2,1)S(1)}, u32[]{:S(2)}, u32[]{:S(2)}) collective-permute-start(bf16[1024,128]{1,0:T(8,128)(2,1)S(1)} %collective-permute-done), channel_id=1, source_target_pairs={{0,2},{2,4},{4,6},{6,0},{1,3},{3,5},{5,7},{7,1},{8,10},{10,12},{12... | collective-permute-start | bytes 786440 | tf_op jit(solution)/shard_map/ppermute | solution.py:229
  37.5 7.3 %collective-permute-done.4 = bf16[1024,128]{1,0:T(8,128)(2,1)S(1)} collective-permute-done((bf16[1024,128]{1,0:T(8,128)(2,1)S(1)}, bf16[1024,128]{1,0:T(8,128)(2,1)S(1)}, u32[]{:S(2)}, u32[]{:S(2)}) %collective-permute-start.4) | collective-permute-done | bytes 262176 | tf_op jit(solution)/shard_map/ppermute | solution.py:229
  50.5 3.3 %first.1 = (bf16[112,2048]{1,0:T(8,128)(2,1)}, f32[112,1024]{1,0:T(8,128)}) custom-call(s32[10]{0:T(128)} %stack.97.idx, bf16[8,256,128]{2,1,0:T(8,128)(2,1)} %copy-done.3, bf16[4,1024,128]{2,1,0:T(8,128)(2,1)} %copy-done.9, bf16[4,1024,128]{2,1,0:T(8,128)(2,1)} %copy-done.16), custom_call_target="tpu_custom_call" | custom-call | flops 20000000000 | bytes 4194304 | tf_op jit(solution)/shard_map/first/pallas_call | solution.py:45
  55.0 4.3 %second.3 = (bf16[2,112,1536]{2,1,0:T(8,128)(2,1)}, f32[112,1024]{1,0:T(8,128)}, f32[112,384]{1,0:T(8,128)}, f32[8,2,384]{2,1,0:T(2,128)}, bf16[384,1024]{1,0:T(8,128)(2,1)}) custom-call(s32[10]{0:T(128)} %stack.97.idx, bf16[112,2048]{1,0:T(8,128)(2,1)} %get-tuple-element.46.tokhid, bf16[8,256,128]{2,1,0:T(8,128)(2,1)} %copy-done.3, ...), custom_call_target="tpu_custom_call" | custom-call | flops 500000000 | bytes 4194304 | tf_op jit(solution)/shard_map/second/pallas_call | solution.py:45
  59.3 8.6 %all_to_all.25 = f32[8,2,384]{2,1,0:T(2,128)S(1)} all-to-all(f32[8,2,384]{2,1,0:T(2,128)} %get-tuple-element.51), channel_id=1, replica_groups=mesh['z'=8,'y'=8,'x'=4,'core'=2] {'x','core'}, dimensions={0} | all-to-all | bytes 49152 | tf_op jit(solution)/shard_map/all_to_all | solution.py:282
  67.9 3.1 %collective-permute-start.10 = (bf16[2,112,1536]{2,1,0:T(8,128)(2,1)}, bf16[2,112,1536]{2,1,0:T(8,128)(2,1)S(1)}, u32[]{:S(2)}, u32[]{:S(2)}) collective-permute-start(bf16[2,112,1536]{2,1,0:T(8,128)(2,1)} %get-tuple-element.62), channel_id=1, source_target_pairs={{0,6},{2,0},{4,2},{6,4},{1,7},{3,1},{5,3},{7,5},{8,14},{10,8},{12,... | collective-permute-start | bytes 2064392 | tf_op jit(solution)/shard_map/ppermute | solution.py:229
  71.0 2.8 %collective-permute-start.9 = (bf16[2,112,1536]{2,1,0:T(8,128)(2,1)}, bf16[2,112,1536]{2,1,0:T(8,128)(2,1)S(1)}, u32[]{:S(2)}, u32[]{:S(2)}) collective-permute-start(bf16[2,112,1536]{2,1,0:T(8,128)(2,1)} %get-tuple-element.62), channel_id=1, source_target_pairs={{0,2},{2,4},{4,6},{6,0},{1,3},{3,5},{5,7},{7,1},{8,10},{10,12},{12... | collective-permute-start | bytes 2064392 | tf_op jit(solution)/shard_map/ppermute | solution.py:229
  75.2 16.6 %all-to-all-start.2 = ((f32[64,2,384]{2,1,0:T(2,128)}), f32[64,2,384]{2,1,0:T(2,128)S(1)}, u32[]{:S(2)}, u32[]{:S(2)}) async-start(f32[64,2,384]{2,1,0:T(2,128)} %broadcast_in_dim.9), calls=%async_computation.2 | async-start | bytes 393216 | tf_op jit(solution)/shard_map/all_to_all | solution.py:285
  91.8 4.3 %collective-permute-start.12 = (bf16[112,1536]{1,0:T(8,128)(2,1)S(1)}, bf16[112,1536]{1,0:T(8,128)(2,1)S(1)}, u32[]{:S(2)}, u32[]{:S(2)}) collective-permute-start(bf16[112,1536]{1,0:T(8,128)(2,1)S(1)} %slice_bitcast_fusion), channel_id=1, source_target_pairs={{0,6},{2,0},{4,2},{6,4},{1,7},{3,1},{5,3},{7,5},{8,14},{10,8},{12,... | collective-permute-start | bytes 1032200 | tf_op jit(solution)/shard_map/ppermute | solution.py:229
  98.1 6.2 %all-to-all-done.2.sums = f32[64,2,384]{2,1,0:T(2,128)S(1)} async-done(((f32[64,2,384]{2,1,0:T(2,128)}), f32[64,2,384]{2,1,0:T(2,128)S(1)}, u32[]{:S(2)}, u32[]{:S(2)}) %all-to-all-start.2) | async-done | bytes 196640 | tf_op jit(solution)/shard_map/all_to_all | solution.py:285
  104.9 4.8 %backward.1 = (bf16[8,112,384]{2,1,0:T(8,128)(2,1)}, bf16[112,1024]{1,0:T(8,128)(2,1)}, f32[1,1]{1,0:T(1,128)}) custom-call(s32[10]{0:T(128)} %stack.97.idx, f32[1]{0:T(128)} %bitcast.33.scale, f32[64,2,384]{2,1,0:T(2,128)} %copy-done.12, f32[112,384]{1,0:T(8,128)} %get-tuple-element.54.me, f32[112,1024]{1,0:T(8,128)} %get-tuple-element.55.slope1, ...), custom_call_target="tpu_custom_call" | custom-call | flops 30000001024 | bytes 4194304 | tf_op jit(solution)/shard_map/backward/pallas_call | solution.py:45
  109.8 3.7 %all-to-all-start.3 = ((bf16[8,112,384]{2,1,0:T(8,128)(2,1)}), bf16[8,112,384]{2,1,0:T(8,128)(2,1)S(1)}, u32[]{:S(2)}, u32[]{:S(2)}) async-start(bf16[8,112,384]{2,1,0:T(8,128)(2,1)} %get-tuple-element.63), calls=%async_computation.3 | async-start | bytes 1376256 | tf_op jit(solution)/shard_map/all_to_all | solution.py:298
  116.1 2.4 %collective-permute-start.13 = (bf16[4,2,112,1536]{3,2,1,0:T(8,128)(2,1)S(1)}, bf16[4,2,112,1536]{3,2,1,0:T(8,128)(2,1)}, u32[]{:S(2)}, u32[]{:S(2)}) collective-permute-start(bf16[4,2,112,1536]{3,2,1,0:T(8,128)(2,1)S(1)} %pad_maximum_fusion.near), channel_id=1, source_target_pairs={{0,1},{1,0},{2,3},{3,2},{4,5},{5,4},{6,7},{7,6},{8,9},{9,8},{10,11... | collective-permute-start | bytes 8257544 | tf_op jit(solution)/shard_map/ppermute | solution.py:233
  118.5 3.2 %token_.1 = (f32[4,112,128]{2,1,0:T(8,128)}, f32[4,112,128]{2,1,0:T(8,128)}) custom-call(s32[10]{0:T(128)} %stack.97.idx, bf16[112,1024]{1,0:T(8,128)(2,1)} %get-tuple-element.59.grad1, bf16[4,1024,128]{2,1,0:T(8,128)(2,1)} %copy-done.9, bf16[4,1024,128]{2,1,0:T(8,128)(2,1)} %copy-done.16), custom_call_target="tpu_custom_call" | custom-call | flops 30000001024 | bytes 4194304 | tf_op jit(solution)/shard_map/token/pallas_call | solution.py:45
  126.4 4.9 %weight.1 = bf16[64,40,128]{2,1,0:T(8,128)(2,1)} custom-call(s32[10]{0:T(128)} %stack.97.idx, bf16[4,2,112,1536]{3,2,1,0:T(8,128)(2,1)} %copy-done, bf16[4,2,112,1536]{3,2,1,0:T(8,128)(2,1)} %collective-permute-done.13.far, bf16[8,112,384]{2,1,0:T(8,128)(2,1)} %copy-done.2), custom_call_target="tpu_custom_call" | custom-call | flops 800000000 | bytes 4194304 | tf_op jit(solution)/shard_map/weight/pallas_call | solution.py:45
  131.3 7.4 %all-to-all-start.4 = ((bf16[64,40,128]{2,1,0:T(8,128)(2,1)}), bf16[64,40,128]{2,1,0:T(8,128)(2,1)S(1)}, u32[]{:S(2)}, u32[]{:S(2)}) async-start(bf16[64,40,128]{2,1,0:T(8,128)(2,1)} %weight.1), calls=%async_computation.4 | async-start | bytes 1310720 | tf_op jit(solution)/shard_map/all_to_all | solution.py:308
  140.6 2.5 %collective-permute-start.14 = (f32[2,112,128]{2,1,0:T(8,128)}, f32[2,112,128]{2,1,0:T(8,128)S(1)}, u32[]{:S(2)}, u32[]{:S(2)}) collective-permute-start(f32[2,112,128]{2,1,0:T(8,128)} %get-tuple-element.67), channel_id=1, source_target_pairs={{0,2},{2,4},{4,6},{6,0},{1,3},{3,5},{5,7},{7,1},{8,10},{10,12},{12... | collective-permute-start | bytes 344072 | tf_op jit(solution)/shard_map/ppermute | solution.py:229
  143.0 4.6 %collective-permute-start.15 = (f32[2,112,128]{2,1,0:T(8,128)}, f32[2,112,128]{2,1,0:T(8,128)S(1)}, u32[]{:S(2)}, u32[]{:S(2)}) collective-permute-start(f32[2,112,128]{2,1,0:T(8,128)} %get-tuple-element.68), channel_id=1, source_target_pairs={{0,6},{2,0},{4,2},{6,4},{1,7},{3,1},{5,3},{7,5},{8,14},{10,8},{12,... | collective-permute-start | bytes 344072 | tf_op jit(solution)/shard_map/ppermute | solution.py:229
  151.5 4.5 %collective-permute-done.16.across = f32[2,112,128]{2,1,0:T(8,128)S(1)} collective-permute-done((f32[2,112,128]{2,1,0:T(8,128)}, f32[2,112,128]{2,1,0:T(8,128)S(1)}, u32[]{:S(2)}, u32[]{:S(2)}) %collective-permute-start.16) | collective-permute-done | bytes 114720 | tf_op jit(solution)/shard_map/ppermute | solution.py:229
  (77 shorter events, 38.2 us)
Async XLA Ops:
  2.9 44.0 %copy-start.10 = (bf16[1408,128]{1,0:T(8,128)(2,1)S(1)}, bf16[1408,128]{1,0:T(8,128)(2,1)}, u32[]{:S(2)}) copy-start(bf16[1408,128]{1,0:T(8,128)(2,1)} %get-tuple-element.38) | copy-start | bytes 1081348
  2.9 28.7 %all-to-all-start = ((bf16[8,256,128]{2,1,0:T(8,128)(2,1)}), bf16[8,256,128]{2,1,0:T(8,128)(2,1)S(1)}, u32[]{:S(2)}, u32[]{:S(2)}) async-start(bf16[8,256,128]{2,1,0:T(8,128)(2,1)} %get-tuple-element.39), calls=%async_computation | async-start | bytes 1048576 | tf_op jit(solution)/shard_map/all_to_all | solution.py:258
  7.3 24.3 %collective-permute-start.3 = (bf16[1408,128]{1,0:T(8,128)(2,1)}, bf16[1408,128]{1,0:T(8,128)(2,1)S(1)}, u32[]{:S(2)}, u32[]{:S(2)}) collective-permute-start(bf16[1408,128]{1,0:T(8,128)(2,1)} %get-tuple-element.38), channel_id=1, source_target_pairs={{0,6},{2,0},{4,2},{6,4},{1,7},{3,1},{5,3},{7,5},{8,14},{10,8},{12,... | collective-permute-start | bytes 1081352 | tf_op jit(solution)/shard_map/ppermute | solution.py:229
  12.5 19.1 %collective-permute-start.2 = (bf16[1408,128]{1,0:T(8,128)(2,1)}, bf16[1408,128]{1,0:T(8,128)(2,1)S(1)}, u32[]{:S(2)}, u32[]{:S(2)}) collective-permute-start(bf16[1408,128]{1,0:T(8,128)(2,1)} %get-tuple-element.38), channel_id=1, source_target_pairs={{0,2},{2,4},{4,6},{6,0},{1,3},{3,5},{5,7},{7,1},{8,10},{10,12},{12... | collective-permute-start | bytes 1081352 | tf_op jit(solution)/shard_map/ppermute | solution.py:229
  14.4 17.2 %collective-permute-start = (bf16[1024,128]{1,0:T(8,128)(2,1)S(1)}, bf16[1024,128]{1,0:T(8,128)(2,1)S(1)}, u32[]{:S(2)}, u32[]{:S(2)}) collective-permute-start(bf16[1024,128]{1,0:T(8,128)(2,1)S(1)} %copy-done.11), channel_id=1, source_target_pairs={{0,2},{2,4},{4,6},{6,0},{1,3},{3,5},{5,7},{7,1},{8,10},{10,12},{12... | collective-permute-start | bytes 786440 | tf_op jit(solution)/shard_map/ppermute | solution.py:229
  17.1 14.5 %collective-permute-start.1 = (bf16[1024,128]{1,0:T(8,128)(2,1)S(1)}, bf16[1024,128]{1,0:T(8,128)(2,1)S(1)}, u32[]{:S(2)}, u32[]{:S(2)}) collective-permute-start(bf16[1024,128]{1,0:T(8,128)(2,1)S(1)} %copy-done.11), channel_id=1, source_target_pairs={{0,6},{2,0},{4,2},{6,4},{1,7},{3,1},{5,3},{7,5},{8,14},{10,8},{12,... | collective-permute-start | bytes 786440 | tf_op jit(solution)/shard_map/ppermute | solution.py:229
  31.6 15.5 %copy-start.3 = (bf16[8,256,128]{2,1,0:T(8,128)(2,1)}, bf16[8,256,128]{2,1,0:T(8,128)(2,1)S(1)}, u32[]{:S(2)}) copy-start(bf16[8,256,128]{2,1,0:T(8,128)(2,1)S(1)} %all-to-all-done.given) | copy-start | bytes 1572868
  31.6 13.2 %collective-permute-start.5 = (bf16[1408,128]{1,0:T(8,128)(2,1)S(1)}, bf16[1408,128]{1,0:T(8,128)(2,1)S(1)}, u32[]{:S(2)}, u32[]{:S(2)}) collective-permute-start(bf16[1408,128]{1,0:T(8,128)(2,1)S(1)} %collective-permute-done.3), channel_id=1, source_target_pairs={{0,6},{2,0},{4,2},{6,4},{1,7},{3,1},{5,3},{7,5},{8,14},{10,8},{12,... | collective-permute-start | bytes 1081352 | tf_op jit(solution)/shard_map/ppermute | solution.py:229
  34.0 10.9 %collective-permute-start.4 = (bf16[1024,128]{1,0:T(8,128)(2,1)S(1)}, bf16[1024,128]{1,0:T(8,128)(2,1)S(1)}, u32[]{:S(2)}, u32[]{:S(2)}) collective-permute-start(bf16[1024,128]{1,0:T(8,128)(2,1)S(1)} %collective-permute-done), channel_id=1, source_target_pairs={{0,2},{2,4},{4,6},{6,0},{1,3},{3,5},{5,7},{7,1},{8,10},{10,12},{12... | collective-permute-start | bytes 786440 | tf_op jit(solution)/shard_map/ppermute | solution.py:229
  45.0 4.6 %collective-permute-start.6 = (bf16[4,1024,128]{2,1,0:T(8,128)(2,1)S(1)}, bf16[4,1024,128]{2,1,0:T(8,128)(2,1)S(1)}, u32[]{:S(2)}, u32[]{:S(2)}) collective-permute-start(bf16[4,1024,128]{2,1,0:T(8,128)(2,1)S(1)} %pad_maximum_fusion.2.near), channel_id=1, source_target_pairs={{0,1},{1,0},{2,3},{3,2},{4,5},{5,4},{6,7},{7,6},{8,9},{9,8},{10,11... | collective-permute-start | bytes 3145736 | tf_op jit(solution)/shard_map/ppermute | solution.py:233
  47.1 6.7 %collective-permute-start.7 = (bf16[4,1408,128]{2,1,0:T(8,128)(2,1)S(1)}, bf16[4,1408,128]{2,1,0:T(8,128)(2,1)S(1)}, u32[]{:S(2)}, u32[]{:S(2)}) collective-permute-start(bf16[4,1408,128]{2,1,0:T(8,128)(2,1)S(1)} %pad_maximum_fusion.1.near), channel_id=1, source_target_pairs={{0,1},{1,0},{2,3},{3,2},{4,5},{5,4},{6,7},{7,6},{8,9},{9,8},{10,11... | collective-permute-start | bytes 4325384 | tf_op jit(solution)/shard_map/ppermute | solution.py:233
  67.9 23.8 %collective-permute-start.10 = (bf16[2,112,1536]{2,1,0:T(8,128)(2,1)}, bf16[2,112,1536]{2,1,0:T(8,128)(2,1)S(1)}, u32[]{:S(2)}, u32[]{:S(2)}) collective-permute-start(bf16[2,112,1536]{2,1,0:T(8,128)(2,1)} %get-tuple-element.62), channel_id=1, source_target_pairs={{0,6},{2,0},{4,2},{6,4},{1,7},{3,1},{5,3},{7,5},{8,14},{10,8},{12,... | collective-permute-start | bytes 2064392 | tf_op jit(solution)/shard_map/ppermute | solution.py:229
  71.0 25.1 %collective-permute-start.9 = (bf16[2,112,1536]{2,1,0:T(8,128)(2,1)}, bf16[2,112,1536]{2,1,0:T(8,128)(2,1)S(1)}, u32[]{:S(2)}, u32[]{:S(2)}) collective-permute-start(bf16[2,112,1536]{2,1,0:T(8,128)(2,1)} %get-tuple-element.62), channel_id=1, source_target_pairs={{0,2},{2,4},{4,6},{6,0},{1,3},{3,5},{5,7},{7,1},{8,10},{10,12},{12... | collective-permute-start | bytes 2064392 | tf_op jit(solution)/shard_map/ppermute | solution.py:229
  75.2 29.1 %all-to-all-start.2 = ((f32[64,2,384]{2,1,0:T(2,128)}), f32[64,2,384]{2,1,0:T(2,128)S(1)}, u32[]{:S(2)}, u32[]{:S(2)}) async-start(f32[64,2,384]{2,1,0:T(2,128)} %broadcast_in_dim.9), calls=%async_computation.2 | async-start | bytes 393216 | tf_op jit(solution)/shard_map/all_to_all | solution.py:285
  91.8 18.0 %copy-start.4 = (bf16[2,112,1536]{2,1,0:T(8,128)(2,1)}, bf16[2,112,1536]{2,1,0:T(8,128)(2,1)S(1)}, u32[]{:S(2)}) copy-start(bf16[2,112,1536]{2,1,0:T(8,128)(2,1)S(1)} %collective-permute-done.10) | copy-start | bytes 2064388
  91.8 21.6 %collective-permute-start.12 = (bf16[112,1536]{1,0:T(8,128)(2,1)S(1)}, bf16[112,1536]{1,0:T(8,128)(2,1)S(1)}, u32[]{:S(2)}, u32[]{:S(2)}) collective-permute-start(bf16[112,1536]{1,0:T(8,128)(2,1)S(1)} %slice_bitcast_fusion), channel_id=1, source_target_pairs={{0,6},{2,0},{4,2},{6,4},{1,7},{3,1},{5,3},{7,5},{8,14},{10,8},{12,... | collective-permute-start | bytes 1032200 | tf_op jit(solution)/shard_map/ppermute | solution.py:229
  96.2 17.3 %collective-permute-start.11 = (bf16[112,1536]{1,0:T(8,128)(2,1)S(1)}, bf16[112,1536]{1,0:T(8,128)(2,1)S(1)}, u32[]{:S(2)}, u32[]{:S(2)}) collective-permute-start(bf16[112,1536]{1,0:T(8,128)(2,1)S(1)} %slice_bitcast_fusion.1), channel_id=1, source_target_pairs={{0,2},{2,4},{4,6},{6,0},{1,3},{3,5},{5,7},{7,1},{8,10},{10,12},{12... | collective-permute-start | bytes 1032200 | tf_op jit(solution)/shard_map/ppermute | solution.py:229
  109.8 15.8 %all-to-all-start.3 = ((bf16[8,112,384]{2,1,0:T(8,128)(2,1)}), bf16[8,112,384]{2,1,0:T(8,128)(2,1)S(1)}, u32[]{:S(2)}, u32[]{:S(2)}) async-start(bf16[8,112,384]{2,1,0:T(8,128)(2,1)} %get-tuple-element.63), calls=%async_computation.3 | async-start | bytes 1376256 | tf_op jit(solution)/shard_map/all_to_all | solution.py:298
  116.1 9.4 %collective-permute-start.13 = (bf16[4,2,112,1536]{3,2,1,0:T(8,128)(2,1)S(1)}, bf16[4,2,112,1536]{3,2,1,0:T(8,128)(2,1)}, u32[]{:S(2)}, u32[]{:S(2)}) collective-permute-start(bf16[4,2,112,1536]{3,2,1,0:T(8,128)(2,1)S(1)} %pad_maximum_fusion.near), channel_id=1, source_target_pairs={{0,1},{1,0},{2,3},{3,2},{4,5},{5,4},{6,7},{7,6},{8,9},{9,8},{10,11... | collective-permute-start | bytes 8257544 | tf_op jit(solution)/shard_map/ppermute | solution.py:233
  121.8 9.5 %collective-permute-start.8 = (f32[4,112,128]{2,1,0:T(8,128)}, f32[4,112,128]{2,1,0:T(8,128)}, u32[]{:S(2)}, u32[]{:S(2)}) collective-permute-start(f32[4,112,128]{2,1,0:T(8,128)} %get-tuple-element.60), channel_id=1, source_target_pairs={{0,1},{1,0},{2,3},{3,2},{4,5},{5,4},{6,7},{7,6},{8,9},{9,8},{10,11... | collective-permute-start | bytes 688136 | tf_op jit(solution)/shard_map/ppermute | solution.py:233
  131.3 29.2 %all-to-all-start.4 = ((bf16[64,40,128]{2,1,0:T(8,128)(2,1)}), bf16[64,40,128]{2,1,0:T(8,128)(2,1)S(1)}, u32[]{:S(2)}, u32[]{:S(2)}) async-start(bf16[64,40,128]{2,1,0:T(8,128)(2,1)} %weight.1), calls=%async_computation.4 | async-start | bytes 1310720 | tf_op jit(solution)/shard_map/all_to_all | solution.py:308
  140.6 9.4 %collective-permute-start.14 = (f32[2,112,128]{2,1,0:T(8,128)}, f32[2,112,128]{2,1,0:T(8,128)S(1)}, u32[]{:S(2)}, u32[]{:S(2)}) collective-permute-start(f32[2,112,128]{2,1,0:T(8,128)} %get-tuple-element.67), channel_id=1, source_target_pairs={{0,2},{2,4},{4,6},{6,0},{1,3},{3,5},{5,7},{7,1},{8,10},{10,12},{12... | collective-permute-start | bytes 344072 | tf_op jit(solution)/shard_map/ppermute | solution.py:229
  143.0 8.4 %collective-permute-start.15 = (f32[2,112,128]{2,1,0:T(8,128)}, f32[2,112,128]{2,1,0:T(8,128)S(1)}, u32[]{:S(2)}, u32[]{:S(2)}) collective-permute-start(f32[2,112,128]{2,1,0:T(8,128)} %get-tuple-element.68), channel_id=1, source_target_pairs={{0,6},{2,0},{4,2},{6,4},{1,7},{3,1},{5,3},{7,5},{8,14},{10,8},{12,... | collective-permute-start | bytes 344072 | tf_op jit(solution)/shard_map/ppermute | solution.py:229
  147.6 8.4 %collective-permute-start.16 = (f32[2,112,128]{2,1,0:T(8,128)}, f32[2,112,128]{2,1,0:T(8,128)S(1)}, u32[]{:S(2)}, u32[]{:S(2)}) collective-permute-start(f32[2,112,128]{2,1,0:T(8,128)} %get-tuple-element.69), channel_id=1, source_target_pairs={{0,4},{2,6},{4,0},{6,2},{1,5},{3,7},{5,1},{7,3},{8,12},{10,14},{12... | collective-permute-start | bytes 344072 | tf_op jit(solution)/shard_map/ppermute | solution.py:229
  (14 other events, 59.2 us)

commit v7 on v6

--- a/solution.py
+++ b/solution.py
@@ -255,14 +255,15 @@
         prep_body, "prep", [((8, PIECE, 128), BF), ((D + COLS, 128), BF)],
         [variable_kind, tokens, targets, second_weight, head_weight], smem=(0,),
     )
-    given = lax.all_to_all(given, TENSOR, 0, 0, tiled=True)
     w1_m1, w1_p1 = shift(first_weight, 1), shift(first_weight, 3)
     w2_m1, w2_p1 = shift(packed, 1), shift(packed, 3)
-    w1_m1, w1_p1, w2_m1, w2_p1, given, idx, land, weights = lax.optimization_barrier(
-        (w1_m1, w1_p1, w2_m1, w2_p1, given, idx, land, weights)
+    given, w1_m1 = lax.optimization_barrier((given, w1_m1))
+    given = lax.all_to_all(given, TENSOR, 0, 0, tiled=True)
+    w1_m1, w1_p1, w2_m1, w2_p1, idx, land, weights = lax.optimization_barrier(
+        (w1_m1, w1_p1, w2_m1, w2_p1, idx, land, weights)
     )
     w1_last, w2_last = shift(w1_m1, 1), shift(w2_p1, 3)
-    w1_last, w2_last = lax.optimization_barrier((w1_last, w2_last))
+    w1_last, w2_last, given = lax.optimization_barrier((w1_last, w2_last, given))
     near1 = jnp.stack([first_weight, w1_m1, w1_p1, w1_last])
     near2 = jnp.stack([packed, w2_m1, w2_p1, w2_last])
     far1, far2 = flip(near1), flip(near2)

time: 163 us -> 158 us (0.969)
  waiting for transfers between devices: 30.8 us -> 25.5 us
    ppermute x13, waiting for transfers between devices: 20.8 us -> 15.5 us  [shift(): return lax.ppermute(v, 'x', [(i, (i + by) % 4) for i in range(4)])]
  transfers between devices with their start and end apart: 21 -> 21, of which waited for: 7 -> 7; matrix products, arithmetic and copies ran while one was open for 3% -> 3% of each run, Pallas kernels for 12% -> 14%
where the time goes in v7:
time: 158 us; the launch traced here: 157 us
  starting transfers between devices  82.4 us (52%)
  Pallas kernels  26.5 us (17%)
  waiting for transfers between devices  25.5 us (16%)
  blocking collectives  8.97 us (6%)
  local copies, waits for them, and re-layouts  8.18 us (5%)
  other arithmetic  3.89 us (2%)
  between operations  1.78 us (1%)
    ppermute x13, starting transfers between devices, shift(): return lax.ppermute(v, 'x', [(i, (i + by) % 4) for i in range(4)])  42.5 us
    pallas_call x8, Pallas kernels, call(): pl.pallas_call(body, name=name, out_shape=tuple((jax.ShapeDtypeStruct(s,...  26.5 us
    all_to_all x1, starting transfers between devices, per_device(): sums = lax.all_to_all(spread, SPACE, 0, 0, tiled=True)  16.6 us
    ppermute x13, waiting for transfers between devices, shift(): return lax.ppermute(v, 'x', [(i, (i + by) % 4) for i in range(4)])  15.5 us
    all_to_all x1, blocking collectives, per_device(): sums = lax.all_to_all(sums, TENSOR, 0, 0, tiled=True)  8.97 us
    ppermute x4, starting transfers between devices, flip(): return lax.ppermute(v, 'core', [(0, 1), (1, 0)])  8.65 us
    all_to_all x1, starting transfers between devices, per_device(): out = lax.all_to_all(out, SPACE, 0, 0, tiled=True)  7.41 us
    all_to_all x1, waiting for transfers between devices, per_device(): sums = lax.all_to_all(spread, SPACE, 0, 0, tiled=True)  6.16 us
  transfers between devices with their start and end apart: 21, of which 7 were waited for; matrix products, arithmetic and copies ran while one was open for 3% of the time, Pallas kernels for 14%

profile of v7, /device:TPU:8, one launch (start us, length us, event | category | flops | bytes accessed | tf_op | source)
XLA Modules:
  0.0 157.2 jit_solution(14359774317537782631)
XLA Ops:
  0.6 3.5 %collective-permute-start = (bf16[1024,128]{1,0:T(8,128)(2,1)}, bf16[1024,128]{1,0:T(8,128)(2,1)S(1)}, u32[]{:S(2)}, u32[]{:S(2)}) collective-permute-start(bf16[1024,128]{1,0:T(8,128)(2,1)} %param.9), channel_id=1, source_target_pairs={{0,2},{2,4},{4,6},{6,0},{1,3},{3,5},{5,7},{7,1},{8,10},{10,12},{12... | collective-permute-start | bytes 786440 | tf_op jit(solution)/shard_map/ppermute | solution.py:229
  6.4 3.6 %collective-permute-start.3 = (bf16[1408,128]{1,0:T(8,128)(2,1)}, bf16[1408,128]{1,0:T(8,128)(2,1)S(1)}, u32[]{:S(2)}, u32[]{:S(2)}) collective-permute-start(bf16[1408,128]{1,0:T(8,128)(2,1)} %get-tuple-element.42), channel_id=1, source_target_pairs={{0,6},{2,0},{4,2},{6,4},{1,7},{3,1},{5,3},{7,5},{8,14},{10,8},{12,... | collective-permute-start | bytes 1081352 | tf_op jit(solution)/shard_map/ppermute | solution.py:229
  12.3 4.9 %collective-permute-start.1 = (bf16[1024,128]{1,0:T(8,128)(2,1)}, bf16[1024,128]{1,0:T(8,128)(2,1)S(1)}, u32[]{:S(2)}, u32[]{:S(2)}) collective-permute-start(bf16[1024,128]{1,0:T(8,128)(2,1)} %param.9), channel_id=1, source_target_pairs={{0,6},{2,0},{4,2},{6,4},{1,7},{3,1},{5,3},{7,5},{8,14},{10,8},{12,... | collective-permute-start | bytes 786440 | tf_op jit(solution)/shard_map/ppermute | solution.py:229
  19.2 3.6 %all-to-all-start = ((bf16[8,256,128]{2,1,0:T(8,128)(2,1)}), bf16[8,256,128]{2,1,0:T(8,128)(2,1)S(1)}, u32[]{:S(2)}, u32[]{:S(2)}) async-start(bf16[8,256,128]{2,1,0:T(8,128)(2,1)} %get-tuple-element.46), calls=%async_computation | async-start | bytes 1048576 | tf_op jit(solution)/shard_map/all_to_all | solution.py:261
  24.0 4.9 %collective-permute-start.5 = (bf16[1408,128]{1,0:T(8,128)(2,1)S(1)}, bf16[1408,128]{1,0:T(8,128)(2,1)S(1)}, u32[]{:S(2)}, u32[]{:S(2)}) collective-permute-start(bf16[1408,128]{1,0:T(8,128)(2,1)S(1)} %collective-permute-done.3), channel_id=1, source_target_pairs={{0,6},{2,0},{4,2},{6,4},{1,7},{3,1},{5,3},{7,5},{8,14},{10,8},{12,... | collective-permute-start | bytes 1081352 | tf_op jit(solution)/shard_map/ppermute | solution.py:229
  30.8 9.0 %collective-permute-done.4 = bf16[1024,128]{1,0:T(8,128)(2,1)S(1)} collective-permute-done((bf16[1024,128]{1,0:T(8,128)(2,1)S(1)}, bf16[1024,128]{1,0:T(8,128)(2,1)S(1)}, u32[]{:S(2)}, u32[]{:S(2)}) %collective-permute-start.4) | collective-permute-done | bytes 262176 | tf_op jit(solution)/shard_map/ppermute | solution.py:229
  42.1 2.4 %collective-permute-start.7 = (bf16[4,1408,128]{2,1,0:T(8,128)(2,1)S(1)}, bf16[4,1408,128]{2,1,0:T(8,128)(2,1)S(1)}, u32[]{:S(2)}, u32[]{:S(2)}) collective-permute-start(bf16[4,1408,128]{2,1,0:T(8,128)(2,1)S(1)} %pad_maximum_fusion.1.near), channel_id=1, source_target_pairs={{0,1},{1,0},{2,3},{3,2},{4,5},{5,4},{6,7},{7,6},{8,9},{9,8},{10,11... | collective-permute-start | bytes 4325384 | tf_op jit(solution)/shard_map/ppermute | solution.py:233
  45.5 3.3 %first.1 = (bf16[112,2048]{1,0:T(8,128)(2,1)}, f32[112,1024]{1,0:T(8,128)}) custom-call(s32[10]{0:T(128)} %stack.97.idx, bf16[8,256,128]{2,1,0:T(8,128)(2,1)} %copy-done.3, bf16[4,1024,128]{2,1,0:T(8,128)(2,1)} %copy-done.9, bf16[4,1024,128]{2,1,0:T(8,128)(2,1)} %copy-done.16), custom_call_target="tpu_custom_call" | custom-call | flops 20000000000 | bytes 4194304 | tf_op jit(solution)/shard_map/first/pallas_call | solution.py:45
  49.9 4.3 %second.3 = (bf16[2,112,1536]{2,1,0:T(8,128)(2,1)}, f32[112,1024]{1,0:T(8,128)}, f32[112,384]{1,0:T(8,128)}, f32[8,2,384]{2,1,0:T(2,128)}, bf16[384,1024]{1,0:T(8,128)(2,1)}) custom-call(s32[10]{0:T(128)} %stack.97.idx, bf16[112,2048]{1,0:T(8,128)(2,1)} %get-tuple-element.50.tokhid, bf16[8,256,128]{2,1,0:T(8,128)(2,1)} %copy-done.3, ...), custom_call_target="tpu_custom_call" | custom-call | flops 500000000 | bytes 4194304 | tf_op jit(solution)/shard_map/second/pallas_call | solution.py:45
  54.2 9.0 %all_to_all.25 = f32[8,2,384]{2,1,0:T(2,128)S(1)} all-to-all(f32[8,2,384]{2,1,0:T(2,128)} %get-tuple-element.55), channel_id=1, replica_groups=mesh['z'=8,'y'=8,'x'=4,'core'=2] {'x','core'}, dimensions={0} | all-to-all | bytes 49152 | tf_op jit(solution)/shard_map/all_to_all | solution.py:283
  63.2 3.1 %collective-permute-start.10 = (bf16[2,112,1536]{2,1,0:T(8,128)(2,1)}, bf16[2,112,1536]{2,1,0:T(8,128)(2,1)S(1)}, u32[]{:S(2)}, u32[]{:S(2)}) collective-permute-start(bf16[2,112,1536]{2,1,0:T(8,128)(2,1)} %get-tuple-element.66), channel_id=1, source_target_pairs={{0,6},{2,0},{4,2},{6,4},{1,7},{3,1},{5,3},{7,5},{8,14},{10,8},{12,... | collective-permute-start | bytes 2064392 | tf_op jit(solution)/shard_map/ppermute | solution.py:229
  66.3 2.8 %collective-permute-start.9 = (bf16[2,112,1536]{2,1,0:T(8,128)(2,1)}, bf16[2,112,1536]{2,1,0:T(8,128)(2,1)S(1)}, u32[]{:S(2)}, u32[]{:S(2)}) collective-permute-start(bf16[2,112,1536]{2,1,0:T(8,128)(2,1)} %get-tuple-element.66), channel_id=1, source_target_pairs={{0,2},{2,4},{4,6},{6,0},{1,3},{3,5},{5,7},{7,1},{8,10},{10,12},{12... | collective-permute-start | bytes 2064392 | tf_op jit(solution)/shard_map/ppermute | solution.py:229
  70.5 16.6 %all-to-all-start.2 = ((f32[64,2,384]{2,1,0:T(2,128)}), f32[64,2,384]{2,1,0:T(2,128)S(1)}, u32[]{:S(2)}, u32[]{:S(2)}) async-start(f32[64,2,384]{2,1,0:T(2,128)} %broadcast_in_dim.9), calls=%async_computation.2 | async-start | bytes 393216 | tf_op jit(solution)/shard_map/all_to_all | solution.py:286
  87.1 4.3 %collective-permute-start.12 = (bf16[112,1536]{1,0:T(8,128)(2,1)S(1)}, bf16[112,1536]{1,0:T(8,128)(2,1)S(1)}, u32[]{:S(2)}, u32[]{:S(2)}) collective-permute-start(bf16[112,1536]{1,0:T(8,128)(2,1)S(1)} %slice_bitcast_fusion), channel_id=1, source_target_pairs={{0,6},{2,0},{4,2},{6,4},{1,7},{3,1},{5,3},{7,5},{8,14},{10,8},{12,... | collective-permute-start | bytes 1032200 | tf_op jit(solution)/shard_map/ppermute | solution.py:229
  93.4 6.2 %all-to-all-done.2.sums = f32[64,2,384]{2,1,0:T(2,128)S(1)} async-done(((f32[64,2,384]{2,1,0:T(2,128)}), f32[64,2,384]{2,1,0:T(2,128)S(1)}, u32[]{:S(2)}, u32[]{:S(2)}) %all-to-all-start.2) | async-done | bytes 196640 | tf_op jit(solution)/shard_map/all_to_all | solution.py:286
  100.2 4.8 %backward.1 = (bf16[8,112,384]{2,1,0:T(8,128)(2,1)}, bf16[112,1024]{1,0:T(8,128)(2,1)}, f32[1,1]{1,0:T(1,128)}) custom-call(s32[10]{0:T(128)} %stack.97.idx, f32[1]{0:T(128)} %bitcast.33.scale, f32[64,2,384]{2,1,0:T(2,128)} %copy-done.12, f32[112,384]{1,0:T(8,128)} %get-tuple-element.58.me, f32[112,1024]{1,0:T(8,128)} %get-tuple-element.59.slope1, ...), custom_call_target="tpu_custom_call" | custom-call | flops 30000001024 | bytes 4194304 | tf_op jit(solution)/shard_map/backward/pallas_call | solution.py:45
  105.1 3.7 %all-to-all-start.3 = ((bf16[8,112,384]{2,1,0:T(8,128)(2,1)}), bf16[8,112,384]{2,1,0:T(8,128)(2,1)S(1)}, u32[]{:S(2)}, u32[]{:S(2)}) async-start(bf16[8,112,384]{2,1,0:T(8,128)(2,1)} %get-tuple-element.67), calls=%async_computation.3 | async-start | bytes 1376256 | tf_op jit(solution)/shard_map/all_to_all | solution.py:299
  111.4 2.4 %collective-permute-start.13 = (bf16[4,2,112,1536]{3,2,1,0:T(8,128)(2,1)S(1)}, bf16[4,2,112,1536]{3,2,1,0:T(8,128)(2,1)}, u32[]{:S(2)}, u32[]{:S(2)}) collective-permute-start(bf16[4,2,112,1536]{3,2,1,0:T(8,128)(2,1)S(1)} %pad_maximum_fusion.near), channel_id=1, source_target_pairs={{0,1},{1,0},{2,3},{3,2},{4,5},{5,4},{6,7},{7,6},{8,9},{9,8},{10,11... | collective-permute-start | bytes 8257544 | tf_op jit(solution)/shard_map/ppermute | solution.py:233
  113.8 3.2 %token_.1 = (f32[4,112,128]{2,1,0:T(8,128)}, f32[4,112,128]{2,1,0:T(8,128)}) custom-call(s32[10]{0:T(128)} %stack.97.idx, bf16[112,1024]{1,0:T(8,128)(2,1)} %get-tuple-element.63.grad1, bf16[4,1024,128]{2,1,0:T(8,128)(2,1)} %copy-done.9, bf16[4,1024,128]{2,1,0:T(8,128)(2,1)} %copy-done.16), custom_call_target="tpu_custom_call" | custom-call | flops 30000001024 | bytes 4194304 | tf_op jit(solution)/shard_map/token/pallas_call | solution.py:45
  121.7 4.9 %weight.1 = bf16[64,40,128]{2,1,0:T(8,128)(2,1)} custom-call(s32[10]{0:T(128)} %stack.97.idx, bf16[4,2,112,1536]{3,2,1,0:T(8,128)(2,1)} %copy-done, bf16[4,2,112,1536]{3,2,1,0:T(8,128)(2,1)} %collective-permute-done.13.far, bf16[8,112,384]{2,1,0:T(8,128)(2,1)} %copy-done.2), custom_call_target="tpu_custom_call" | custom-call | flops 800000000 | bytes 4194304 | tf_op jit(solution)/shard_map/weight/pallas_call | solution.py:45
  126.6 7.4 %all-to-all-start.4 = ((bf16[64,40,128]{2,1,0:T(8,128)(2,1)}), bf16[64,40,128]{2,1,0:T(8,128)(2,1)S(1)}, u32[]{:S(2)}, u32[]{:S(2)}) async-start(bf16[64,40,128]{2,1,0:T(8,128)(2,1)} %weight.1), calls=%async_computation.4 | async-start | bytes 1310720 | tf_op jit(solution)/shard_map/all_to_all | solution.py:309
  135.9 2.5 %collective-permute-start.14 = (f32[2,112,128]{2,1,0:T(8,128)}, f32[2,112,128]{2,1,0:T(8,128)S(1)}, u32[]{:S(2)}, u32[]{:S(2)}) collective-permute-start(f32[2,112,128]{2,1,0:T(8,128)} %get-tuple-element.71), channel_id=1, source_target_pairs={{0,2},{2,4},{4,6},{6,0},{1,3},{3,5},{5,7},{7,1},{8,10},{10,12},{12... | collective-permute-start | bytes 344072 | tf_op jit(solution)/shard_map/ppermute | solution.py:229
  138.4 4.6 %collective-permute-start.15 = (f32[2,112,128]{2,1,0:T(8,128)}, f32[2,112,128]{2,1,0:T(8,128)S(1)}, u32[]{:S(2)}, u32[]{:S(2)}) collective-permute-start(f32[2,112,128]{2,1,0:T(8,128)} %get-tuple-element.72), channel_id=1, source_target_pairs={{0,6},{2,0},{4,2},{6,4},{1,7},{3,1},{5,3},{7,5},{8,14},{10,8},{12,... | collective-permute-start | bytes 344072 | tf_op jit(solution)/shard_map/ppermute | solution.py:229
  146.8 4.5 %collective-permute-done.16.across = f32[2,112,128]{2,1,0:T(8,128)S(1)} collective-permute-done((f32[2,112,128]{2,1,0:T(8,128)}, f32[2,112,128]{2,1,0:T(8,128)S(1)}, u32[]{:S(2)}, u32[]{:S(2)}) %collective-permute-start.16) | collective-permute-done | bytes 114720 | tf_op jit(solution)/shard_map/ppermute | solution.py:229
  (77 shorter events, 36.1 us)
Async XLA Ops:
  0.6 39.1 %copy-start.11 = (bf16[1024,128]{1,0:T(8,128)(2,1)S(1)}, bf16[1024,128]{1,0:T(8,128)(2,1)}, u32[]{:S(2)}) copy-start(bf16[1024,128]{1,0:T(8,128)(2,1)} %param.9) | copy-start | bytes 786436
  0.6 18.6 %collective-permute-start = (bf16[1024,128]{1,0:T(8,128)(2,1)}, bf16[1024,128]{1,0:T(8,128)(2,1)S(1)}, u32[]{:S(2)}, u32[]{:S(2)}) collective-permute-start(bf16[1024,128]{1,0:T(8,128)(2,1)} %param.9), channel_id=1, source_target_pairs={{0,2},{2,4},{4,6},{6,0},{1,3},{3,5},{5,7},{7,1},{8,10},{10,12},{12... | collective-permute-start | bytes 786440 | tf_op jit(solution)/shard_map/ppermute | solution.py:229
  6.4 17.6 %collective-permute-start.3 = (bf16[1408,128]{1,0:T(8,128)(2,1)}, bf16[1408,128]{1,0:T(8,128)(2,1)S(1)}, u32[]{:S(2)}, u32[]{:S(2)}) collective-permute-start(bf16[1408,128]{1,0:T(8,128)(2,1)} %get-tuple-element.42), channel_id=1, source_target_pairs={{0,6},{2,0},{4,2},{6,4},{1,7},{3,1},{5,3},{7,5},{8,14},{10,8},{12,... | collective-permute-start | bytes 1081352 | tf_op jit(solution)/shard_map/ppermute | solution.py:229
  10.1 13.9 %collective-permute-start.2 = (bf16[1408,128]{1,0:T(8,128)(2,1)}, bf16[1408,128]{1,0:T(8,128)(2,1)S(1)}, u32[]{:S(2)}, u32[]{:S(2)}) collective-permute-start(bf16[1408,128]{1,0:T(8,128)(2,1)} %get-tuple-element.42), channel_id=1, source_target_pairs={{0,2},{2,4},{4,6},{6,0},{1,3},{3,5},{5,7},{7,1},{8,10},{10,12},{12... | collective-permute-start | bytes 1081352 | tf_op jit(solution)/shard_map/ppermute | solution.py:229
  12.3 11.7 %collective-permute-start.1 = (bf16[1024,128]{1,0:T(8,128)(2,1)}, bf16[1024,128]{1,0:T(8,128)(2,1)S(1)}, u32[]{:S(2)}, u32[]{:S(2)}) collective-permute-start(bf16[1024,128]{1,0:T(8,128)(2,1)} %param.9), channel_id=1, source_target_pairs={{0,6},{2,0},{4,2},{6,4},{1,7},{3,1},{5,3},{7,5},{8,14},{10,8},{12,... | collective-permute-start | bytes 786440 | tf_op jit(solution)/shard_map/ppermute | solution.py:229
  19.2 22.7 %copy-start.10 = (bf16[1408,128]{1,0:T(8,128)(2,1)S(1)}, bf16[1408,128]{1,0:T(8,128)(2,1)}, u32[]{:S(2)}) copy-start(bf16[1408,128]{1,0:T(8,128)(2,1)} %get-tuple-element.42) | copy-start | bytes 1081348
  19.2 20.6 %all-to-all-start = ((bf16[8,256,128]{2,1,0:T(8,128)(2,1)}), bf16[8,256,128]{2,1,0:T(8,128)(2,1)S(1)}, u32[]{:S(2)}, u32[]{:S(2)}) async-start(bf16[8,256,128]{2,1,0:T(8,128)(2,1)} %get-tuple-element.46), calls=%async_computation | async-start | bytes 1048576 | tf_op jit(solution)/shard_map/all_to_all | solution.py:261
  24.0 15.8 %collective-permute-start.5 = (bf16[1408,128]{1,0:T(8,128)(2,1)S(1)}, bf16[1408,128]{1,0:T(8,128)(2,1)S(1)}, u32[]{:S(2)}, u32[]{:S(2)}) collective-permute-start(bf16[1408,128]{1,0:T(8,128)(2,1)S(1)} %collective-permute-done.3), channel_id=1, source_target_pairs={{0,6},{2,0},{4,2},{6,4},{1,7},{3,1},{5,3},{7,5},{8,14},{10,8},{12,... | collective-permute-start | bytes 1081352 | tf_op jit(solution)/shard_map/ppermute | solution.py:229
  28.9 10.9 %collective-permute-start.4 = (bf16[1024,128]{1,0:T(8,128)(2,1)S(1)}, bf16[1024,128]{1,0:T(8,128)(2,1)S(1)}, u32[]{:S(2)}, u32[]{:S(2)}) collective-permute-start(bf16[1024,128]{1,0:T(8,128)(2,1)S(1)} %collective-permute-done), channel_id=1, source_target_pairs={{0,2},{2,4},{4,6},{6,0},{1,3},{3,5},{5,7},{7,1},{8,10},{10,12},{12... | collective-permute-start | bytes 786440 | tf_op jit(solution)/shard_map/ppermute | solution.py:229
  39.9 4.6 %collective-permute-start.6 = (bf16[4,1024,128]{2,1,0:T(8,128)(2,1)S(1)}, bf16[4,1024,128]{2,1,0:T(8,128)(2,1)S(1)}, u32[]{:S(2)}, u32[]{:S(2)}) collective-permute-start(bf16[4,1024,128]{2,1,0:T(8,128)(2,1)S(1)} %pad_maximum_fusion.2.near), channel_id=1, source_target_pairs={{0,1},{1,0},{2,3},{3,2},{4,5},{5,4},{6,7},{7,6},{8,9},{9,8},{10,11... | collective-permute-start | bytes 3145736 | tf_op jit(solution)/shard_map/ppermute | solution.py:233
  42.1 6.7 %collective-permute-start.7 = (bf16[4,1408,128]{2,1,0:T(8,128)(2,1)S(1)}, bf16[4,1408,128]{2,1,0:T(8,128)(2,1)S(1)}, u32[]{:S(2)}, u32[]{:S(2)}) collective-permute-start(bf16[4,1408,128]{2,1,0:T(8,128)(2,1)S(1)} %pad_maximum_fusion.1.near), channel_id=1, source_target_pairs={{0,1},{1,0},{2,3},{3,2},{4,5},{5,4},{6,7},{7,6},{8,9},{9,8},{10,11... | collective-permute-start | bytes 4325384 | tf_op jit(solution)/shard_map/ppermute | solution.py:233
  63.2 23.9 %collective-permute-start.10 = (bf16[2,112,1536]{2,1,0:T(8,128)(2,1)}, bf16[2,112,1536]{2,1,0:T(8,128)(2,1)S(1)}, u32[]{:S(2)}, u32[]{:S(2)}) collective-permute-start(bf16[2,112,1536]{2,1,0:T(8,128)(2,1)} %get-tuple-element.66), channel_id=1, source_target_pairs={{0,6},{2,0},{4,2},{6,4},{1,7},{3,1},{5,3},{7,5},{8,14},{10,8},{12,... | collective-permute-start | bytes 2064392 | tf_op jit(solution)/shard_map/ppermute | solution.py:229
  66.3 25.1 %collective-permute-start.9 = (bf16[2,112,1536]{2,1,0:T(8,128)(2,1)}, bf16[2,112,1536]{2,1,0:T(8,128)(2,1)S(1)}, u32[]{:S(2)}, u32[]{:S(2)}) collective-permute-start(bf16[2,112,1536]{2,1,0:T(8,128)(2,1)} %get-tuple-element.66), channel_id=1, source_target_pairs={{0,2},{2,4},{4,6},{6,0},{1,3},{3,5},{5,7},{7,1},{8,10},{10,12},{12... | collective-permute-start | bytes 2064392 | tf_op jit(solution)/shard_map/ppermute | solution.py:229
  70.5 29.1 %all-to-all-start.2 = ((f32[64,2,384]{2,1,0:T(2,128)}), f32[64,2,384]{2,1,0:T(2,128)S(1)}, u32[]{:S(2)}, u32[]{:S(2)}) async-start(f32[64,2,384]{2,1,0:T(2,128)} %broadcast_in_dim.9), calls=%async_computation.2 | async-start | bytes 393216 | tf_op jit(solution)/shard_map/all_to_all | solution.py:286
  87.1 18.0 %copy-start.4 = (bf16[2,112,1536]{2,1,0:T(8,128)(2,1)}, bf16[2,112,1536]{2,1,0:T(8,128)(2,1)S(1)}, u32[]{:S(2)}) copy-start(bf16[2,112,1536]{2,1,0:T(8,128)(2,1)S(1)} %collective-permute-done.10) | copy-start | bytes 2064388
  87.1 21.6 %collective-permute-start.12 = (bf16[112,1536]{1,0:T(8,128)(2,1)S(1)}, bf16[112,1536]{1,0:T(8,128)(2,1)S(1)}, u32[]{:S(2)}, u32[]{:S(2)}) collective-permute-start(bf16[112,1536]{1,0:T(8,128)(2,1)S(1)} %slice_bitcast_fusion), channel_id=1, source_target_pairs={{0,6},{2,0},{4,2},{6,4},{1,7},{3,1},{5,3},{7,5},{8,14},{10,8},{12,... | collective-permute-start | bytes 1032200 | tf_op jit(solution)/shard_map/ppermute | solution.py:229
  91.5 17.3 %collective-permute-start.11 = (bf16[112,1536]{1,0:T(8,128)(2,1)S(1)}, bf16[112,1536]{1,0:T(8,128)(2,1)S(1)}, u32[]{:S(2)}, u32[]{:S(2)}) collective-permute-start(bf16[112,1536]{1,0:T(8,128)(2,1)S(1)} %slice_bitcast_fusion.1), channel_id=1, source_target_pairs={{0,2},{2,4},{4,6},{6,0},{1,3},{3,5},{5,7},{7,1},{8,10},{10,12},{12... | collective-permute-start | bytes 1032200 | tf_op jit(solution)/shard_map/ppermute | solution.py:229
  105.1 15.8 %all-to-all-start.3 = ((bf16[8,112,384]{2,1,0:T(8,128)(2,1)}), bf16[8,112,384]{2,1,0:T(8,128)(2,1)S(1)}, u32[]{:S(2)}, u32[]{:S(2)}) async-start(bf16[8,112,384]{2,1,0:T(8,128)(2,1)} %get-tuple-element.67), calls=%async_computation.3 | async-start | bytes 1376256 | tf_op jit(solution)/shard_map/all_to_all | solution.py:299
  111.4 9.4 %collective-permute-start.13 = (bf16[4,2,112,1536]{3,2,1,0:T(8,128)(2,1)S(1)}, bf16[4,2,112,1536]{3,2,1,0:T(8,128)(2,1)}, u32[]{:S(2)}, u32[]{:S(2)}) collective-permute-start(bf16[4,2,112,1536]{3,2,1,0:T(8,128)(2,1)S(1)} %pad_maximum_fusion.near), channel_id=1, source_target_pairs={{0,1},{1,0},{2,3},{3,2},{4,5},{5,4},{6,7},{7,6},{8,9},{9,8},{10,11... | collective-permute-start | bytes 8257544 | tf_op jit(solution)/shard_map/ppermute | solution.py:233
  117.1 9.5 %collective-permute-start.8 = (f32[4,112,128]{2,1,0:T(8,128)}, f32[4,112,128]{2,1,0:T(8,128)}, u32[]{:S(2)}, u32[]{:S(2)}) collective-permute-start(f32[4,112,128]{2,1,0:T(8,128)} %get-tuple-element.64), channel_id=1, source_target_pairs={{0,1},{1,0},{2,3},{3,2},{4,5},{5,4},{6,7},{7,6},{8,9},{9,8},{10,11... | collective-permute-start | bytes 688136 | tf_op jit(solution)/shard_map/ppermute | solution.py:233
  126.6 29.2 %all-to-all-start.4 = ((bf16[64,40,128]{2,1,0:T(8,128)(2,1)}), bf16[64,40,128]{2,1,0:T(8,128)(2,1)S(1)}, u32[]{:S(2)}, u32[]{:S(2)}) async-start(bf16[64,40,128]{2,1,0:T(8,128)(2,1)} %weight.1), calls=%async_computation.4 | async-start | bytes 1310720 | tf_op jit(solution)/shard_map/all_to_all | solution.py:309
  135.9 9.4 %collective-permute-start.14 = (f32[2,112,128]{2,1,0:T(8,128)}, f32[2,112,128]{2,1,0:T(8,128)S(1)}, u32[]{:S(2)}, u32[]{:S(2)}) collective-permute-start(f32[2,112,128]{2,1,0:T(8,128)} %get-tuple-element.71), channel_id=1, source_target_pairs={{0,2},{2,4},{4,6},{6,0},{1,3},{3,5},{5,7},{7,1},{8,10},{10,12},{12... | collective-permute-start | bytes 344072 | tf_op jit(solution)/shard_map/ppermute | solution.py:229
  138.4 8.4 %collective-permute-start.15 = (f32[2,112,128]{2,1,0:T(8,128)}, f32[2,112,128]{2,1,0:T(8,128)S(1)}, u32[]{:S(2)}, u32[]{:S(2)}) collective-permute-start(f32[2,112,128]{2,1,0:T(8,128)} %get-tuple-element.72), channel_id=1, source_target_pairs={{0,6},{2,0},{4,2},{6,4},{1,7},{3,1},{5,3},{7,5},{8,14},{10,8},{12,... | collective-permute-start | bytes 344072 | tf_op jit(solution)/shard_map/ppermute | solution.py:229
  142.9 8.4 %collective-permute-start.16 = (f32[2,112,128]{2,1,0:T(8,128)}, f32[2,112,128]{2,1,0:T(8,128)S(1)}, u32[]{:S(2)}, u32[]{:S(2)}) collective-permute-start(f32[2,112,128]{2,1,0:T(8,128)} %get-tuple-element.73), channel_id=1, source_target_pairs={{0,4},{2,6},{4,0},{6,2},{1,5},{3,7},{5,1},{7,3},{8,12},{10,14},{12... | collective-permute-start | bytes 344072 | tf_op jit(solution)/shard_map/ppermute | solution.py:229
  (14 other events, 47.7 us)

commit v8 on v7

--- a/solution.py
+++ b/solution.py
@@ -80,53 +80,72 @@
     return z * cdf, cdf + z * jnp.exp(-0.5 * z * z) * (1.0 / math.sqrt(2.0 * math.pi))
 
 
-def pairs(refs, rows=slice(0, D)):
+def room(shape):
+    return [pltpu.VMEM(shape, BF), pltpu.VMEM(shape, BF), pltpu.SemaphoreType.DMA((2,))]
+
+
+def fetch(sources, targets, sems):
+    copies = [
+        pltpu.make_async_copy(src, dst, sems.at[i])
+        for i, (src, dst) in enumerate(zip(sources, targets))
+    ]
+    for copy in copies:
+        copy.start()
+    return copies
+
+
+def pairs(refs, rows=slice(0, D), copies=None):
     for a in range(2):
+        if copies:
+            copies[a].wait()
         for k in (0, 2):
             both = [refs[a][k, rows, :], refs[a][k + 1, rows, :]]
             yield jnp.concatenate(both, axis=1), 4 * a + k
 
 
-def layer(idx, value, refs, pre):
-    for both, at in pairs(refs):
+def layer(idx, value, refs, pre, copies):
+    for both, at in pairs(refs, copies=copies):
         z = dot(value, both, 1, 0)
         pre[:, lanes(idx[at])] = z[:, :128]
         pre[:, lanes(idx[at + 1])] = z[:, 128:]
     return gelu_parts(pre[...])
 
 
-def back_through(idx, grad, refs, rows=slice(0, D)):
+def back_through(idx, grad, refs, copies):
     total = None
-    for both, at in pairs(refs, rows):
+    for both, at in pairs(refs, copies=copies):
         left = jnp.concatenate([grad[:, lanes(idx[at])], grad[:, lanes(idx[at + 1])]], axis=1)
         term = dot(left, both, 1, 1)
         total = term if total is None else total + term
     return total
 
 
-def first_body(idx, given, near, far, tokhid, slope1, pre):
+def first_body(idx, given, near_at, far_at, tokhid, slope1, pre, near, far, sems):
+    copies = fetch((near_at, far_at), (near, far), sems)
     for j in range(8):
         tokhid[:, 128 * j : 128 * (j + 1)] = given[j, :OWN, :]
-    hidden, slope = layer(idx, tokhid[:, :D], (near, far), pre)
+    hidden, slope = layer(idx, tokhid[:, :D], (near, far), pre, copies)
     tokhid[:, D:] = hidden.astype(BF)
     slope1[...] = slope
 
 
 def second_body(
-    idx, tokhid, given, near, far, land, weights, xh, slope2, me, sums, head, pre, goal
+    idx, tokhid, given, near_at, far_at, land, weights,
+    xh, slope2, me, sums, head, pre, goal, near, far, sems,
 ):
+    copies = fetch((near_at, far_at), (near, far), sems)
     for j in range(8):
         parts = [
             given[j, OWN + HEAD * p : OWN + HEAD * (p + 1), :].astype(F32) for p in range(3)
         ]
         goal[HEAD * j : HEAD * (j + 1), :] = parts[0] + (parts[1] + parts[2])
+    hidden, slope = layer(idx, tokhid[:, D:], (near, far), pre, copies)
     for a, ref in enumerate((near, far)):
         for s in range(4):
             rows = pl.ds(pl.multiple_of(idx[4 * a + s] * HEAD, HEAD), HEAD)
             for i in range(8):
                 piece = ref[s, D + HEAD * i : D + HEAD * (i + 1), :]
                 head[rows, 128 * i : 128 * (i + 1)] = piece
-    hidden, slope = layer(idx, tokhid[:, D:], (near, far), pre)
     hidden2 = hidden.astype(BF)
     xh[0] = tokhid[:, :HALF]
     xh[1, :, : 2 * D - HALF] = tokhid[:, HALF:]
@@ -158,8 +177,10 @@
 
 
 def backward_body(
-    idx, scale, sums, me, slope1, slope2, head, near, far, joined, grad1, loss, g2
+    idx, scale, sums, me, slope1, slope2, head, near_at, far_at,
+    joined, grad1, loss, g2, near, far, sems,
 ):
+    copies = fetch((near_at, far_at), (near, far), sems)
     total = over_cells(jnp.sum(sums[...], axis=0))
     column = lax.broadcasted_iota(jnp.int32, (1, COLS), 1)
     real = column % HEAD < V * PP // 8
@@ -169,7 +190,7 @@
     coef = jnp.where(real, scale[0] / (V * root * weight), 0.0)
     grad_pred = (coef * me[...]).astype(BF)
     g2[...] = (dot(grad_pred, head[...], 1, 0) * slope2[...]).astype(BF)
-    back = back_through(idx, g2, (near, far))
+    back = back_through(idx, g2, (near, far), copies)
     grad1[...] = (back * slope1[...]).astype(BF)
     for j in range(8):
         joined[j, :, :128] = g2[:, 128 * j : 128 * (j + 1)]
@@ -206,19 +227,19 @@
             out[rows, :] = ref[a]
 
 
-def weight_body(idx, near, far, joined, out, order):
+def weight_body(idx, near_at, far_at, joined, out, order, near, far, sems):
+    copies = fetch((near_at, far_at), (near, far), sems)
     for at in range(8):
         order[OWN * at : OWN * (at + 1), :] = joined[idx[at]]
     half = 4 * OWN
-    sums = []
-    places = (((1, 0, 512), (0, D, HALF)), ((0, 0, D),), ((1, 512, HALF),))
-    for to, cuts in zip((0, 128, 256), (places[0][::-1], places[1], places[2])):
-        found = []
-        for h, lo, hi in cuts:
-            term = dot(order[:half, to : to + 128], near[:, h, :, lo:hi].reshape(half, hi - lo), 0, 0)
-            term += dot(order[half:, to : to + 128], far[:, h, :, lo:hi].reshape(half, hi - lo), 0, 0)
-            found.append(term.T)
-        sums.append(found[0] if len(found) == 1 else jnp.concatenate(found, axis=0))
+    cuts = ((0, 0, D, HALF), (0, 1, 0, 512), (128, 0, 0, D), (256, 1, 512, HALF))
+    found = [0.0] * 4
+    for copy, ref, left in ((copies[0], near, order[:half]), (copies[1], far, order[half:])):
+        copy.wait()
+        for i, (to, h, lo, hi) in enumerate(cuts):
+            right = ref[:, h, :, lo:hi].reshape(half, hi - lo)
+            found[i] = found[i] + dot(left[:, to : to + 128], right, 0, 0)
+    sums = [jnp.concatenate([found[0].T, found[1].T], axis=0), found[2].T, found[3].T]
     part = sums[2].reshape(64, 2, 8, 128)
     high = pltpu.roll(part[:, 1].reshape(512, 128), HEAD, 1).reshape(64, 8, 128)
     wide = [sums[0].reshape(64, 16, 128), sums[1].reshape(64, 16, 128), part[:, 0] + high]
@@ -270,14 +291,15 @@
 
     tokhid, slope1 = call(
         first_body, "first", [((OWN, 2 * D), BF), ((OWN, D), F32)], [idx, given, near1, far1],
-        smem=(0,), scratch=[pltpu.VMEM((OWN, D), F32)], flops=FIRST,
+        smem=(0,), loose=(2, 3),
+        scratch=[pltpu.VMEM((OWN, D), F32), *room((4, D, 128))], flops=FIRST,
     )
     xh, slope2, me, sums, head = call(
         second_body, "second",
         [((2, OWN, HALF), BF), ((OWN, D), F32), ((OWN, COLS), F32), ((8, 2, COLS), F32),
          ((COLS, D), BF)],
-        [idx, tokhid, given, near2, far2, land, weights], smem=(0,),
-        scratch=[pltpu.VMEM((OWN, D), F32), pltpu.VMEM((COLS, 128), F32)], flops=5 * 10**8,
+        [idx, tokhid, given, near2, far2, land, weights], smem=(0,), loose=(3, 4), flops=5 * 10**8,
+        scratch=[pltpu.VMEM((OWN, D), F32), pltpu.VMEM((COLS, 128), F32), *room((4, D + COLS, 128))],
     )
 
     sums = lax.all_to_all(sums, TENSOR, 0, 0, tiled=True)
@@ -294,12 +316,14 @@
         backward_body, "backward",
         [((8, OWN, 384), BF), ((OWN, D), BF), ((1, 1), F32)],
         [idx, loss_scale.reshape(1), sums, me, slope1, slope2, head, near2, far2],
-        smem=(0, 1), scratch=[pltpu.VMEM((OWN, D), BF)], flops=BACK,
+        smem=(0, 1), loose=(7, 8), flops=BACK,
+        scratch=[pltpu.VMEM((OWN, D), BF), *room((4, D + COLS, 128))],
     )
     joined = lax.all_to_all(joined, TENSOR, 0, 0, tiled=True)
     (out,) = call(
         weight_body, "weight", [((64, 40, 128), BF)], [idx, xhn, xhf, joined], smem=(0,),
-        scratch=[pltpu.VMEM((8 * OWN, 384), BF)], flops=8 * 10**8,
+        loose=(1, 2), flops=8 * 10**8,
+        scratch=[pltpu.VMEM((8 * OWN, 384), BF), *room((4, 2, OWN, HALF))],
     )
     keep, send = call(
         token_body, "token", [((4, OWN, 128), F32)] * 2, [idx, grad1, near1, far1], smem=(0,),

time: 158 us -> 161 us (1.019)
  Pallas kernels: 26.5 us -> 29.3 us
    pallas_call x8, Pallas kernels: 26.5 us -> 29.3 us  [call(): pl.pallas_call(body, name=name, out_shape=tuple((jax.ShapeDtypeStruct(s,...]
  transfers between devices with their start and end apart: 21 -> 21, of which waited for: 7 -> 7; matrix products, arithmetic and copies ran while one was open for 3% -> 3% of each run, Pallas kernels for 14% -> 15%
where the time goes in v8:
time: 161 us; the launch traced here: 160 us
  starting transfers between devices  82.4 us (51%)
  Pallas kernels  29.3 us (18%)
  waiting for transfers between devices  25.5 us (16%)
  blocking collectives  8.98 us (6%)
  local copies, waits for them, and re-layouts  8.17 us (5%)
  other arithmetic  3.89 us (2%)
  between operations  1.84 us (1%)
    ppermute x13, starting transfers between devices, shift(): return lax.ppermute(v, 'x', [(i, (i + by) % 4) for i in range(4)])  42.4 us
    pallas_call x8, Pallas kernels, call(): pl.pallas_call(body, name=name, out_shape=tuple((jax.ShapeDtypeStruct(s,...  29.3 us
    all_to_all x1, starting transfers between devices, per_device(): sums = lax.all_to_all(spread, SPACE, 0, 0, tiled=True)  16.6 us
    ppermute x13, waiting for transfers between devices, shift(): return lax.ppermute(v, 'x', [(i, (i + by) % 4) for i in range(4)])  15.5 us
    all_to_all x1, blocking collectives, per_device(): sums = lax.all_to_all(sums, TENSOR, 0, 0, tiled=True)  8.98 us
    ppermute x4, starting transfers between devices, flip(): return lax.ppermute(v, 'core', [(0, 1), (1, 0)])  8.65 us
    all_to_all x1, starting transfers between devices, per_device(): out = lax.all_to_all(out, SPACE, 0, 0, tiled=True)  7.41 us
    all_to_all x1, waiting for transfers between devices, per_device(): sums = lax.all_to_all(spread, SPACE, 0, 0, tiled=True)  6.16 us
  transfers between devices with their start and end apart: 21, of which 7 were waited for; matrix products, arithmetic and copies ran while one was open for 3% of the time, Pallas kernels for 15%

profile of v8, /device:TPU:8, one launch (start us, length us, event | category | flops | bytes accessed | tf_op | source)
XLA Modules:
  0.0 160.0 jit_solution(18374473358800716193)
XLA Ops:
  0.6 3.5 %collective-permute-start = (bf16[1024,128]{1,0:T(8,128)(2,1)}, bf16[1024,128]{1,0:T(8,128)(2,1)S(1)}, u32[]{:S(2)}, u32[]{:S(2)}) collective-permute-start(bf16[1024,128]{1,0:T(8,128)(2,1)} %param.9), channel_id=1, source_target_pairs={{0,2},{2,4},{4,6},{6,0},{1,3},{3,5},{5,7},{7,1},{8,10},{10,12},{12... | collective-permute-start | bytes 786440 | tf_op jit(solution)/shard_map/ppermute | solution.py:250
  6.4 3.6 %collective-permute-start.3 = (bf16[1408,128]{1,0:T(8,128)(2,1)}, bf16[1408,128]{1,0:T(8,128)(2,1)S(1)}, u32[]{:S(2)}, u32[]{:S(2)}) collective-permute-start(bf16[1408,128]{1,0:T(8,128)(2,1)} %get-tuple-element.42), channel_id=1, source_target_pairs={{0,6},{2,0},{4,2},{6,4},{1,7},{3,1},{5,3},{7,5},{8,14},{10,8},{12,... | collective-permute-start | bytes 1081352 | tf_op jit(solution)/shard_map/ppermute | solution.py:250
  12.3 4.9 %collective-permute-start.1 = (bf16[1024,128]{1,0:T(8,128)(2,1)}, bf16[1024,128]{1,0:T(8,128)(2,1)S(1)}, u32[]{:S(2)}, u32[]{:S(2)}) collective-permute-start(bf16[1024,128]{1,0:T(8,128)(2,1)} %param.9), channel_id=1, source_target_pairs={{0,6},{2,0},{4,2},{6,4},{1,7},{3,1},{5,3},{7,5},{8,14},{10,8},{12,... | collective-permute-start | bytes 786440 | tf_op jit(solution)/shard_map/ppermute | solution.py:250
  19.2 3.6 %all-to-all-start = ((bf16[8,256,128]{2,1,0:T(8,128)(2,1)}), bf16[8,256,128]{2,1,0:T(8,128)(2,1)S(1)}, u32[]{:S(2)}, u32[]{:S(2)}) async-start(bf16[8,256,128]{2,1,0:T(8,128)(2,1)} %get-tuple-element.46), calls=%async_computation | async-start | bytes 1048576 | tf_op jit(solution)/shard_map/all_to_all | solution.py:282
  24.0 4.9 %collective-permute-start.5 = (bf16[1408,128]{1,0:T(8,128)(2,1)S(1)}, bf16[1408,128]{1,0:T(8,128)(2,1)S(1)}, u32[]{:S(2)}, u32[]{:S(2)}) collective-permute-start(bf16[1408,128]{1,0:T(8,128)(2,1)S(1)} %collective-permute-done.3), channel_id=1, source_target_pairs={{0,6},{2,0},{4,2},{6,4},{1,7},{3,1},{5,3},{7,5},{8,14},{10,8},{12,... | collective-permute-start | bytes 1081352 | tf_op jit(solution)/shard_map/ppermute | solution.py:250
  30.8 9.0 %collective-permute-done.4 = bf16[1024,128]{1,0:T(8,128)(2,1)S(1)} collective-permute-done((bf16[1024,128]{1,0:T(8,128)(2,1)S(1)}, bf16[1024,128]{1,0:T(8,128)(2,1)S(1)}, u32[]{:S(2)}, u32[]{:S(2)}) %collective-permute-start.4) | collective-permute-done | bytes 262176 | tf_op jit(solution)/shard_map/ppermute | solution.py:250
  42.1 2.4 %collective-permute-start.7 = (bf16[4,1408,128]{2,1,0:T(8,128)(2,1)S(1)}, bf16[4,1408,128]{2,1,0:T(8,128)(2,1)S(1)}, u32[]{:S(2)}, u32[]{:S(2)}) collective-permute-start(bf16[4,1408,128]{2,1,0:T(8,128)(2,1)S(1)} %pad_maximum_fusion.1.near_at), channel_id=1, source_target_pairs={{0,1},{1,0},{2,3},{3,2},{4,5},{5,4},{6,7},{7,6},{8,9},{9,8},{10,11... | collective-permute-start | bytes 4325384 | tf_op jit(solution)/shard_map/ppermute | solution.py:254
  45.5 4.1 %first.1 = (bf16[112,2048]{1,0:T(8,128)(2,1)}, f32[112,1024]{1,0:T(8,128)}) custom-call(s32[10]{0:T(128)} %stack.97.idx, bf16[8,256,128]{2,1,0:T(8,128)(2,1)} %copy-done.3, bf16[4,1024,128]{2,1,0:T(8,128)(2,1)} %copy-done.9, bf16[4,1024,128]{2,1,0:T(8,128)(2,1)} %copy-done.16), custom_call_target="tpu_custom_call" | custom-call | flops 20000000000 | bytes 4194304 | tf_op jit(solution)/shard_map/first/pallas_call | solution.py:45
  50.8 5.0 %second.3 = (bf16[2,112,1536]{2,1,0:T(8,128)(2,1)}, f32[112,1024]{1,0:T(8,128)}, f32[112,384]{1,0:T(8,128)}, f32[8,2,384]{2,1,0:T(2,128)}, bf16[384,1024]{1,0:T(8,128)(2,1)}) custom-call(s32[10]{0:T(128)} %stack.97.idx, bf16[112,2048]{1,0:T(8,128)(2,1)} %get-tuple-element.50.tokhid, bf16[8,256,128]{2,1,0:T(8,128)(2,1)} %copy-done.3, ...), custom_call_target="tpu_custom_call" | custom-call | flops 500000000 | bytes 4194304 | tf_op jit(solution)/shard_map/second/pallas_call | solution.py:45
  55.8 9.0 %all_to_all.25 = f32[8,2,384]{2,1,0:T(2,128)S(1)} all-to-all(f32[8,2,384]{2,1,0:T(2,128)} %get-tuple-element.55), channel_id=1, replica_groups=mesh['z'=8,'y'=8,'x'=4,'core'=2] {'x','core'}, dimensions={0} | all-to-all | bytes 49152 | tf_op jit(solution)/shard_map/all_to_all | solution.py:305
  64.8 3.1 %collective-permute-start.10 = (bf16[2,112,1536]{2,1,0:T(8,128)(2,1)}, bf16[2,112,1536]{2,1,0:T(8,128)(2,1)S(1)}, u32[]{:S(2)}, u32[]{:S(2)}) collective-permute-start(bf16[2,112,1536]{2,1,0:T(8,128)(2,1)} %get-tuple-element.66), channel_id=1, source_target_pairs={{0,6},{2,0},{4,2},{6,4},{1,7},{3,1},{5,3},{7,5},{8,14},{10,8},{12,... | collective-permute-start | bytes 2064392 | tf_op jit(solution)/shard_map/ppermute | solution.py:250
  67.9 2.8 %collective-permute-start.9 = (bf16[2,112,1536]{2,1,0:T(8,128)(2,1)}, bf16[2,112,1536]{2,1,0:T(8,128)(2,1)S(1)}, u32[]{:S(2)}, u32[]{:S(2)}) collective-permute-start(bf16[2,112,1536]{2,1,0:T(8,128)(2,1)} %get-tuple-element.66), channel_id=1, source_target_pairs={{0,2},{2,4},{4,6},{6,0},{1,3},{3,5},{5,7},{7,1},{8,10},{10,12},{12... | collective-permute-start | bytes 2064392 | tf_op jit(solution)/shard_map/ppermute | solution.py:250
  72.0 16.6 %all-to-all-start.2 = ((f32[64,2,384]{2,1,0:T(2,128)}), f32[64,2,384]{2,1,0:T(2,128)S(1)}, u32[]{:S(2)}, u32[]{:S(2)}) async-start(f32[64,2,384]{2,1,0:T(2,128)} %broadcast_in_dim.9), calls=%async_computation.2 | async-start | bytes 393216 | tf_op jit(solution)/shard_map/all_to_all | solution.py:308
  88.7 4.3 %collective-permute-start.12 = (bf16[112,1536]{1,0:T(8,128)(2,1)S(1)}, bf16[112,1536]{1,0:T(8,128)(2,1)S(1)}, u32[]{:S(2)}, u32[]{:S(2)}) collective-permute-start(bf16[112,1536]{1,0:T(8,128)(2,1)S(1)} %slice_bitcast_fusion), channel_id=1, source_target_pairs={{0,6},{2,0},{4,2},{6,4},{1,7},{3,1},{5,3},{7,5},{8,14},{10,8},{12,... | collective-permute-start | bytes 1032200 | tf_op jit(solution)/shard_map/ppermute | solution.py:250
  94.9 6.2 %all-to-all-done.2.sums = f32[64,2,384]{2,1,0:T(2,128)S(1)} async-done(((f32[64,2,384]{2,1,0:T(2,128)}), f32[64,2,384]{2,1,0:T(2,128)S(1)}, u32[]{:S(2)}, u32[]{:S(2)}) %all-to-all-start.2) | async-done | bytes 196640 | tf_op jit(solution)/shard_map/all_to_all | solution.py:308
  101.8 5.1 %backward.1 = (bf16[8,112,384]{2,1,0:T(8,128)(2,1)}, bf16[112,1024]{1,0:T(8,128)(2,1)}, f32[1,1]{1,0:T(1,128)}) custom-call(s32[10]{0:T(128)} %stack.97.idx, f32[1]{0:T(128)} %bitcast.33.scale, f32[64,2,384]{2,1,0:T(2,128)} %copy-done.12, f32[112,384]{1,0:T(8,128)} %get-tuple-element.58.me, f32[112,1024]{1,0:T(8,128)} %get-tuple-element.59.slope1, ...), custom_call_target="tpu_custom_call" | custom-call | flops 30000001024 | bytes 4194304 | tf_op jit(solution)/shard_map/backward/pallas_call | solution.py:45
  106.9 3.7 %all-to-all-start.3 = ((bf16[8,112,384]{2,1,0:T(8,128)(2,1)}), bf16[8,112,384]{2,1,0:T(8,128)(2,1)S(1)}, u32[]{:S(2)}, u32[]{:S(2)}) async-start(bf16[8,112,384]{2,1,0:T(8,128)(2,1)} %get-tuple-element.67), calls=%async_computation.3 | async-start | bytes 1376256 | tf_op jit(solution)/shard_map/all_to_all | solution.py:322
  113.2 2.4 %collective-permute-start.13 = (bf16[4,2,112,1536]{3,2,1,0:T(8,128)(2,1)S(1)}, bf16[4,2,112,1536]{3,2,1,0:T(8,128)(2,1)}, u32[]{:S(2)}, u32[]{:S(2)}) collective-permute-start(bf16[4,2,112,1536]{3,2,1,0:T(8,128)(2,1)S(1)} %pad_maximum_fusion.near_at), channel_id=1, source_target_pairs={{0,1},{1,0},{2,3},{3,2},{4,5},{5,4},{6,7},{7,6},{8,9},{9,8},{10,11... | collective-permute-start | bytes 8257544 | tf_op jit(solution)/shard_map/ppermute | solution.py:254
  115.7 3.2 %token_.1 = (f32[4,112,128]{2,1,0:T(8,128)}, f32[4,112,128]{2,1,0:T(8,128)}) custom-call(s32[10]{0:T(128)} %stack.97.idx, bf16[112,1024]{1,0:T(8,128)(2,1)} %get-tuple-element.63.grad1, bf16[4,1024,128]{2,1,0:T(8,128)(2,1)} %copy-done.9, bf16[4,1024,128]{2,1,0:T(8,128)(2,1)} %copy-done.16), custom_call_target="tpu_custom_call" | custom-call | flops 30000001024 | bytes 4194304 | tf_op jit(solution)/shard_map/token/pallas_call | solution.py:45
  123.5 5.8 %weight.1 = bf16[64,40,128]{2,1,0:T(8,128)(2,1)} custom-call(s32[10]{0:T(128)} %stack.97.idx, bf16[4,2,112,1536]{3,2,1,0:T(8,128)(2,1)} %copy-done, bf16[4,2,112,1536]{3,2,1,0:T(8,128)(2,1)} %collective-permute-done.13.far_at, bf16[8,112,384]{2,1,0:T(8,128)(2,1)} %copy-done.2), custom_call_target="tpu_custom_call" | custom-call | flops 800000000 | bytes 4194304 | tf_op jit(solution)/shard_map/weight/pallas_call | solution.py:45
  129.4 7.4 %all-to-all-start.4 = ((bf16[64,40,128]{2,1,0:T(8,128)(2,1)}), bf16[64,40,128]{2,1,0:T(8,128)(2,1)S(1)}, u32[]{:S(2)}, u32[]{:S(2)}) async-start(bf16[64,40,128]{2,1,0:T(8,128)(2,1)} %weight.1), calls=%async_computation.4 | async-start | bytes 1310720 | tf_op jit(solution)/shard_map/all_to_all | solution.py:333
  138.7 2.5 %collective-permute-start.14 = (f32[2,112,128]{2,1,0:T(8,128)}, f32[2,112,128]{2,1,0:T(8,128)S(1)}, u32[]{:S(2)}, u32[]{:S(2)}) collective-permute-start(f32[2,112,128]{2,1,0:T(8,128)} %get-tuple-element.71), channel_id=1, source_target_pairs={{0,2},{2,4},{4,6},{6,0},{1,3},{3,5},{5,7},{7,1},{8,10},{10,12},{12... | collective-permute-start | bytes 344072 | tf_op jit(solution)/shard_map/ppermute | solution.py:250
  141.2 4.6 %collective-permute-start.15 = (f32[2,112,128]{2,1,0:T(8,128)}, f32[2,112,128]{2,1,0:T(8,128)S(1)}, u32[]{:S(2)}, u32[]{:S(2)}) collective-permute-start(f32[2,112,128]{2,1,0:T(8,128)} %get-tuple-element.72), channel_id=1, source_target_pairs={{0,6},{2,0},{4,2},{6,4},{1,7},{3,1},{5,3},{7,5},{8,14},{10,8},{12,... | collective-permute-start | bytes 344072 | tf_op jit(solution)/shard_map/ppermute | solution.py:250
  149.6 4.5 %collective-permute-done.16.across = f32[2,112,128]{2,1,0:T(8,128)S(1)} collective-permute-done((f32[2,112,128]{2,1,0:T(8,128)}, f32[2,112,128]{2,1,0:T(8,128)S(1)}, u32[]{:S(2)}, u32[]{:S(2)}) %collective-permute-start.16) | collective-permute-done | bytes 114720 | tf_op jit(solution)/shard_map/ppermute | solution.py:250
  (77 shorter events, 36.1 us)
Async XLA Ops:
  0.6 39.1 %copy-start.11 = (bf16[1024,128]{1,0:T(8,128)(2,1)S(1)}, bf16[1024,128]{1,0:T(8,128)(2,1)}, u32[]{:S(2)}) copy-start(bf16[1024,128]{1,0:T(8,128)(2,1)} %param.9) | copy-start | bytes 786436
  0.6 18.6 %collective-permute-start = (bf16[1024,128]{1,0:T(8,128)(2,1)}, bf16[1024,128]{1,0:T(8,128)(2,1)S(1)}, u32[]{:S(2)}, u32[]{:S(2)}) collective-permute-start(bf16[1024,128]{1,0:T(8,128)(2,1)} %param.9), channel_id=1, source_target_pairs={{0,2},{2,4},{4,6},{6,0},{1,3},{3,5},{5,7},{7,1},{8,10},{10,12},{12... | collective-permute-start | bytes 786440 | tf_op jit(solution)/shard_map/ppermute | solution.py:250
  6.4 17.6 %collective-permute-start.3 = (bf16[1408,128]{1,0:T(8,128)(2,1)}, bf16[1408,128]{1,0:T(8,128)(2,1)S(1)}, u32[]{:S(2)}, u32[]{:S(2)}) collective-permute-start(bf16[1408,128]{1,0:T(8,128)(2,1)} %get-tuple-element.42), channel_id=1, source_target_pairs={{0,6},{2,0},{4,2},{6,4},{1,7},{3,1},{5,3},{7,5},{8,14},{10,8},{12,... | collective-permute-start | bytes 1081352 | tf_op jit(solution)/shard_map/ppermute | solution.py:250
  10.1 13.9 %collective-permute-start.2 = (bf16[1408,128]{1,0:T(8,128)(2,1)}, bf16[1408,128]{1,0:T(8,128)(2,1)S(1)}, u32[]{:S(2)}, u32[]{:S(2)}) collective-permute-start(bf16[1408,128]{1,0:T(8,128)(2,1)} %get-tuple-element.42), channel_id=1, source_target_pairs={{0,2},{2,4},{4,6},{6,0},{1,3},{3,5},{5,7},{7,1},{8,10},{10,12},{12... | collective-permute-start | bytes 1081352 | tf_op jit(solution)/shard_map/ppermute | solution.py:250
  12.3 11.7 %collective-permute-start.1 = (bf16[1024,128]{1,0:T(8,128)(2,1)}, bf16[1024,128]{1,0:T(8,128)(2,1)S(1)}, u32[]{:S(2)}, u32[]{:S(2)}) collective-permute-start(bf16[1024,128]{1,0:T(8,128)(2,1)} %param.9), channel_id=1, source_target_pairs={{0,6},{2,0},{4,2},{6,4},{1,7},{3,1},{5,3},{7,5},{8,14},{10,8},{12,... | collective-permute-start | bytes 786440 | tf_op jit(solution)/shard_map/ppermute | solution.py:250
  19.2 22.7 %copy-start.10 = (bf16[1408,128]{1,0:T(8,128)(2,1)S(1)}, bf16[1408,128]{1,0:T(8,128)(2,1)}, u32[]{:S(2)}) copy-start(bf16[1408,128]{1,0:T(8,128)(2,1)} %get-tuple-element.42) | copy-start | bytes 1081348
  19.2 20.6 %all-to-all-start = ((bf16[8,256,128]{2,1,0:T(8,128)(2,1)}), bf16[8,256,128]{2,1,0:T(8,128)(2,1)S(1)}, u32[]{:S(2)}, u32[]{:S(2)}) async-start(bf16[8,256,128]{2,1,0:T(8,128)(2,1)} %get-tuple-element.46), calls=%async_computation | async-start | bytes 1048576 | tf_op jit(solution)/shard_map/all_to_all | solution.py:282
  24.0 15.8 %collective-permute-start.5 = (bf16[1408,128]{1,0:T(8,128)(2,1)S(1)}, bf16[1408,128]{1,0:T(8,128)(2,1)S(1)}, u32[]{:S(2)}, u32[]{:S(2)}) collective-permute-start(bf16[1408,128]{1,0:T(8,128)(2,1)S(1)} %collective-permute-done.3), channel_id=1, source_target_pairs={{0,6},{2,0},{4,2},{6,4},{1,7},{3,1},{5,3},{7,5},{8,14},{10,8},{12,... | collective-permute-start | bytes 1081352 | tf_op jit(solution)/shard_map/ppermute | solution.py:250
  28.9 10.9 %collective-permute-start.4 = (bf16[1024,128]{1,0:T(8,128)(2,1)S(1)}, bf16[1024,128]{1,0:T(8,128)(2,1)S(1)}, u32[]{:S(2)}, u32[]{:S(2)}) collective-permute-start(bf16[1024,128]{1,0:T(8,128)(2,1)S(1)} %collective-permute-done), channel_id=1, source_target_pairs={{0,2},{2,4},{4,6},{6,0},{1,3},{3,5},{5,7},{7,1},{8,10},{10,12},{12... | collective-permute-start | bytes 786440 | tf_op jit(solution)/shard_map/ppermute | solution.py:250
  39.9 4.6 %collective-permute-start.6 = (bf16[4,1024,128]{2,1,0:T(8,128)(2,1)S(1)}, bf16[4,1024,128]{2,1,0:T(8,128)(2,1)S(1)}, u32[]{:S(2)}, u32[]{:S(2)}) collective-permute-start(bf16[4,1024,128]{2,1,0:T(8,128)(2,1)S(1)} %pad_maximum_fusion.2.near_at.near), channel_id=1, source_target_pairs={{0,1},{1,0},{2,3},{3,2},{4,5},{5,4},{6,7},{7,6},{8,9},{9,8},{10,11... | collective-permute-start | bytes 3145736 | tf_op jit(solution)/shard_map/ppermute | solution.py:254
  42.1 7.6 %collective-permute-start.7 = (bf16[4,1408,128]{2,1,0:T(8,128)(2,1)S(1)}, bf16[4,1408,128]{2,1,0:T(8,128)(2,1)S(1)}, u32[]{:S(2)}, u32[]{:S(2)}) collective-permute-start(bf16[4,1408,128]{2,1,0:T(8,128)(2,1)S(1)} %pad_maximum_fusion.1.near_at), channel_id=1, source_target_pairs={{0,1},{1,0},{2,3},{3,2},{4,5},{5,4},{6,7},{7,6},{8,9},{9,8},{10,11... | collective-permute-start | bytes 4325384 | tf_op jit(solution)/shard_map/ppermute | solution.py:254
  64.8 23.8 %collective-permute-start.10 = (bf16[2,112,1536]{2,1,0:T(8,128)(2,1)}, bf16[2,112,1536]{2,1,0:T(8,128)(2,1)S(1)}, u32[]{:S(2)}, u32[]{:S(2)}) collective-permute-start(bf16[2,112,1536]{2,1,0:T(8,128)(2,1)} %get-tuple-element.66), channel_id=1, source_target_pairs={{0,6},{2,0},{4,2},{6,4},{1,7},{3,1},{5,3},{7,5},{8,14},{10,8},{12,... | collective-permute-start | bytes 2064392 | tf_op jit(solution)/shard_map/ppermute | solution.py:250
  67.9 25.1 %collective-permute-start.9 = (bf16[2,112,1536]{2,1,0:T(8,128)(2,1)}, bf16[2,112,1536]{2,1,0:T(8,128)(2,1)S(1)}, u32[]{:S(2)}, u32[]{:S(2)}) collective-permute-start(bf16[2,112,1536]{2,1,0:T(8,128)(2,1)} %get-tuple-element.66), channel_id=1, source_target_pairs={{0,2},{2,4},{4,6},{6,0},{1,3},{3,5},{5,7},{7,1},{8,10},{10,12},{12... | collective-permute-start | bytes 2064392 | tf_op jit(solution)/shard_map/ppermute | solution.py:250
  72.0 29.1 %all-to-all-start.2 = ((f32[64,2,384]{2,1,0:T(2,128)}), f32[64,2,384]{2,1,0:T(2,128)S(1)}, u32[]{:S(2)}, u32[]{:S(2)}) async-start(f32[64,2,384]{2,1,0:T(2,128)} %broadcast_in_dim.9), calls=%async_computation.2 | async-start | bytes 393216 | tf_op jit(solution)/shard_map/all_to_all | solution.py:308
  88.6 18.3 %copy-start.4 = (bf16[2,112,1536]{2,1,0:T(8,128)(2,1)}, bf16[2,112,1536]{2,1,0:T(8,128)(2,1)S(1)}, u32[]{:S(2)}) copy-start(bf16[2,112,1536]{2,1,0:T(8,128)(2,1)S(1)} %collective-permute-done.10) | copy-start | bytes 2064388
  88.7 21.9 %collective-permute-start.12 = (bf16[112,1536]{1,0:T(8,128)(2,1)S(1)}, bf16[112,1536]{1,0:T(8,128)(2,1)S(1)}, u32[]{:S(2)}, u32[]{:S(2)}) collective-permute-start(bf16[112,1536]{1,0:T(8,128)(2,1)S(1)} %slice_bitcast_fusion), channel_id=1, source_target_pairs={{0,6},{2,0},{4,2},{6,4},{1,7},{3,1},{5,3},{7,5},{8,14},{10,8},{12,... | collective-permute-start | bytes 1032200 | tf_op jit(solution)/shard_map/ppermute | solution.py:250
  93.0 17.6 %collective-permute-start.11 = (bf16[112,1536]{1,0:T(8,128)(2,1)S(1)}, bf16[112,1536]{1,0:T(8,128)(2,1)S(1)}, u32[]{:S(2)}, u32[]{:S(2)}) collective-permute-start(bf16[112,1536]{1,0:T(8,128)(2,1)S(1)} %slice_bitcast_fusion.1), channel_id=1, source_target_pairs={{0,2},{2,4},{4,6},{6,0},{1,3},{3,5},{5,7},{7,1},{8,10},{10,12},{12... | collective-permute-start | bytes 1032200 | tf_op jit(solution)/shard_map/ppermute | solution.py:250
  106.9 15.8 %all-to-all-start.3 = ((bf16[8,112,384]{2,1,0:T(8,128)(2,1)}), bf16[8,112,384]{2,1,0:T(8,128)(2,1)S(1)}, u32[]{:S(2)}, u32[]{:S(2)}) async-start(bf16[8,112,384]{2,1,0:T(8,128)(2,1)} %get-tuple-element.67), calls=%async_computation.3 | async-start | bytes 1376256 | tf_op jit(solution)/shard_map/all_to_all | solution.py:322
  113.2 9.4 %collective-permute-start.13 = (bf16[4,2,112,1536]{3,2,1,0:T(8,128)(2,1)S(1)}, bf16[4,2,112,1536]{3,2,1,0:T(8,128)(2,1)}, u32[]{:S(2)}, u32[]{:S(2)}) collective-permute-start(bf16[4,2,112,1536]{3,2,1,0:T(8,128)(2,1)S(1)} %pad_maximum_fusion.near_at), channel_id=1, source_target_pairs={{0,1},{1,0},{2,3},{3,2},{4,5},{5,4},{6,7},{7,6},{8,9},{9,8},{10,11... | collective-permute-start | bytes 8257544 | tf_op jit(solution)/shard_map/ppermute | solution.py:254
  118.9 10.5 %collective-permute-start.8 = (f32[4,112,128]{2,1,0:T(8,128)}, f32[4,112,128]{2,1,0:T(8,128)}, u32[]{:S(2)}, u32[]{:S(2)}) collective-permute-start(f32[4,112,128]{2,1,0:T(8,128)} %get-tuple-element.64), channel_id=1, source_target_pairs={{0,1},{1,0},{2,3},{3,2},{4,5},{5,4},{6,7},{7,6},{8,9},{9,8},{10,11... | collective-permute-start | bytes 688136 | tf_op jit(solution)/shard_map/ppermute | solution.py:254
  129.4 29.2 %all-to-all-start.4 = ((bf16[64,40,128]{2,1,0:T(8,128)(2,1)}), bf16[64,40,128]{2,1,0:T(8,128)(2,1)S(1)}, u32[]{:S(2)}, u32[]{:S(2)}) async-start(bf16[64,40,128]{2,1,0:T(8,128)(2,1)} %weight.1), calls=%async_computation.4 | async-start | bytes 1310720 | tf_op jit(solution)/shard_map/all_to_all | solution.py:333
  138.7 9.4 %collective-permute-start.14 = (f32[2,112,128]{2,1,0:T(8,128)}, f32[2,112,128]{2,1,0:T(8,128)S(1)}, u32[]{:S(2)}, u32[]{:S(2)}) collective-permute-start(f32[2,112,128]{2,1,0:T(8,128)} %get-tuple-element.71), channel_id=1, source_target_pairs={{0,2},{2,4},{4,6},{6,0},{1,3},{3,5},{5,7},{7,1},{8,10},{10,12},{12... | collective-permute-start | bytes 344072 | tf_op jit(solution)/shard_map/ppermute | solution.py:250
  141.2 8.4 %collective-permute-start.15 = (f32[2,112,128]{2,1,0:T(8,128)}, f32[2,112,128]{2,1,0:T(8,128)S(1)}, u32[]{:S(2)}, u32[]{:S(2)}) collective-permute-start(f32[2,112,128]{2,1,0:T(8,128)} %get-tuple-element.72), channel_id=1, source_target_pairs={{0,6},{2,0},{4,2},{6,4},{1,7},{3,1},{5,3},{7,5},{8,14},{10,8},{12,... | collective-permute-start | bytes 344072 | tf_op jit(solution)/shard_map/ppermute | solution.py:250
  145.7 8.4 %collective-permute-start.16 = (f32[2,112,128]{2,1,0:T(8,128)}, f32[2,112,128]{2,1,0:T(8,128)S(1)}, u32[]{:S(2)}, u32[]{:S(2)}) collective-permute-start(f32[2,112,128]{2,1,0:T(8,128)} %get-tuple-element.73), channel_id=1, source_target_pairs={{0,4},{2,6},{4,0},{6,2},{1,5},{3,7},{5,1},{7,3},{8,12},{10,14},{12... | collective-permute-start | bytes 344072 | tf_op jit(solution)/shard_map/ppermute | solution.py:250
  (14 other events, 48.8 us)

commit v9 on v7

--- a/solution.py
+++ b/solution.py
@@ -35,7 +35,7 @@
     return pl.ds(pl.multiple_of(j * 128, 128), 128)
 
 
-def call(body, name, outs, args, smem=(), scratch=(), flops=0, vmem=56, loose=()):
+def call(body, name, outs, args, smem=(), scratch=(), flops=0, vmem=28, loose=()):
     specs = [
         pl.BlockSpec(
             memory_space=pltpu.SMEM if i in smem else pl.ANY if i in loose else pltpu.VMEM

time: 158 us -> 161 us (1.019)
  Pallas kernels: 26.5 us -> 14.6 us
  local copies, waits for them, and re-layouts: 8.18 us -> 18.7 us
  starting transfers between devices: 82.4 us -> 85.9 us
    pallas_call x8, Pallas kernels: 26.5 us -> 14.6 us  [call(): pl.pallas_call(body, name=name, out_shape=tuple((jax.ShapeDtypeStruct(s,...]
    unnamed x34 -> x48, local copies, waits for them, and re-layouts: 5.51 us -> 13.7 us
    all_to_all x1, starting transfers between devices: 7.41 us -> 10.9 us  [per_device(): out = lax.all_to_all(out, SPACE, 0, 0, tiled=True)]
    squeeze x2, local copies, waits for them, and re-layouts: 0.05 us -> 3.5 us  [per_device(): xh_last = jnp.stack([shift(xh_m1[0], 1), shift(xh_p1[1], 3)])]
    all_to_all x1, waiting for transfers between devices: 6.16 us -> 2.76 us  [per_device(): sums = lax.all_to_all(spread, SPACE, 0, 0, tiled=True)]
    all_to_all x1, waiting for transfers between devices: 1.99 us -> 4.22 us  [per_device(): out = lax.all_to_all(out, SPACE, 0, 0, tiled=True)]
  transfers between devices with their start and end apart: 21 -> 21, of which waited for: 7 -> 8; matrix products, arithmetic and copies ran while one was open for 3% -> 5% of each run, Pallas kernels for 14% -> 8%
where the time goes in v9:
time: 161 us; the launch traced here: 160 us
  starting transfers between devices  85.9 us (53%)
  waiting for transfers between devices  25.5 us (16%)
  local copies, waits for them, and re-layouts  18.7 us (12%)
  Pallas kernels  14.6 us (9%)
  blocking collectives  8.66 us (5%)
  other arithmetic  4.89 us (3%)
  between operations  1.78 us (1%)
    ppermute x13, starting transfers between devices, shift(): return lax.ppermute(v, 'x', [(i, (i + by) % 4) for i in range(4)])  42.6 us
    all_to_all x1, starting transfers between devices, per_device(): sums = lax.all_to_all(spread, SPACE, 0, 0, tiled=True)  16.6 us
    ppermute x13, waiting for transfers between devices, shift(): return lax.ppermute(v, 'x', [(i, (i + by) % 4) for i in range(4)])  15.8 us
    pallas_call x8, Pallas kernels, call(): pl.pallas_call(body, name=name, out_shape=tuple((jax.ShapeDtypeStruct(s,...  14.6 us
    unnamed x48, local copies, waits for them, and re-layouts  13.7 us
    all_to_all x1, starting transfers between devices, per_device(): out = lax.all_to_all(out, SPACE, 0, 0, tiled=True)  10.9 us
    all_to_all x1, blocking collectives, per_device(): sums = lax.all_to_all(sums, TENSOR, 0, 0, tiled=True)  8.66 us
    ppermute x4, starting transfers between devices, flip(): return lax.ppermute(v, 'core', [(0, 1), (1, 0)])  8.65 us
  transfers between devices with their start and end apart: 21, of which 8 were waited for; matrix products, arithmetic and copies ran while one was open for 5% of the time, Pallas kernels for 8%

profile of v9, /device:TPU:8, one launch (start us, length us, event | category | flops | bytes accessed | tf_op | source)
XLA Modules:
  0.0 160.0 jit_solution(10290905293354564055)
XLA Ops:
  0.6 3.4 %collective-permute-start = (bf16[1024,128]{1,0:T(8,128)(2,1)}, bf16[1024,128]{1,0:T(8,128)(2,1)S(1)}, u32[]{:S(2)}, u32[]{:S(2)}) collective-permute-start(bf16[1024,128]{1,0:T(8,128)(2,1)} %param.9), channel_id=1, source_target_pairs={{0,2},{2,4},{4,6},{6,0},{1,3},{3,5},{5,7},{7,1},{8,10},{10,12},{12... | collective-permute-start | bytes 786440 | tf_op jit(solution)/shard_map/ppermute | solution.py:229
  9.9 3.6 %collective-permute-start.3 = (bf16[1408,128]{1,0:T(8,128)(2,1)S(1)}, bf16[1408,128]{1,0:T(8,128)(2,1)S(1)}, u32[]{:S(2)}, u32[]{:S(2)}) collective-permute-start(bf16[1408,128]{1,0:T(8,128)(2,1)S(1)} %get-tuple-element.42), channel_id=1, source_target_pairs={{0,6},{2,0},{4,2},{6,4},{1,7},{3,1},{5,3},{7,5},{8,14},{10,8},{12,... | collective-permute-start | bytes 1081352 | tf_op jit(solution)/shard_map/ppermute | solution.py:229
  13.5 2.2 %collective-permute-start.2 = (bf16[1408,128]{1,0:T(8,128)(2,1)S(1)}, bf16[1408,128]{1,0:T(8,128)(2,1)S(1)}, u32[]{:S(2)}, u32[]{:S(2)}) collective-permute-start(bf16[1408,128]{1,0:T(8,128)(2,1)S(1)} %get-tuple-element.42), channel_id=1, source_target_pairs={{0,2},{2,4},{4,6},{6,0},{1,3},{3,5},{5,7},{7,1},{8,10},{10,12},{12... | collective-permute-start | bytes 1081352 | tf_op jit(solution)/shard_map/ppermute | solution.py:229
  15.7 4.9 %collective-permute-start.1 = (bf16[1024,128]{1,0:T(8,128)(2,1)}, bf16[1024,128]{1,0:T(8,128)(2,1)S(1)}, u32[]{:S(2)}, u32[]{:S(2)}) collective-permute-start(bf16[1024,128]{1,0:T(8,128)(2,1)} %param.9), channel_id=1, source_target_pairs={{0,6},{2,0},{4,2},{6,4},{1,7},{3,1},{5,3},{7,5},{8,14},{10,8},{12,... | collective-permute-start | bytes 786440 | tf_op jit(solution)/shard_map/ppermute | solution.py:229
  21.6 3.5 %all-to-all-start = ((bf16[8,256,128]{2,1,0:T(8,128)(2,1)}), bf16[8,256,128]{2,1,0:T(8,128)(2,1)S(1)}, u32[]{:S(2)}, u32[]{:S(2)}) async-start(bf16[8,256,128]{2,1,0:T(8,128)(2,1)} %get-tuple-element.46), calls=%async_computation | async-start | bytes 1048576 | tf_op jit(solution)/shard_map/all_to_all | solution.py:261
  27.3 5.2 %collective-permute-start.5 = (bf16[1408,128]{1,0:T(8,128)(2,1)S(1)}, bf16[1408,128]{1,0:T(8,128)(2,1)S(1)}, u32[]{:S(2)}, u32[]{:S(2)}) collective-permute-start(bf16[1408,128]{1,0:T(8,128)(2,1)S(1)} %collective-permute-done.3), channel_id=1, source_target_pairs={{0,6},{2,0},{4,2},{6,4},{1,7},{3,1},{5,3},{7,5},{8,14},{10,8},{12,... | collective-permute-start | bytes 1081352 | tf_op jit(solution)/shard_map/ppermute | solution.py:229
  34.4 7.8 %collective-permute-done.4 = bf16[1024,128]{1,0:T(8,128)(2,1)S(1)} collective-permute-done((bf16[1024,128]{1,0:T(8,128)(2,1)S(1)}, bf16[1024,128]{1,0:T(8,128)(2,1)S(1)}, u32[]{:S(2)}, u32[]{:S(2)}) %collective-permute-start.4) | collective-permute-done | bytes 262176 | tf_op jit(solution)/shard_map/ppermute | solution.py:229
  44.5 2.4 %collective-permute-start.7 = (bf16[4,1408,128]{2,1,0:T(8,128)(2,1)S(1)}, bf16[4,1408,128]{2,1,0:T(8,128)(2,1)S(1)}, u32[]{:S(2)}, u32[]{:S(2)}) collective-permute-start(bf16[4,1408,128]{2,1,0:T(8,128)(2,1)S(1)} %pad_maximum_fusion.1.near), channel_id=1, source_target_pairs={{0,1},{1,0},{2,3},{3,2},{4,5},{5,4},{6,7},{7,6},{8,9},{9,8},{10,11... | collective-permute-start | bytes 4325384 | tf_op jit(solution)/shard_map/ppermute | solution.py:233
  49.8 2.4 %second.3 = (bf16[2,112,1536]{2,1,0:T(8,128)(2,1)}, f32[112,1024]{1,0:T(8,128)S(1)}, f32[112,384]{1,0:T(8,128)S(1)}, f32[8,2,384]{2,1,0:T(2,128)S(1)}, bf16[384,1024]{1,0:T(8,128)(2,1)S(1)}) custom-call(s32[10]{0:T(128)S(1)} %stack.97.idx, bf16[112,2048]{1,0:T(8,128)(2,1)S(1)} %get-tuple-element.50.tokhid, bf16[8,256,128]{2,1,0:T(8,128)(2,1)S(1)} %all-to-all-done.given, ...), custom_call_target="tpu_custom_call" | custom-call | flops 500000000 | bytes 4194304 | tf_op jit(solution)/shard_map/second/pallas_call | solution.py:45
  54.5 8.7 %all_to_all.25 = f32[8,2,384]{2,1,0:T(2,128)S(1)} all-to-all(f32[8,2,384]{2,1,0:T(2,128)S(1)} %get-tuple-element.55), channel_id=1, replica_groups=mesh['z'=8,'y'=8,'x'=4,'core'=2] {'x','core'}, dimensions={0} | all-to-all | bytes 49152 | tf_op jit(solution)/shard_map/all_to_all | solution.py:283
  63.2 3.1 %collective-permute-start.10 = (bf16[2,112,1536]{2,1,0:T(8,128)(2,1)}, bf16[2,112,1536]{2,1,0:T(8,128)(2,1)}, u32[]{:S(2)}, u32[]{:S(2)}) collective-permute-start(bf16[2,112,1536]{2,1,0:T(8,128)(2,1)} %get-tuple-element.66), channel_id=1, source_target_pairs={{0,6},{2,0},{4,2},{6,4},{1,7},{3,1},{5,3},{7,5},{8,14},{10,8},{12,... | collective-permute-start | bytes 2064392 | tf_op jit(solution)/shard_map/ppermute | solution.py:229
  66.2 2.8 %collective-permute-start.9 = (bf16[2,112,1536]{2,1,0:T(8,128)(2,1)}, bf16[2,112,1536]{2,1,0:T(8,128)(2,1)}, u32[]{:S(2)}, u32[]{:S(2)}) collective-permute-start(bf16[2,112,1536]{2,1,0:T(8,128)(2,1)} %get-tuple-element.66), channel_id=1, source_target_pairs={{0,2},{2,4},{4,6},{6,0},{1,3},{3,5},{5,7},{7,1},{8,10},{10,12},{12... | collective-permute-start | bytes 2064392 | tf_op jit(solution)/shard_map/ppermute | solution.py:229
  70.4 16.6 %all-to-all-start.2 = ((f32[64,2,384]{2,1,0:T(2,128)}), f32[64,2,384]{2,1,0:T(2,128)S(1)}, u32[]{:S(2)}, u32[]{:S(2)}) async-start(f32[64,2,384]{2,1,0:T(2,128)} %broadcast_in_dim.9), calls=%async_computation.2 | async-start | bytes 393216 | tf_op jit(solution)/shard_map/all_to_all | solution.py:286
  88.8 4.3 %collective-permute-start.12 = (bf16[112,1536]{1,0:T(8,128)(2,1)}, bf16[112,1536]{1,0:T(8,128)(2,1)}, u32[]{:S(2)}, u32[]{:S(2)}) collective-permute-start(bf16[112,1536]{1,0:T(8,128)(2,1)} %slice_bitcast_fusion), channel_id=1, source_target_pairs={{0,6},{2,0},{4,2},{6,4},{1,7},{3,1},{5,3},{7,5},{8,14},{10,8},{12,... | collective-permute-start | bytes 1032200 | tf_op jit(solution)/shard_map/ppermute | solution.py:229
  96.7 2.8 %all-to-all-done.2.sums = f32[64,2,384]{2,1,0:T(2,128)S(1)} async-done(((f32[64,2,384]{2,1,0:T(2,128)}), f32[64,2,384]{2,1,0:T(2,128)S(1)}, u32[]{:S(2)}, u32[]{:S(2)}) %all-to-all-start.2) | async-done | bytes 196640 | tf_op jit(solution)/shard_map/all_to_all | solution.py:286
  106.2 3.6 %all-to-all-start.3 = ((bf16[8,112,384]{2,1,0:T(8,128)(2,1)}), bf16[8,112,384]{2,1,0:T(8,128)(2,1)S(1)}, u32[]{:S(2)}, u32[]{:S(2)}) async-start(bf16[8,112,384]{2,1,0:T(8,128)(2,1)} %copy-done.3), calls=%async_computation.3 | async-start | bytes 1376256 | tf_op jit(solution)/shard_map/all_to_all | solution.py:299
  112.8 2.4 %collective-permute-start.13 = (bf16[4,2,112,1536]{3,2,1,0:T(8,128)(2,1)S(1)}, bf16[4,2,112,1536]{3,2,1,0:T(8,128)(2,1)}, u32[]{:S(2)}, u32[]{:S(2)}) collective-permute-start(bf16[4,2,112,1536]{3,2,1,0:T(8,128)(2,1)S(1)} %pad_maximum_fusion.near), channel_id=1, source_target_pairs={{0,1},{1,0},{2,3},{3,2},{4,5},{5,4},{6,7},{7,6},{8,9},{9,8},{10,11... | collective-permute-start | bytes 8257544 | tf_op jit(solution)/shard_map/ppermute | solution.py:233
  121.9 3.1 %weight.1 = bf16[64,40,128]{2,1,0:T(8,128)(2,1)S(1)} custom-call(s32[10]{0:T(128)S(1)} %stack.97.idx, bf16[4,2,112,1536]{3,2,1,0:T(8,128)(2,1)S(1)} %pad_maximum_fusion.near, bf16[4,2,112,1536]{3,2,1,0:T(8,128)(2,1)} %collective-permute-done.13.far, bf16[8,112,384]{2,1,0:T(8,128)(2,1)S(1)} %all-to-all-done.3.joined), custom_call_target="tpu_custom_call" | custom-call | flops 800000000 | bytes 4194304 | tf_op jit(solution)/shard_map/weight/pallas_call | solution.py:45
  125.9 10.9 %all-to-all-start.4 = ((bf16[64,40,128]{2,1,0:T(8,128)(2,1)}), bf16[64,40,128]{2,1,0:T(8,128)(2,1)S(1)}, u32[]{:S(2)}, u32[]{:S(2)}) async-start(bf16[64,40,128]{2,1,0:T(8,128)(2,1)} %copy-done), calls=%async_computation.4 | async-start | bytes 1310720 | tf_op jit(solution)/shard_map/all_to_all | solution.py:309
  137.8 2.5 %collective-permute-start.14 = (f32[2,112,128]{2,1,0:T(8,128)S(1)}, f32[2,112,128]{2,1,0:T(8,128)S(1)}, u32[]{:S(2)}, u32[]{:S(2)}) collective-permute-start(f32[2,112,128]{2,1,0:T(8,128)S(1)} %get-tuple-element.71), channel_id=1, source_target_pairs={{0,2},{2,4},{4,6},{6,0},{1,3},{3,5},{5,7},{7,1},{8,10},{10,12},{12... | collective-permute-start | bytes 344072 | tf_op jit(solution)/shard_map/ppermute | solution.py:229
  140.3 4.6 %collective-permute-start.15 = (f32[2,112,128]{2,1,0:T(8,128)S(1)}, f32[2,112,128]{2,1,0:T(8,128)S(1)}, u32[]{:S(2)}, u32[]{:S(2)}) collective-permute-start(f32[2,112,128]{2,1,0:T(8,128)S(1)} %get-tuple-element.72), channel_id=1, source_target_pairs={{0,6},{2,0},{4,2},{6,4},{1,7},{3,1},{5,3},{7,5},{8,14},{10,8},{12,... | collective-permute-start | bytes 344072 | tf_op jit(solution)/shard_map/ppermute | solution.py:229
  144.9 2.3 %collective-permute-start.16 = (f32[2,112,128]{2,1,0:T(8,128)S(1)}, f32[2,112,128]{2,1,0:T(8,128)S(1)}, u32[]{:S(2)}, u32[]{:S(2)}) collective-permute-start(f32[2,112,128]{2,1,0:T(8,128)S(1)} %get-tuple-element.73), channel_id=1, source_target_pairs={{0,4},{2,6},{4,0},{6,2},{1,5},{3,7},{5,1},{7,3},{8,12},{10,14},{12... | collective-permute-start | bytes 344072 | tf_op jit(solution)/shard_map/ppermute | solution.py:229
  148.4 4.6 %collective-permute-done.16.across = f32[2,112,128]{2,1,0:T(8,128)S(1)} collective-permute-done((f32[2,112,128]{2,1,0:T(8,128)S(1)}, f32[2,112,128]{2,1,0:T(8,128)S(1)}, u32[]{:S(2)}, u32[]{:S(2)}) %collective-permute-start.16) | collective-permute-done | bytes 114720 | tf_op jit(solution)/shard_map/ppermute | solution.py:229
  154.4 4.2 %all-to-all-done.4 = bf16[64,40,128]{2,1,0:T(8,128)(2,1)S(1)} async-done(((bf16[64,40,128]{2,1,0:T(8,128)(2,1)}), bf16[64,40,128]{2,1,0:T(8,128)(2,1)S(1)}, u32[]{:S(2)}, u32[]{:S(2)}) %all-to-all-start.4) | async-done | bytes 655392 | tf_op jit(solution)/shard_map/all_to_all | solution.py:309
  (91 shorter events, 46.4 us)
Async XLA Ops:
  0.6 20.9 %collective-permute-start = (bf16[1024,128]{1,0:T(8,128)(2,1)}, bf16[1024,128]{1,0:T(8,128)(2,1)S(1)}, u32[]{:S(2)}, u32[]{:S(2)}) collective-permute-start(bf16[1024,128]{1,0:T(8,128)(2,1)} %param.9), channel_id=1, source_target_pairs={{0,2},{2,4},{4,6},{6,0},{1,3},{3,5},{5,7},{7,1},{8,10},{10,12},{12... | collective-permute-start | bytes 786440 | tf_op jit(solution)/shard_map/ppermute | solution.py:229
  8.4 33.9 %copy-start.23 = (bf16[1024,128]{1,0:T(8,128)(2,1)S(1)}, bf16[1024,128]{1,0:T(8,128)(2,1)}, u32[]{:S(2)}) copy-start(bf16[1024,128]{1,0:T(8,128)(2,1)} %param.9) | copy-start | bytes 786436
  9.9 17.4 %collective-permute-start.3 = (bf16[1408,128]{1,0:T(8,128)(2,1)S(1)}, bf16[1408,128]{1,0:T(8,128)(2,1)S(1)}, u32[]{:S(2)}, u32[]{:S(2)}) collective-permute-start(bf16[1408,128]{1,0:T(8,128)(2,1)S(1)} %get-tuple-element.42), channel_id=1, source_target_pairs={{0,6},{2,0},{4,2},{6,4},{1,7},{3,1},{5,3},{7,5},{8,14},{10,8},{12,... | collective-permute-start | bytes 1081352 | tf_op jit(solution)/shard_map/ppermute | solution.py:229
  13.5 13.7 %collective-permute-start.2 = (bf16[1408,128]{1,0:T(8,128)(2,1)S(1)}, bf16[1408,128]{1,0:T(8,128)(2,1)S(1)}, u32[]{:S(2)}, u32[]{:S(2)}) collective-permute-start(bf16[1408,128]{1,0:T(8,128)(2,1)S(1)} %get-tuple-element.42), channel_id=1, source_target_pairs={{0,2},{2,4},{4,6},{6,0},{1,3},{3,5},{5,7},{7,1},{8,10},{10,12},{12... | collective-permute-start | bytes 1081352 | tf_op jit(solution)/shard_map/ppermute | solution.py:229
  15.7 11.5 %collective-permute-start.1 = (bf16[1024,128]{1,0:T(8,128)(2,1)}, bf16[1024,128]{1,0:T(8,128)(2,1)S(1)}, u32[]{:S(2)}, u32[]{:S(2)}) collective-permute-start(bf16[1024,128]{1,0:T(8,128)(2,1)} %param.9), channel_id=1, source_target_pairs={{0,6},{2,0},{4,2},{6,4},{1,7},{3,1},{5,3},{7,5},{8,14},{10,8},{12,... | collective-permute-start | bytes 786440 | tf_op jit(solution)/shard_map/ppermute | solution.py:229
  21.6 20.7 %all-to-all-start = ((bf16[8,256,128]{2,1,0:T(8,128)(2,1)}), bf16[8,256,128]{2,1,0:T(8,128)(2,1)S(1)}, u32[]{:S(2)}, u32[]{:S(2)}) async-start(bf16[8,256,128]{2,1,0:T(8,128)(2,1)} %get-tuple-element.46), calls=%async_computation | async-start | bytes 1048576 | tf_op jit(solution)/shard_map/all_to_all | solution.py:261
  27.3 15.0 %collective-permute-start.5 = (bf16[1408,128]{1,0:T(8,128)(2,1)S(1)}, bf16[1408,128]{1,0:T(8,128)(2,1)S(1)}, u32[]{:S(2)}, u32[]{:S(2)}) collective-permute-start(bf16[1408,128]{1,0:T(8,128)(2,1)S(1)} %collective-permute-done.3), channel_id=1, source_target_pairs={{0,6},{2,0},{4,2},{6,4},{1,7},{3,1},{5,3},{7,5},{8,14},{10,8},{12,... | collective-permute-start | bytes 1081352 | tf_op jit(solution)/shard_map/ppermute | solution.py:229
  32.5 9.7 %collective-permute-start.4 = (bf16[1024,128]{1,0:T(8,128)(2,1)S(1)}, bf16[1024,128]{1,0:T(8,128)(2,1)S(1)}, u32[]{:S(2)}, u32[]{:S(2)}) collective-permute-start(bf16[1024,128]{1,0:T(8,128)(2,1)S(1)} %collective-permute-done), channel_id=1, source_target_pairs={{0,2},{2,4},{4,6},{6,0},{1,3},{3,5},{5,7},{7,1},{8,10},{10,12},{12... | collective-permute-start | bytes 786440 | tf_op jit(solution)/shard_map/ppermute | solution.py:229
  42.4 4.6 %collective-permute-start.6 = (bf16[4,1024,128]{2,1,0:T(8,128)(2,1)S(1)}, bf16[4,1024,128]{2,1,0:T(8,128)(2,1)S(1)}, u32[]{:S(2)}, u32[]{:S(2)}) collective-permute-start(bf16[4,1024,128]{2,1,0:T(8,128)(2,1)S(1)} %pad_maximum_fusion.2.near), channel_id=1, source_target_pairs={{0,1},{1,0},{2,3},{3,2},{4,5},{5,4},{6,7},{7,6},{8,9},{9,8},{10,11... | collective-permute-start | bytes 3145736 | tf_op jit(solution)/shard_map/ppermute | solution.py:233
  44.5 5.2 %collective-permute-start.7 = (bf16[4,1408,128]{2,1,0:T(8,128)(2,1)S(1)}, bf16[4,1408,128]{2,1,0:T(8,128)(2,1)S(1)}, u32[]{:S(2)}, u32[]{:S(2)}) collective-permute-start(bf16[4,1408,128]{2,1,0:T(8,128)(2,1)S(1)} %pad_maximum_fusion.1.near), channel_id=1, source_target_pairs={{0,1},{1,0},{2,3},{3,2},{4,5},{5,4},{6,7},{7,6},{8,9},{9,8},{10,11... | collective-permute-start | bytes 4325384 | tf_op jit(solution)/shard_map/ppermute | solution.py:233
  54.5 45.0 %copy-start.18 = (f32[112,384]{1,0:T(8,128)S(1)}, f32[112,384]{1,0:T(8,128)}, u32[]{:S(2)}) copy-start(f32[112,384]{1,0:T(8,128)} %copy-done.17) | copy-start | bytes 516100
  63.2 23.9 %collective-permute-start.10 = (bf16[2,112,1536]{2,1,0:T(8,128)(2,1)}, bf16[2,112,1536]{2,1,0:T(8,128)(2,1)}, u32[]{:S(2)}, u32[]{:S(2)}) collective-permute-start(bf16[2,112,1536]{2,1,0:T(8,128)(2,1)} %get-tuple-element.66), channel_id=1, source_target_pairs={{0,6},{2,0},{4,2},{6,4},{1,7},{3,1},{5,3},{7,5},{8,14},{10,8},{12,... | collective-permute-start | bytes 2064392 | tf_op jit(solution)/shard_map/ppermute | solution.py:229
  66.2 26.8 %collective-permute-start.9 = (bf16[2,112,1536]{2,1,0:T(8,128)(2,1)}, bf16[2,112,1536]{2,1,0:T(8,128)(2,1)}, u32[]{:S(2)}, u32[]{:S(2)}) collective-permute-start(bf16[2,112,1536]{2,1,0:T(8,128)(2,1)} %get-tuple-element.66), channel_id=1, source_target_pairs={{0,2},{2,4},{4,6},{6,0},{1,3},{3,5},{5,7},{7,1},{8,10},{10,12},{12... | collective-permute-start | bytes 2064392 | tf_op jit(solution)/shard_map/ppermute | solution.py:229
  70.4 29.1 %all-to-all-start.2 = ((f32[64,2,384]{2,1,0:T(2,128)}), f32[64,2,384]{2,1,0:T(2,128)S(1)}, u32[]{:S(2)}, u32[]{:S(2)}) async-start(f32[64,2,384]{2,1,0:T(2,128)} %broadcast_in_dim.9), calls=%async_computation.2 | async-start | bytes 393216 | tf_op jit(solution)/shard_map/all_to_all | solution.py:286
  88.8 21.0 %collective-permute-start.12 = (bf16[112,1536]{1,0:T(8,128)(2,1)}, bf16[112,1536]{1,0:T(8,128)(2,1)}, u32[]{:S(2)}, u32[]{:S(2)}) collective-permute-start(bf16[112,1536]{1,0:T(8,128)(2,1)} %slice_bitcast_fusion), channel_id=1, source_target_pairs={{0,6},{2,0},{4,2},{6,4},{1,7},{3,1},{5,3},{7,5},{8,14},{10,8},{12,... | collective-permute-start | bytes 1032200 | tf_op jit(solution)/shard_map/ppermute | solution.py:229
  94.8 15.0 %collective-permute-start.11 = (bf16[112,1536]{1,0:T(8,128)(2,1)}, bf16[112,1536]{1,0:T(8,128)(2,1)}, u32[]{:S(2)}, u32[]{:S(2)}) collective-permute-start(bf16[112,1536]{1,0:T(8,128)(2,1)} %slice_bitcast_fusion.1), channel_id=1, source_target_pairs={{0,2},{2,4},{4,6},{6,0},{1,3},{3,5},{5,7},{7,1},{8,10},{10,12},{12... | collective-permute-start | bytes 1032200 | tf_op jit(solution)/shard_map/ppermute | solution.py:229
  106.2 15.8 %all-to-all-start.3 = ((bf16[8,112,384]{2,1,0:T(8,128)(2,1)}), bf16[8,112,384]{2,1,0:T(8,128)(2,1)S(1)}, u32[]{:S(2)}, u32[]{:S(2)}) async-start(bf16[8,112,384]{2,1,0:T(8,128)(2,1)} %copy-done.3), calls=%async_computation.3 | async-start | bytes 1376256 | tf_op jit(solution)/shard_map/all_to_all | solution.py:299
  112.8 9.1 %collective-permute-start.13 = (bf16[4,2,112,1536]{3,2,1,0:T(8,128)(2,1)S(1)}, bf16[4,2,112,1536]{3,2,1,0:T(8,128)(2,1)}, u32[]{:S(2)}, u32[]{:S(2)}) collective-permute-start(bf16[4,2,112,1536]{3,2,1,0:T(8,128)(2,1)S(1)} %pad_maximum_fusion.near), channel_id=1, source_target_pairs={{0,1},{1,0},{2,3},{3,2},{4,5},{5,4},{6,7},{7,6},{8,9},{9,8},{10,11... | collective-permute-start | bytes 8257544 | tf_op jit(solution)/shard_map/ppermute | solution.py:233
  118.0 7.9 %collective-permute-start.8 = (f32[4,112,128]{2,1,0:T(8,128)}, f32[4,112,128]{2,1,0:T(8,128)}, u32[]{:S(2)}, u32[]{:S(2)}) collective-permute-start(f32[4,112,128]{2,1,0:T(8,128)} %get-tuple-element.64), channel_id=1, source_target_pairs={{0,1},{1,0},{2,3},{3,2},{4,5},{5,4},{6,7},{7,6},{8,9},{9,8},{10,11... | collective-permute-start | bytes 688136 | tf_op jit(solution)/shard_map/ppermute | solution.py:233
  125.8 11.0 %copy-start.6 = (f32[4,112,128]{2,1,0:T(8,128)S(1)}, f32[4,112,128]{2,1,0:T(8,128)}, u32[]{:S(2)}) copy-start(f32[4,112,128]{2,1,0:T(8,128)} %copy-done.5) | copy-start | bytes 688132
  125.9 32.8 %all-to-all-start.4 = ((bf16[64,40,128]{2,1,0:T(8,128)(2,1)}), bf16[64,40,128]{2,1,0:T(8,128)(2,1)S(1)}, u32[]{:S(2)}, u32[]{:S(2)}) async-start(bf16[64,40,128]{2,1,0:T(8,128)(2,1)} %copy-done), calls=%async_computation.4 | async-start | bytes 1310720 | tf_op jit(solution)/shard_map/all_to_all | solution.py:309
  137.8 9.4 %collective-permute-start.14 = (f32[2,112,128]{2,1,0:T(8,128)S(1)}, f32[2,112,128]{2,1,0:T(8,128)S(1)}, u32[]{:S(2)}, u32[]{:S(2)}) collective-permute-start(f32[2,112,128]{2,1,0:T(8,128)S(1)} %get-tuple-element.71), channel_id=1, source_target_pairs={{0,2},{2,4},{4,6},{6,0},{1,3},{3,5},{5,7},{7,1},{8,10},{10,12},{12... | collective-permute-start | bytes 344072 | tf_op jit(solution)/shard_map/ppermute | solution.py:229
  140.3 8.1 %collective-permute-start.15 = (f32[2,112,128]{2,1,0:T(8,128)S(1)}, f32[2,112,128]{2,1,0:T(8,128)S(1)}, u32[]{:S(2)}, u32[]{:S(2)}) collective-permute-start(f32[2,112,128]{2,1,0:T(8,128)S(1)} %get-tuple-element.72), channel_id=1, source_target_pairs={{0,6},{2,0},{4,2},{6,4},{1,7},{3,1},{5,3},{7,5},{8,14},{10,8},{12,... | collective-permute-start | bytes 344072 | tf_op jit(solution)/shard_map/ppermute | solution.py:229
  144.9 8.2 %collective-permute-start.16 = (f32[2,112,128]{2,1,0:T(8,128)S(1)}, f32[2,112,128]{2,1,0:T(8,128)S(1)}, u32[]{:S(2)}, u32[]{:S(2)}) collective-permute-start(f32[2,112,128]{2,1,0:T(8,128)S(1)} %get-tuple-element.73), channel_id=1, source_target_pairs={{0,4},{2,6},{4,0},{6,2},{1,5},{3,7},{5,1},{7,3},{8,12},{10,14},{12... | collective-permute-start | bytes 344072 | tf_op jit(solution)/shard_map/ppermute | solution.py:229
  (21 other events, 32.6 us)
